TPU v7x, 512 devices: a whole 4x4x16 slice. The times are simulated.
512 devices in a mesh: dp: 128 (over y_hi, z, x), tensor: 4 (over y_lo, core).
Axes of the slice: x: 4, y: 4 (y_hi: 2, y_lo: 2; y = y_hi * 2 + y_lo), z: 16, core: 2. Of those that a mesh axis runs over, the one named last changes fastest.
Arguments:
- rows_in: bfloat16 [32768, 1152], P('dp'), may hold values from -6 to 6
- patch_counts: int32 [128, 2], P('dp'), may hold values from 32 to 128, as said below
- row_slots: int32 [128, 256], P('dp'), may hold values from 0 to 255, each once within a row
- w_qkv: bfloat16 [1152, 3456], P(None, 'tensor'), may hold values from -0.1875 to 0.1875
- w_out: bfloat16 [1152, 1152], P('tensor'), may hold values from -0.1875 to 0.1875
- w_fc1: bfloat16 [1152, 4304], P(None, 'tensor'), may hold values from -0.1875 to 0.1875
- w_fc2: bfloat16 [4304, 1152], P('tensor'), may hold values from -0.09375 to 0.09375
- text_embeds: bfloat16 [256, 1152], P('dp'), may hold values from -6 to 6
- similarity_multiplier: float32 [1], replicated, may hold values from 2 to 8
- similarity_shift_term: float32 [1], replicated, may hold values from -6 to -2
Outputs:
- rows_out: bfloat16 [32768, 1152], P('dp')
- pooled_grad: float32 [256, 1152], P('dp')
Inputs may be any that keep to these rules, and one draw needn't show every extreme that they name: `patch_counts`: each device's 2 images fill its first rows one after another; the remaining rows are padding. Both bounds are reached in every draw. Each device's row of row_slots is a permutation of 0 to 255.
All inputs are finite; a program needn't handle non-finite values.
Results may differ from a plain program's by a relative error of at most 0.015.
Values may be sent and summed in bfloat16 or wider, within the bound.
No kernel may reach another device: no remote copies, remote signals or barrier semaphores. Data moves between devices by JAX's collectives and lax.ppermute only.
A program may use at most 64 MiB of HBM per device.

v0:
```python
import math

import jax
import jax.numpy as jnp
from jax import lax
from jax.sharding import PartitionSpec as P

HEAD_DIM = 72


def layer_norm(values):
    mean_val = jnp.mean(values, axis=-1, keepdims=True)
    centred = values - mean_val
    var_val = jnp.mean(centred * centred, axis=-1, keepdims=True)
    return centred * lax.rsqrt(var_val + 1e-06)


def feed_forward(residual, w_fc1, w_fc2):
    normed_two = layer_norm(residual.astype(jnp.float32)).astype(jnp.bfloat16)
    hidden = jax.nn.gelu(
        jnp.dot(normed_two, w_fc1, preferred_element_type=jnp.float32), approximate=True
    ).astype(jnp.bfloat16)
    partial_out = jnp.dot(hidden, w_fc2, preferred_element_type=jnp.float32).astype(jnp.bfloat16)
    summed = lax.psum(partial_out, "tensor").astype(jnp.float32)
    return (residual.astype(jnp.float32) + summed).astype(jnp.bfloat16)


def route_rows(blocks):
    return lax.all_to_all(blocks, "dp", split_axis=0, concat_axis=0, tiled=True)


def per_device(
    rows_in,
    patch_counts,
    row_slots,
    w_qkv,
    w_out,
    w_fc1,
    w_fc2,
    text_embeds,
    similarity_multiplier,
    similarity_shift_term,
):
    row_count, feat_width = rows_in.shape
    image_count = patch_counts.shape[1]
    head_count = w_out.shape[0] // HEAD_DIM
    peer_count = lax.axis_size("dp")
    per_peer = row_count // peer_count
    slots_here = row_slots[0]
    bounds = jnp.cumsum(patch_counts[0])
    positions = jnp.arange(row_count, dtype=jnp.int32)
    segment = jnp.sum((positions[:, None] >= bounds[None, :]).astype(jnp.int32), axis=1)
    normed = layer_norm(rows_in.astype(jnp.float32)).astype(jnp.bfloat16)
    projected = jnp.dot(normed, w_qkv, preferred_element_type=jnp.float32).astype(jnp.bfloat16)
    projected = projected.reshape(row_count, 3, head_count, HEAD_DIM)
    queries = projected[:, 0]
    keys_local = projected[:, 1]
    values_local = projected[:, 2]
    scores = jnp.einsum(
        "qhd,khd->hqk", queries, keys_local, preferred_element_type=jnp.float32
    ) / math.sqrt(HEAD_DIM)
    same_image = segment[:, None] == segment[None, :]
    scores = jnp.where(same_image[None], scores, -1e30)
    row_max = jnp.max(scores, axis=-1, keepdims=True)
    exp_scores = jnp.exp(scores - row_max)
    weights = (exp_scores / jnp.sum(exp_scores, axis=-1, keepdims=True)).astype(jnp.bfloat16)
    attended = jnp.einsum(
        "hqk,khd->qhd", weights, values_local, preferred_element_type=jnp.float32
    ).astype(jnp.bfloat16)
    attended = attended.reshape(row_count, head_count * HEAD_DIM)
    partial_attn = jnp.dot(attended, w_out, preferred_element_type=jnp.float32).astype(jnp.bfloat16)
    attn_mixed = lax.psum(partial_attn, "tensor").astype(jnp.float32)
    residual = (rows_in.astype(jnp.float32) + attn_mixed).astype(jnp.bfloat16)
    home_rows = feed_forward(residual, w_fc1, w_fc2)
    outgoing = jnp.zeros_like(home_rows).at[slots_here].set(home_rows)
    rows_out = route_rows(outgoing.reshape(peer_count, per_peer, feat_width)).reshape(
        row_count, feat_width
    )
    post_norm = layer_norm(home_rows.astype(jnp.float32))
    member = (segment[None, :] == jnp.arange(image_count, dtype=jnp.int32)[:, None]).astype(
        jnp.float32
    )
    pooled = jnp.dot(member, post_norm, precision=lax.Precision.HIGHEST) / patch_counts[0][
        :, None
    ].astype(jnp.float32)
    norm_img = jnp.sqrt(jnp.sum(pooled * pooled, axis=1, keepdims=True) + 1e-06)
    picture_unit_length_direction = pooled / norm_img
    similarity_sharpness_factor = similarity_multiplier[0]
    logit_offset_value = similarity_shift_term[0]
    image_index = lax.axis_index("dp") * image_count + jnp.arange(image_count, dtype=jnp.int32)
    text_piece = lax.all_gather(text_embeds, "dp", axis=0, tiled=True)
    text_f = text_piece.astype(jnp.float32)
    caption_unit_length_direction = text_f / jnp.sqrt(
        jnp.sum(text_f * text_f, axis=1, keepdims=True) + 1e-06
    )
    similarity_matrix_entries = (
        similarity_sharpness_factor
        * jnp.dot(
            picture_unit_length_direction,
            caption_unit_length_direction.T,
            precision=lax.Precision.HIGHEST,
        )
        + logit_offset_value
    )
    column = jnp.arange(text_piece.shape[0], dtype=jnp.int32)
    target = (image_index[:, None] == column[None, :]).astype(jnp.float32)
    similarity_matrix_derivative = jax.nn.sigmoid(similarity_matrix_entries) - target
    picture_feature_derivative_wrt = similarity_sharpness_factor * jnp.dot(
        similarity_matrix_derivative, caption_unit_length_direction, precision=lax.Precision.HIGHEST
    )
    pooled_grad = (
        picture_feature_derivative_wrt
        - picture_unit_length_direction
        * jnp.sum(
            picture_unit_length_direction * picture_feature_derivative_wrt, axis=1, keepdims=True
        )
    ) / norm_img
    return (rows_out, pooled_grad)


def solution(mesh):
    placed = (
        P("dp", None),
        P("dp", None),
        P("dp", None),
        P(None, "tensor"),
        P("tensor", None),
        P(None, "tensor"),
        P("tensor", None),
        P("dp", None),
        P(),
        P(),
    )
    return jax.shard_map(
        per_device,
        mesh=mesh,
        in_specs=placed,
        out_specs=(P("dp", None), P("dp", None)),
        check_vma=False,
    )
```

profile of v0, /device:TPU:1, one launch (start us, length us, event | category | flops | bytes accessed | tf_op | source)
XLA Modules:
  0.0 509.6 jit_solution(4541663512600566641)
XLA Ops:
  7.2 0.0 copy-start
  7.2 0.0 copy-start.1
  7.2 0.0 copy-start.8
  7.2 0.0 all-reduce.3.cloned.1.call-start
  7.2 1.4 convert_reduce_fusion.1
  8.6 1.4 fusion.12
  10.0 0.0 copy-done.8
  10.0 0.2 reduce-window.8
  10.2 0.1 fusion.56
  10.3 0.1 broadcast_compare_fusion
  10.4 0.0 copy-done.1
  10.4 0.0 copy-start.4
  10.4 2.4 convolution_convert_fusion.2
  12.8 0.0 copy-start.5
  12.9 0.0 copy-done.4
  12.9 0.7 copy-done.5
  13.6 0.3 fusion.9
  14.0 1.5 fusion.69
  15.5 1.9 convolution_convert_fusion.3
  17.5 2.5 convolution_convert_fusion.1
  20.0 0.0 all-reduce.3.cloned.1.call-update
  20.0 0.0 all-reduce.5.cloned.1.call-start
  20.0 0.0 copy-done.6
  20.0 311.1 %all-gather = bf16[128,2,1152]{2,1,0:T(2,128)(2,1)S(1)} all-gather(bf16[1,2,1152]{2,1,0:T(2,128)(2,1)S(1)} %bitcast.47), channel_id=1, replica_groups=mesh['dp'=128,'tensor'=4] {'dp'}, dimensions={0}, use_global_device_ids=true | all-gather | bytes 594432 | tf_op jit(solution)/shard_map/all_gather | solution.py:91
  331.2 1.2 reshape.174
  333.7 0.0 all-reduce.3.cloned.1.call-done
  333.7 1.5 convert_reduce_fusion
  335.2 0.3 fusion.10
  335.5 0.0 copy-done
  335.5 5.8 %convolution_convert_fusion = bf16[256,1152]{1,0:T(8,128)(2,1)} fusion(bf16[1076,1152]{1,0:T(8,128)(2,1)S(1)} %copy-done, bf16[1152,1076]{0,1:T(8,128)(2,1)} %param.15, bf16[256,1152]{1,0:T(8,128)(2,1)S(1)} %get-tuple-element.5, f32[256]{0:T(256)S(1)} %add_rsqrt_fusion.1, f32[256]{0:T(256)S(1)} %broadcast_multiply_fusion.1), kind=kOutput, calls=%fused_computation.2 | convolution fusion | flops 1273254912 | bytes 6139904 | tf_op jit(solution)/shard_map/dot_general | solution.py:23
  341.3 0.0 all-reduce.5.cloned.1.call-update
  341.3 1.4 multiply_reduce_fusion
  342.8 0.0 copy-done.7
  342.8 93.9 %all-reduce.5.cloned.1.call-done = bf16[256,1152]{1,0:T(8,128)(2,1)} async-done(((bf16[256,1152]{1,0:T(8,128)(2,1)}), bf16[256,1152]{1,0:T(8,128)(2,1)}) %all-reduce.5.cloned.1.call-update) | async-done | bytes 589840 | tf_op jit(solution)/shard_map/psum | solution.py:24
  436.7 2.0 convert_reduce_fusion.2
  438.7 3.0 scatter_custom_fusion
  441.8 2.7 reshape.162
  444.4 19.1 %all-to-all-start = ((bf16[128,2,1152]{2,1,0:T(2,128)(2,1)}), bf16[128,2,1152]{2,1,0:T(2,128)(2,1)}, u32[]{:S(2)}, u32[]{:S(2)}) async-start(bf16[128,2,1152]{2,1,0:T(2,128)(2,1)} %reshape.162), calls=%async_computation | async-start | bytes 1179648 | tf_op jit(solution)/shard_map/all_to_all | solution.py:29
  463.5 0.0 copy-start.2
  463.6 0.0 copy-done.3
  463.6 0.3 fusion.14
  463.9 0.8 fusion.54
  464.7 0.1 copy-done.2
  464.8 1.1 fusion.24
  465.9 0.9 multiply_reduce_fusion.1
  466.8 0.7 subtract_divide_fusion
  467.5 32.6 %all-to-all-done = bf16[128,2,1152]{2,1,0:T(2,128)(2,1)} async-done(((bf16[128,2,1152]{2,1,0:T(2,128)(2,1)}), bf16[128,2,1152]{2,1,0:T(2,128)(2,1)}, u32[]{:S(2)}, u32[]{:S(2)}) %all-to-all-start) | async-done | bytes 589856 | tf_op jit(solution)/shard_map/all_to_all | solution.py:29
  500.1 2.6 reshape.163
  (14 shorter events, 0.1 us)
Async XLA Ops:
  7.2 328.4 %copy-start = (bf16[1076,1152]{1,0:T(8,128)(2,1)S(1)}, bf16[1076,1152]{1,0:T(8,128)(2,1)}, u32[]{:S(2)}) copy-start(bf16[1076,1152]{1,0:T(8,128)(2,1)} %param.16) | copy-start | bytes 7437316
  7.2 3.2 copy-start.1
  7.2 2.8 copy-start.8
  7.2 326.5 %all-reduce.3.cloned.1.call-start = ((), (), s32[]{:S(2)}) async-start(), calls=%async_computation.1 | async-start | bytes 1179648 | tf_op jit(solution)/shard_map/psum | solution.py:72
  10.4 2.5 copy-start.4
  12.8 0.8 copy-start.5
  17.5 2.6 copy-start.6
  20.0 416.7 %all-reduce.5.cloned.1.call-start = ((), (), s32[]{:S(2)}) async-start(), calls=%async_computation.2 | async-start | bytes 1179648 | tf_op jit(solution)/shard_map/psum | solution.py:24
  341.3 1.5 copy-start.7
  441.8 21.8 %copy-start.3 = (bf16[256,1152]{1,0:T(8,128)(2,1)S(1)}, bf16[256,1152]{1,0:T(8,128)(2,1)}, u32[]{:S(2)}) copy-start(bf16[256,1152]{1,0:T(8,128)(2,1)} %get-tuple-element.3) | copy-start | bytes 1769476
  444.4 55.7 %all-to-all-start = ((bf16[128,2,1152]{2,1,0:T(2,128)(2,1)}), bf16[128,2,1152]{2,1,0:T(2,128)(2,1)}, u32[]{:S(2)}, u32[]{:S(2)}) async-start(bf16[128,2,1152]{2,1,0:T(2,128)(2,1)} %reshape.162), calls=%async_computation | async-start | bytes 1179648 | tf_op jit(solution)/shard_map/all_to_all | solution.py:29
  463.5 1.3 copy-start.2
Sparse Core Ops, SparseCore 0:
  20.1 59.6 all-reduce.2
  341.4 95.1 all-reduce.4
where the time goes:
time: 511 us; the launch traced here: 510 us
  blocking collectives  311 us (61%)
  waiting for transfers between devices  127 us (25%)
  starting transfers between devices  19.1 us (4%)
  matrix products  17.4 us (3%)
  between operations  15.6 us (3%)
  local copies, waits for them, and re-layouts  10.4 us (2%)
  other arithmetic  9.44 us (2%)
    all_gather x1, blocking collectives, per_device(): text_piece = lax.all_gather(text_embeds, 'dp', axis=0, tiled=True)  311 us
    psum x1, waiting for transfers between devices, feed_forward(): summed = lax.psum(partial_out, 'tensor').astype(jnp.float32)  93.9 us
    all_to_all x1, waiting for transfers between devices, route_rows(): return lax.all_to_all(blocks, 'dp', split_axis=0, concat_axis=0, tiled=True)  32.6 us
    all_to_all x1, starting transfers between devices, route_rows(): return lax.all_to_all(blocks, 'dp', split_axis=0, concat_axis=0, tiled=True)  19.1 us
  transfers between devices with their start and end apart: 3, of which 2 were waited for; matrix products, arithmetic and copies ran while one was open for 1% of the time, Pallas kernels for 0%

commit v1 on v0

v1 whole, which is shorter than its diff:
```python
import math

import jax
import jax.numpy as jnp
from jax import lax
from jax.sharding import Mesh
from jax.sharding import PartitionSpec as P

HEAD_DIM = 72
N_YH, N_Z, N_X, N_YL, N_CORE = 2, 16, 4, 2, 2
DP = ("yh", "z", "x")
TP = ("yl", "core")
RING = ("yh", "z")
HIGH = lax.Precision.HIGHEST


def layer_norm(values):
    mean_val = jnp.mean(values, axis=-1, keepdims=True)
    centred = values - mean_val
    var_val = jnp.mean(centred * centred, axis=-1, keepdims=True)
    return centred * lax.rsqrt(var_val + 1e-06)


def unit_rows(values):
    return values / jnp.sqrt(jnp.sum(values * values, axis=1, keepdims=True) + 1e-06)


def swap_quarters(values):
    pairs = [(x * N_X + t, t * N_X + x) for x in range(N_X) for t in range(N_X)]
    return lax.ppermute(values, ("x",) + TP, pairs)


def sum_scatter(partial):
    rows, width = partial.shape
    parts = lax.all_to_all(partial.reshape(4, rows // 4, width), TP, 0, 0, tiled=True)
    return jnp.sum(parts.astype(jnp.float32), axis=0)


def per_device(rows_in, patch_counts, row_slots, w_qkv, w_out, w_fc1, w_fc2, text_embeds, multiplier, shift):
    row_count, width = rows_in.shape
    image_count = patch_counts.shape[1]
    head_count = w_out.shape[0] // HEAD_DIM
    quarter = row_count // 4
    ring = N_YH * N_Z
    my_x, my_t = lax.axis_index("x"), lax.axis_index(TP)

    slots = row_slots[0]
    peer, place = slots // 2, slots % 2
    order = (peer % N_X) * quarter + (peer // N_X) * 2 + place
    positions = jnp.arange(row_count, dtype=jnp.int32)
    moved = (positions[:, None] == order[None, :]).astype(jnp.bfloat16)
    bounds = jnp.cumsum(patch_counts[0])
    origin = jnp.sum(jnp.where(positions[:, None] == order[None, :], positions[None, :], 0), axis=1)
    segment = jnp.sum((origin[:, None] >= bounds[None, :]).astype(jnp.int32), axis=1)
    rows = jnp.dot(moved, rows_in, preferred_element_type=jnp.float32).astype(jnp.bfloat16)

    my_texts = swap_quarters(text_embeds)
    texts = lax.all_to_all(jnp.broadcast_to(my_texts[None], (ring,) + my_texts.shape), RING, 0, 0, tiled=True)
    texts = texts.reshape(ring * image_count, width)

    normed = layer_norm(rows.astype(jnp.float32)).astype(jnp.bfloat16)
    projected = jnp.dot(normed, w_qkv, preferred_element_type=jnp.float32).astype(jnp.bfloat16)
    projected = projected.reshape(row_count, 3, head_count, HEAD_DIM)
    queries, keys, values = projected[:, 0], projected[:, 1], projected[:, 2]
    scores = jnp.einsum("qhd,khd->hqk", queries, keys, preferred_element_type=jnp.float32) / math.sqrt(HEAD_DIM)
    same_image = segment[:, None] == segment[None, :]
    scores = jnp.where(same_image[None], scores, -1e30)
    row_max = jnp.max(scores, axis=-1, keepdims=True)
    exp_scores = jnp.exp(scores - row_max)
    weights = (exp_scores / jnp.sum(exp_scores, axis=-1, keepdims=True)).astype(jnp.bfloat16)
    attended = jnp.einsum("hqk,khd->qhd", weights, values, preferred_element_type=jnp.float32).astype(jnp.bfloat16)
    attended = attended.reshape(row_count, head_count * HEAD_DIM)
    attn_part = jnp.dot(attended, w_out, preferred_element_type=jnp.float32).astype(jnp.bfloat16)

    own = lax.dynamic_slice_in_dim(rows, my_t * quarter, quarter, axis=0)
    own_segment = lax.dynamic_slice_in_dim(segment, my_t * quarter, quarter, axis=0)
    resid = (own.astype(jnp.float32) + sum_scatter(attn_part)).astype(jnp.bfloat16)
    normed_own = layer_norm(resid.astype(jnp.float32)).astype(jnp.bfloat16)
    normed_two = lax.all_gather(normed_own, TP, axis=0, tiled=True)
    hidden = jax.nn.gelu(
        jnp.dot(normed_two, w_fc1, preferred_element_type=jnp.float32), approximate=True
    ).astype(jnp.bfloat16)
    mlp_part = jnp.dot(hidden, w_fc2, preferred_element_type=jnp.float32).astype(jnp.bfloat16)
    layer = (resid.astype(jnp.float32) + sum_scatter(mlp_part)).astype(jnp.bfloat16)

    outgoing = swap_quarters(layer).reshape(ring, 2, width)
    arrived = lax.all_to_all(outgoing, RING, 0, 0, tiled=True)
    arrived = lax.all_gather(arrived.reshape(quarter, width), TP, axis=0, tiled=True)
    rows_out = arrived.reshape(N_X, ring, 2, width).transpose(1, 0, 2, 3).reshape(row_count, width)

    images = jnp.arange(image_count, dtype=jnp.int32)
    member = (own_segment[None, :] == images[:, None]).astype(jnp.float32)
    pooled = jnp.dot(member, layer_norm(layer.astype(jnp.float32)), precision=HIGH)
    pooled = lax.psum(pooled, TP) / patch_counts[0][:, None].astype(jnp.float32)
    norm_img = jnp.sqrt(jnp.sum(pooled * pooled, axis=1, keepdims=True) + 1e-06)
    image_unit = pooled / norm_img
    text_unit = unit_rows(texts.astype(jnp.float32))
    logits = multiplier[0] * jnp.dot(image_unit, text_unit.T, precision=HIGH) + shift[0]
    text_peer = jnp.arange(ring, dtype=jnp.int32) * N_X + my_t
    text_index = (text_peer[:, None] * image_count + images[None, :]).reshape(-1)
    image_index = lax.axis_index(DP) * image_count + images
    target = (image_index[:, None] == text_index[None, :]).astype(jnp.float32)
    logit_grad = jax.nn.sigmoid(logits) - target
    image_grad = lax.psum(multiplier[0] * jnp.dot(logit_grad, text_unit, precision=HIGH), TP)
    along = jnp.sum(image_unit * image_grad, axis=1, keepdims=True)
    pooled_grad = (image_grad - image_unit * along) / norm_img
    return rows_out, pooled_grad


def solution(mesh):
    fine = Mesh(mesh.devices.reshape(N_YH, N_Z, N_X, N_YL, N_CORE), DP + TP)
    placed = (
        P(DP, None),
        P(DP, None),
        P(DP, None),
        P(None, TP),
        P(TP, None),
        P(None, TP),
        P(TP, None),
        P(DP, None),
        P(),
        P(),
    )
    return jax.shard_map(per_device, mesh=fine, in_specs=placed, out_specs=(P(DP, None), P(DP, None)), check_vma=False)
```

time: 511 us -> 134 us (0.26)
  blocking collectives: 311 us -> 33.8 us
  waiting for transfers between devices: 127 us -> 21.2 us
  starting transfers between devices: 19.1 us -> 46.1 us
  between operations: 15.6 us -> 2.14 us
    all_gather x1 -> x2, blocking collectives: 311 us -> 19.1 us  [the longest x1 10.8 us: per_device(): lax.all_gather(arrived.reshape(quarter, width), TP, axis=0, tiled=True)]
    psum x2 -> x0, waiting for transfers between devices: 93.9 us -> none  [the longest x1 93.9 us: feed_forward(): summed = lax.psum(partial_out, 'tensor').astype(jnp.float32)]
    all_to_all x1 -> x4, starting transfers between devices: 19.1 us -> 40.4 us  [the longest x2 18 us: sum_scatter(): lax.all_to_all(partial.reshape(4, rows // 4, width), TP, 0, 0, tiled=True)]
    psum x0 -> x2, blocking collectives: none -> 14.7 us  [the longest x1 7.61 us: per_device(): lax.psum(multiplier[0] * jnp.dot(logit_grad, text_unit, precision=HIGH), TP)]
    all_to_all x1 -> x4, waiting for transfers between devices: 32.6 us -> 19.4 us  [the longest x2 11 us: sum_scatter(): lax.all_to_all(partial.reshape(4, rows // 4, width), TP, 0, 0, tiled=True)]
    ppermute x0 -> x2, starting transfers between devices: none -> 5.77 us  [swap_quarters(): return lax.ppermute(values, ('x',) + TP, pairs)]
    dot_general x6 -> x7, matrix products: 10.9 us -> 11.7 us  [the longest x1 5.7 us: per_device(): jnp.dot(hidden, w_fc2, preferred_element_type=jnp.float32)]
  transfers between devices with their start and end apart: 3 -> 6, of which waited for: 2 -> 5; matrix products, arithmetic and copies ran while one was open for 1% -> 8% of each run, Pallas kernels for 0% -> 0%
where the time goes in v1:
time: 134 us; the launch traced here: 133 us
  starting transfers between devices  46.1 us (34%)
  blocking collectives  33.8 us (25%)
  waiting for transfers between devices  21.2 us (16%)
  matrix products  18 us (13%)
  local copies, waits for them, and re-layouts  6.86 us (5%)
  other arithmetic  5.17 us (4%)
  between operations  2.14 us (2%)
    all_to_all x2, starting transfers between devices, sum_scatter(): lax.all_to_all(partial.reshape(4, rows // 4, width), TP, 0, 0, tiled=True)  18 us
    all_to_all x1, starting transfers between devices, per_device(): lax.all_to_all(jnp.broadcast_to(my_texts[None], (ring,) + my_texts.shape)...  12.5 us
    all_to_all x2, waiting for transfers between devices, sum_scatter(): lax.all_to_all(partial.reshape(4, rows // 4, width), TP, 0, 0, tiled=True)  11 us
    all_gather x1, blocking collectives, per_device(): lax.all_gather(arrived.reshape(quarter, width), TP, axis=0, tiled=True)  10.8 us
    all_to_all x1, starting transfers between devices, per_device(): arrived = lax.all_to_all(outgoing, RING, 0, 0, tiled=True)  9.93 us
    all_gather x1, blocking collectives, per_device(): normed_two = lax.all_gather(normed_own, TP, axis=0, tiled=True)  8.33 us
    all_to_all x1, waiting for transfers between devices, per_device(): arrived = lax.all_to_all(outgoing, RING, 0, 0, tiled=True)  7.63 us
    psum x1, blocking collectives, per_device(): lax.psum(multiplier[0] * jnp.dot(logit_grad, text_unit, precision=HIGH), TP)  7.61 us
  transfers between devices with their start and end apart: 6, of which 5 were waited for; matrix products, arithmetic and copies ran while one was open for 8% of the time, Pallas kernels for 0%

profile of v1, /device:TPU:1, one launch (start us, length us, event | category | flops | bytes accessed | tf_op | source)
XLA Modules:
  0.0 133.4 jit_solution(9643775347697913670)
XLA Ops:
  0.7 0.9 fusion.46
  1.5 0.1 select_reduce_fusion
  1.6 1.5 %convert_reduce_fusion = (f32[256]{0:T(256)S(1)}, bf16[256,1152]{1,0:T(8,128)(2,1)S(1)}) fusion(bf16[256,1152]{1,0:T(8,128)(2,1)} %param.10, s32[256]{0:T(256)S(1)} %bitcast.54), kind=kOutput, calls=%fused_computation.8 | convolution fusion | flops 151944960 | bytes 1181696 | tf_op jit(solution)/shard_map/dot_general | solution.py:55
  3.1 0.3 fusion.6
  3.4 0.2 reduce-window.8
  3.7 0.1 broadcast_compare_fusion
  3.8 2.4 %convolution_convert_fusion.3 = bf16[256,864]{0,1:T(8,128)(2,1)S(1)} fusion(bf16[1152,864]{0,1:T(8,128)(2,1)} %param.13, bf16[256,1152]{1,0:T(8,128)(2,1)S(1)} %get-tuple-element.9, f32[256]{0:T(256)S(1)} %add_rsqrt_fusion, f32[256]{0:T(256)S(1)} %broadcast_multiply_fusion), kind=kOutput, calls=%fused_computation.14 | convolution fusion | flops 511008768 | bytes 3024896 | tf_op jit(solution)/shard_map/dot_general | solution.py:62
  6.3 0.8 copy-done.2
  7.0 1.4 %fusion.5 = f32[4,256,256]{1,2,0:T(8,128)} fusion(pred[256,256]{0,1:T(8,128)(4,1)S(1)} %broadcast_compare_fusion, bf16[256,3,4,72]{0,3,2,1:T(8,128)(2,1)S(1)} %bitcast.49), kind=kOutput, calls=%fused_computation.13 | convolution fusion | flops 38273024 | bytes 1409024 | tf_op jit(solution)/shard_map/qhd,khd->hqk/dot_general | solution.py:65
  8.4 1.5 %fusion.60 = f32[4,256]{1,0:T(4,128)S(1)} fusion(pred[256,256]{0,1:T(8,128)(4,1)S(1)} %broadcast_compare_fusion, bf16[256,3,4,72]{0,3,2,1:T(8,128)(2,1)} %bitcast.50), kind=kOutput, calls=%fused_computation.112 | convolution fusion | flops 38797568 | bytes 364544 | tf_op jit(solution)/shard_map/sub | solution.py:69
  9.9 2.0 %convolution_convert_fusion.4 = bf16[4,72,256]{2,1,0:T(8,128)(2,1)S(1)} fusion(f32[4,256]{1,0:T(4,128)S(1)} %fusion.60, bf16[256,3,4,72]{0,3,2,1:T(8,128)(2,1)} %bitcast.51, f32[4,256,256]{1,2,0:T(8,128)} %fusion.5), kind=kOutput, calls=%fused_computation.19 | convolution fusion | flops 38610176 | bytes 2396160 | tf_op jit(solution)/shard_map/hqk,khd->qhd/dot_general | solution.py:71
  11.9 2.4 %convolution_convert_fusion.1 = bf16[256,1152]{1,0:T(8,128)(2,1)} fusion(bf16[256,288]{0,1:T(8,128)(2,1)S(1)} %bitcast.52, bf16[288,1152]{1,0:T(8,128)(2,1)} %param.14), kind=kOutput, calls=%fused_computation.2 | convolution fusion | flops 170164224 | bytes 1400832 | tf_op jit(solution)/shard_map/dot_general | solution.py:73
  14.3 11.0 %all-to-all-start = ((bf16[4,64,1152]{2,1,0:T(8,128)(2,1)}), bf16[4,64,1152]{2,1,0:T(8,128)(2,1)}, u32[]{:S(2)}, u32[]{:S(2)}) async-start(bf16[4,64,1152]{2,1,0:T(8,128)(2,1)} %bitcast.47), calls=%async_computation | async-start | bytes 1179648 | tf_op jit(solution)/shard_map/all_to_all | solution.py:35
  25.3 1.9 %collective-permute-start.1 = (bf16[2,1152]{1,0:T(2,128)(2,1)S(1)}, bf16[2,1152]{1,0:T(2,128)(2,1)S(1)}, u32[]{:S(2)}, u32[]{:S(2)}) collective-permute-start(bf16[2,1152]{1,0:T(2,128)(2,1)S(1)} %copy-done.4), channel_id=1, source_target_pairs={{0,0},{1,4},{2,8},{3,12},{4,1},{5,5},{6,9},{7,13},{8,2},{9,6},{10,... | collective-permute-start | bytes 13832 | tf_op jit(solution)/shard_map/ppermute | solution.py:30
  28.8 1.8 %collective-permute-done.1 = bf16[2,1152]{1,0:T(2,128)(2,1)S(1)} collective-permute-done((bf16[2,1152]{1,0:T(2,128)(2,1)S(1)}, bf16[2,1152]{1,0:T(2,128)(2,1)S(1)}, u32[]{:S(2)}, u32[]{:S(2)}) %collective-permute-start.1) | collective-permute-done | bytes 4640 | tf_op jit(solution)/shard_map/ppermute | solution.py:30
  30.6 3.5 %all-to-all-done = bf16[4,64,1152]{2,1,0:T(8,128)(2,1)} async-done(((bf16[4,64,1152]{2,1,0:T(8,128)(2,1)}), bf16[4,64,1152]{2,1,0:T(8,128)(2,1)}, u32[]{:S(2)}, u32[]{:S(2)}) %all-to-all-start) | async-done | bytes 589856 | tf_op jit(solution)/shard_map/all_to_all | solution.py:35
  34.1 0.7 broadcast_in_dim.26
  34.8 12.5 %all-to-all-start.3 = ((bf16[32,2,1152]{2,1,0:T(2,128)(2,1)}), bf16[32,2,1152]{2,1,0:T(2,128)(2,1)S(1)}, u32[]{:S(2)}, u32[]{:S(2)}) async-start(bf16[32,2,1152]{2,1,0:T(2,128)(2,1)} %broadcast_in_dim.26), calls=%async_computation.3 | async-start | bytes 294912 | tf_op jit(solution)/shard_map/all_to_all | solution.py:58
  47.3 1.2 convert_reduce_fusion.2
  48.5 0.1 convert_reduce_fusion.3
  48.6 0.2 fusion.34
  48.9 0.1 fusion.35
  49.0 8.3 %all_gather.6 = bf16[256,1152]{1,0:T(8,128)(2,1)S(1)} all-gather(bf16[64,1152]{1,0:T(8,128)(2,1)S(1)} %fusion.35), channel_id=1, replica_groups=mesh['yh'=2,'z'=16,'x'=4,'yl'=2,'core'=2] {'yl','core'}, dimensions={0}, use_global_device_ids=true | all-gather | bytes 737280 | tf_op jit(solution)/shard_map/all_gather | solution.py:79
  57.3 5.7 %convolution_convert_fusion = bf16[256,1152]{1,0:T(8,128)(2,1)} fusion(bf16[1076,1152]{1,0:T(8,128)(2,1)S(1)} %copy-done, bf16[256,1152]{1,0:T(8,128)(2,1)S(1)} %all_gather.6, bf16[1152,1076]{0,1:T(8,128)(2,1)} %param.15), kind=kOutput, calls=%fused_computation.1 | convolution fusion | flops 1272075264 | bytes 6137856 | tf_op jit(solution)/shard_map/dot_general | solution.py:83
  63.0 0.7 all-to-all-done.3
  63.7 7.0 %all-to-all-start.1 = ((bf16[4,64,1152]{2,1,0:T(8,128)(2,1)}), bf16[4,64,1152]{2,1,0:T(8,128)(2,1)S(1)}, u32[]{:S(2)}, u32[]{:S(2)}) async-start(bf16[4,64,1152]{2,1,0:T(8,128)(2,1)} %bitcast.48), calls=%async_computation.1 | async-start | bytes 1179648 | tf_op jit(solution)/shard_map/all_to_all | solution.py:35
  70.7 0.2 multiply_reduce_fusion
  71.0 0.1 sqrt.21
  71.1 0.8 reshape.186
  71.8 7.6 %all-to-all-done.1 = bf16[4,64,1152]{2,1,0:T(8,128)(2,1)S(1)} async-done(((bf16[4,64,1152]{2,1,0:T(8,128)(2,1)}), bf16[4,64,1152]{2,1,0:T(8,128)(2,1)S(1)}, u32[]{:S(2)}, u32[]{:S(2)}) %all-to-all-start.1) | async-done | bytes 589856 | tf_op jit(solution)/shard_map/all_to_all | solution.py:35
  79.5 0.1 convert_reduce_fusion.4
  79.6 3.9 %collective-permute-start = (bf16[64,1152]{1,0:T(8,128)(2,1)S(1)}, bf16[64,1152]{1,0:T(8,128)(2,1)S(1)}, u32[]{:S(2)}, u32[]{:S(2)}) collective-permute-start(bf16[64,1152]{1,0:T(8,128)(2,1)S(1)} %get-tuple-element.3), channel_id=1, source_target_pairs={{0,0},{1,4},{2,8},{3,12},{4,1},{5,5},{6,9},{7,13},{8,2},{9,6},{10,... | collective-permute-start | bytes 442376 | tf_op jit(solution)/shard_map/ppermute | solution.py:30
  83.5 0.2 fusion.36
  83.7 0.3 fusion.37
  84.0 7.0 %psum.14 = f32[2,1152]{1,0:T(2,128)S(1)} all-reduce(f32[2,1152]{1,0:T(2,128)S(1)} %fusion.37), channel_id=1, replica_groups=mesh['yh'=2,'z'=16,'x'=4,'yl'=2,'core'=2] {'yl','core'}, use_global_device_ids=true, to_apply=%region_13.14 | all-reduce | flops 2304 | bytes 18432 | tf_op jit(solution)/shard_map/psum | solution.py:94
  91.1 0.2 fusion.43
  91.3 0.4 fusion.13
  91.7 0.4 convolution_multiply_fusion
  92.2 0.7 reshape.182
  92.9 9.9 %all-to-all-start.2 = ((bf16[32,2,1152]{2,1,0:T(2,128)(2,1)}), bf16[32,2,1152]{2,1,0:T(2,128)(2,1)S(1)}, u32[]{:S(2)}, u32[]{:S(2)}) async-start(bf16[32,2,1152]{2,1,0:T(2,128)(2,1)} %reshape.182), calls=%async_computation.2 | async-start | bytes 294912 | tf_op jit(solution)/shard_map/all_to_all | solution.py:87
  102.8 7.6 %psum.15 = f32[2,1152]{1,0:T(2,128)S(1)} all-reduce(f32[2,1152]{1,0:T(2,128)S(1)} %convolution_multiply_fusion), channel_id=1, replica_groups=mesh['yh'=2,'z'=16,'x'=4,'yl'=2,'core'=2] {'yl','core'}, use_global_device_ids=true, to_apply=%region_16.17 | all-reduce | flops 2304 | bytes 18432 | tf_op jit(solution)/shard_map/psum | solution.py:104
  110.4 0.2 multiply_reduce_fusion.1
  110.6 0.7 subtract_divide_fusion
  111.3 7.6 %all-to-all-done.2 = bf16[32,2,1152]{2,1,0:T(2,128)(2,1)S(1)} async-done(((bf16[32,2,1152]{2,1,0:T(2,128)(2,1)}), bf16[32,2,1152]{2,1,0:T(2,128)(2,1)S(1)}, u32[]{:S(2)}, u32[]{:S(2)}) %all-to-all-start.2) | async-done | bytes 147488 | tf_op jit(solution)/shard_map/all_to_all | solution.py:87
  119.0 10.8 %all_gather.7 = bf16[256,1152]{1,0:T(8,128)(2,1)S(1)} all-gather(bf16[64,1152]{1,0:T(8,128)(2,1)S(1)} %reshape.183), channel_id=1, replica_groups=mesh['yh'=2,'z'=16,'x'=4,'yl'=2,'core'=2] {'yl','core'}, dimensions={0}, use_global_device_ids=true | all-gather | bytes 737280 | tf_op jit(solution)/shard_map/all_gather | solution.py:88
  129.8 1.0 reshape.184
  130.9 1.5 %copy.20 = bf16[32,4,2,1152]{3,2,1,0:T(2,128)(2,1)S(1)} copy(bf16[32,4,2,1152]{3,2,0,1:T(2,128)(2,1)} %bitcast.46) | data formatting | bytes 1179648 | tf_op jit(solution)/shard_map/transpose | solution.py:89
  132.3 1.0 reshape.185
  (27 shorter events, 0.6 us)
Async XLA Ops:
  0.6 56.7 %copy-start = (bf16[1076,1152]{1,0:T(8,128)(2,1)S(1)}, bf16[1076,1152]{1,0:T(8,128)(2,1)}, u32[]{:S(2)}) copy-start(bf16[1076,1152]{1,0:T(8,128)(2,1)} %param.16) | copy-start | bytes 7437316
  0.6 2.8 %copy-start.3 = (s32[1,2]{1,0:T(1,128)S(1)}, s32[1,2]{1,0:T(1,128)}, u32[]{:S(2)}) copy-start(s32[1,2]{1,0:T(1,128)} %param.11) | copy-start | bytes 28
  6.2 0.8 copy-start.2
  11.9 13.4 %copy-start.4 = (bf16[2,1152]{1,0:T(2,128)(2,1)S(1)}, bf16[2,1152]{1,0:T(2,128)(2,1)}, u32[]{:S(2)}) copy-start(bf16[2,1152]{1,0:T(2,128)(2,1)} %param.17) | copy-start | bytes 13828
  14.3 19.8 %all-to-all-start = ((bf16[4,64,1152]{2,1,0:T(8,128)(2,1)}), bf16[4,64,1152]{2,1,0:T(8,128)(2,1)}, u32[]{:S(2)}, u32[]{:S(2)}) async-start(bf16[4,64,1152]{2,1,0:T(8,128)(2,1)} %bitcast.47), calls=%async_computation | async-start | bytes 1179648 | tf_op jit(solution)/shard_map/all_to_all | solution.py:35
  25.3 5.3 %collective-permute-start.1 = (bf16[2,1152]{1,0:T(2,128)(2,1)S(1)}, bf16[2,1152]{1,0:T(2,128)(2,1)S(1)}, u32[]{:S(2)}, u32[]{:S(2)}) collective-permute-start(bf16[2,1152]{1,0:T(2,128)(2,1)S(1)} %copy-done.4), channel_id=1, source_target_pairs={{0,0},{1,4},{2,8},{3,12},{4,1},{5,5},{6,9},{7,13},{8,2},{9,6},{10,... | collective-permute-start | bytes 13832 | tf_op jit(solution)/shard_map/ppermute | solution.py:30
  34.8 28.9 %all-to-all-start.3 = ((bf16[32,2,1152]{2,1,0:T(2,128)(2,1)}), bf16[32,2,1152]{2,1,0:T(2,128)(2,1)S(1)}, u32[]{:S(2)}, u32[]{:S(2)}) async-start(bf16[32,2,1152]{2,1,0:T(2,128)(2,1)} %broadcast_in_dim.26), calls=%async_computation.3 | async-start | bytes 294912 | tf_op jit(solution)/shard_map/all_to_all | solution.py:58
  63.7 15.7 %all-to-all-start.1 = ((bf16[4,64,1152]{2,1,0:T(8,128)(2,1)}), bf16[4,64,1152]{2,1,0:T(8,128)(2,1)S(1)}, u32[]{:S(2)}, u32[]{:S(2)}) async-start(bf16[4,64,1152]{2,1,0:T(8,128)(2,1)} %bitcast.48), calls=%async_computation.1 | async-start | bytes 1179648 | tf_op jit(solution)/shard_map/all_to_all | solution.py:35
  71.8 19.5 %copy-start.1 = (f32[64,1152]{1,0:T(8,128)S(1)}, f32[64,1152]{1,0:T(8,128)}, u32[]{:S(2)}) copy-start(f32[64,1152]{1,0:T(8,128)} %reshape.186) | copy-start | bytes 884740
  79.6 12.5 %collective-permute-start = (bf16[64,1152]{1,0:T(8,128)(2,1)S(1)}, bf16[64,1152]{1,0:T(8,128)(2,1)S(1)}, u32[]{:S(2)}, u32[]{:S(2)}) collective-permute-start(bf16[64,1152]{1,0:T(8,128)(2,1)S(1)} %get-tuple-element.3), channel_id=1, source_target_pairs={{0,0},{1,4},{2,8},{3,12},{4,1},{5,5},{6,9},{7,13},{8,2},{9,6},{10,... | collective-permute-start | bytes 442376 | tf_op jit(solution)/shard_map/ppermute | solution.py:30
  92.9 26.1 %all-to-all-start.2 = ((bf16[32,2,1152]{2,1,0:T(2,128)(2,1)}), bf16[32,2,1152]{2,1,0:T(2,128)(2,1)S(1)}, u32[]{:S(2)}, u32[]{:S(2)}) async-start(bf16[32,2,1152]{2,1,0:T(2,128)(2,1)} %reshape.182), calls=%async_computation.2 | async-start | bytes 294912 | tf_op jit(solution)/shard_map/all_to_all | solution.py:87

commit v2 on v1

v2 whole, which is shorter than its diff:
```python
import functools
import math

import jax
import jax.numpy as jnp
from jax import lax
from jax.experimental import pallas as pl
from jax.experimental.pallas import tpu as pltpu
from jax.sharding import Mesh
from jax.sharding import PartitionSpec as P

HEAD_DIM = 72
N_YH, N_Z, N_X, N_YL, N_CORE = 2, 16, 4, 2, 2
DP = ("yh", "z", "x")
TP = ("yl", "core")
RING = ("yh", "z")
HIGH = lax.Precision.HIGHEST
F32, BF16, I32 = jnp.float32, jnp.bfloat16, jnp.int32
VMEM = pl.BlockSpec(memory_space=pltpu.VMEM)
SMEM = pl.BlockSpec(memory_space=pltpu.SMEM)
CONTRACT_LAST = (((1,), (1,)), ((), ()))
CONTRACT_FIRST = (((0,), (0,)), ((), ()))
BIG = 28 * 2**20


def layer_norm(values):
    mean_val = jnp.mean(values, axis=-1, keepdims=True)
    centred = values - mean_val
    var_val = jnp.mean(centred * centred, axis=-1, keepdims=True)
    return centred * lax.rsqrt(var_val + 1e-06)


def unit_rows(values):
    return values / jnp.sqrt(jnp.sum(values * values, axis=1, keepdims=True) + 1e-06)


def swap_quarters(values, flip=0):
    pairs = [(x * N_X + t, (t ^ flip) * N_X + x) for x in range(N_X) for t in range(N_X)]
    return lax.ppermute(values, ("x",) + TP, pairs)


def attend_kernel(place, counts, slots, rows, w_qkv, w_out, keep, send, half, member, packed, part):
    n = rows.shape[0]
    core = place[0]
    slot = slots[...]
    peer = slot >> 1
    order = (peer & 1) * 128 + ((peer >> 1) & 1) * 64 + (peer >> 2) * 2 + (slot & 1)
    moved = jnp.where(lax.broadcasted_iota(I32, (n, n), 0) == order, 1.0, 0.0).astype(BF16)
    first, second = counts[0, 0], counts[0, 0] + counts[0, 1]

    def segment_of(position):
        return jnp.where(position >= first, 1.0, 0.0) + jnp.where(position >= second, 1.0, 0.0)

    seg_lanes = lax.dot_general(
        segment_of(lax.broadcasted_iota(I32, (8, n), 1)).astype(BF16), moved, CONTRACT_LAST, preferred_element_type=F32
    )
    seg_rows = jnp.dot(
        moved, segment_of(lax.broadcasted_iota(I32, (n, 128), 0)).astype(BF16), preferred_element_type=F32
    )
    same = seg_rows[:, :1] == seg_lanes[:1, :]
    ordered = jnp.dot(moved, rows[...], preferred_element_type=F32)
    packed[...] = ordered.astype(BF16)
    normed = layer_norm(ordered).astype(BF16)
    qkv = jnp.dot(normed, w_qkv[...], preferred_element_type=F32)
    heads = w_out.shape[0] // HEAD_DIM
    width = heads * HEAD_DIM
    outs = []
    for h in range(heads):
        q, k, v = (qkv[:, i * width + h * HEAD_DIM : i * width + (h + 1) * HEAD_DIM].astype(BF16) for i in range(3))
        scores = lax.dot_general(q, k, CONTRACT_LAST, preferred_element_type=F32) * (1.0 / math.sqrt(HEAD_DIM))
        scores = jnp.where(same, scores, -1e30)
        raised = jnp.exp(scores - jnp.max(scores, axis=-1, keepdims=True))
        total = jnp.sum(raised, axis=-1, keepdims=True)
        outs.append(jnp.dot(raised.astype(BF16), v, preferred_element_type=F32) / total)
    attended = jnp.concatenate(outs, axis=1).astype(BF16)
    part[...] = jnp.dot(attended, w_out[...], preferred_element_type=F32).astype(BF16)
    mine, other = pl.multiple_of(core * 128, 128), pl.multiple_of(128 - core * 128, 128)
    keep[...] = part[pl.ds(mine, 128), :]
    send[...] = part[pl.ds(other, 128), :]
    half[...] = packed[pl.ds(mine, 128), :]
    images = lax.broadcasted_iota(I32, (n, 128), 1).astype(F32)
    packed[:, :128] = jnp.where(seg_rows == images, 1.0, 0.0).astype(BF16)
    member[...] = packed[pl.ds(mine, 128), :128]


def mlp_kernel(place, half, own_sum, far_sum, member, w1a, w1b, w2a, w2b, first_out, second_out, resid, part):
    base = half[...].astype(F32) + own_sum[...].astype(F32) + far_sum[...].astype(F32)
    resid[...] = base.astype(BF16)
    normed = layer_norm(resid[...].astype(F32)).astype(BF16)
    total = None
    for w1, w2 in ((w1a, w2a), (w1b, w2b)):
        hidden = jax.nn.gelu(jnp.dot(normed, w1[...], preferred_element_type=F32), approximate=True).astype(BF16)
        piece = jnp.dot(hidden, w2[...], preferred_element_type=F32)
        total = piece if total is None else total + piece
    part[...] = total
    yl = place[1]
    mine, other = pl.multiple_of(yl * 64, 64), pl.multiple_of(64 - yl * 64, 64)
    width = half.shape[1]
    first_out[:, :width] = (part[pl.ds(mine, 64), :] + resid[pl.ds(mine, 64), :].astype(F32)).astype(BF16)
    first_out[:, width:] = member[pl.ds(mine, 64), :]
    second_out[...] = part[pl.ds(other, 64), :].astype(BF16)


def pool_kernel(first, second, pooled):
    width = second.shape[1]
    layer = (first[:, :width].astype(F32) + second[...].astype(F32)).astype(BF16)
    member = first[:, width:].astype(F32)
    full = lax.dot_general(
        member, layer_norm(layer.astype(F32)), CONTRACT_FIRST, precision=HIGH, preferred_element_type=F32
    )
    pooled[...] = full[:8]


def loss_kernel(image_base, text_base, counts, multiplier, shift, pooled_sum, texts, partial):
    row8 = lax.broadcasted_iota(I32, (8, 1), 0)
    count = jnp.where(row8 == 0, counts[0, 0], counts[0, 1]).astype(F32)
    pooled = pooled_sum[...] / count
    norm_img = jnp.sqrt(jnp.sum(pooled * pooled, axis=1, keepdims=True) + 1e-06)
    unit = pooled / norm_img
    text_unit = unit_rows(texts[...].astype(F32))
    logits = (
        multiplier[0] * lax.dot_general(unit, text_unit, CONTRACT_LAST, precision=HIGH, preferred_element_type=F32)
        + shift[0]
    )
    n_text = texts.shape[0]
    col = lax.broadcasted_iota(I32, (8, n_text), 1)
    text_index = (col >> 1) * (2 * N_X) + (col & 1) + text_base[0]
    image_index = lax.broadcasted_iota(I32, (8, n_text), 0) + image_base[0]
    slope = 1.0 / (1.0 + jnp.exp(-logits)) - jnp.where(text_index == image_index, 1.0, 0.0)
    grad = multiplier[0] * jnp.dot(slope, text_unit, precision=HIGH, preferred_element_type=F32)
    partial[...] = (grad - unit * jnp.sum(unit * grad, axis=1, keepdims=True)) / norm_img


def call(kernel, specs, outs, scratch=(), limit=None):
    many = isinstance(outs, list)
    return pl.pallas_call(
        kernel,
        in_specs=specs,
        out_specs=[VMEM] * len(outs) if many else VMEM,
        out_shape=outs,
        scratch_shapes=list(scratch),
        compiler_params=pltpu.CompilerParams(vmem_limit_bytes=limit),
    )


def per_device(rows_in, patch_counts, row_slots, w_qkv, w_out, w_fc1, w_fc2, text_embeds, multiplier, shift):
    row_count, width = rows_in.shape
    half_rows, quarter, ring = row_count // 2, row_count // 4, N_YH * N_Z
    shape = jax.ShapeDtypeStruct
    my_t, my_dp = lax.axis_index(TP), lax.axis_index(DP)
    place = jnp.stack([lax.axis_index("core"), lax.axis_index("yl")]).astype(I32)
    pair = [(0, 1), (1, 0)]

    my_texts = swap_quarters(text_embeds)

    keep, send, half, member = call(
        attend_kernel,
        [SMEM, SMEM, VMEM, VMEM, VMEM, VMEM],
        [
            shape((half_rows, width), BF16),
            shape((half_rows, width), BF16),
            shape((half_rows, width), BF16),
            shape((half_rows, 128), BF16),
        ],
        [pltpu.VMEM((row_count, width), BF16), pltpu.VMEM((row_count, width), BF16)],
        BIG,
    )(place, patch_counts, row_slots, rows_in, w_qkv, w_out)

    got = lax.ppermute(send, "core", pair)
    own_sum = (keep.astype(F32) + got.astype(F32)).astype(BF16)
    far_sum = lax.ppermute(own_sum, "yl", pair)
    w1b = lax.ppermute(w_fc1, "core", pair)
    w2b = lax.ppermute(w_fc2, "core", pair)
    spread = jnp.broadcast_to(my_texts[None], (ring,) + my_texts.shape)
    texts = lax.all_to_all(spread, RING, 0, 0, tiled=True).reshape(ring * 2, width)

    first, second = call(
        mlp_kernel,
        [SMEM] + [VMEM] * 8,
        [shape((quarter, width + 128), BF16), shape((quarter, width), BF16)],
        [pltpu.VMEM((half_rows, width), BF16), pltpu.VMEM((half_rows, width), F32)],
        BIG,
    )(place, half, own_sum, far_sum, member, w_fc1, w1b, w_fc2, w2b)

    first = swap_quarters(first)
    second = swap_quarters(second, 2)
    layer = (first[:, :width].astype(F32) + second.astype(F32)).astype(BF16)
    arrived = lax.all_to_all(layer.reshape(ring, 2, width), RING, 0, 0, tiled=True)
    rows_out = lax.all_gather(arrived, TP, axis=1, tiled=False).reshape(row_count, width)

    pooled = call(pool_kernel, [VMEM] * 2, shape((8, width), F32))(first, second)
    pooled = lax.psum(swap_quarters(pooled), TP)
    image_base = (my_dp * 2).astype(I32).reshape(1)
    text_base = (my_t * 2).astype(I32).reshape(1)
    partial = call(loss_kernel, [SMEM] * 5 + [VMEM] * 2, shape((8, width), F32))(
        image_base, text_base, patch_counts, multiplier, shift, pooled, texts
    )
    return rows_out, lax.psum(partial[:2], TP)


def solution(mesh):
    fine = Mesh(mesh.devices.reshape(N_YH, N_Z, N_X, N_YL, N_CORE), DP + TP)
    placed = (
        P(DP, None),
        P(DP, None),
        P(DP, None),
        P(None, TP),
        P(TP, None),
        P(None, TP),
        P(TP, None),
        P(DP, None),
        P(),
        P(),
    )
    return jax.shard_map(per_device, mesh=fine, in_specs=placed, out_specs=(P(DP, None), P(DP, None)), check_vma=False)
```

time: 134 us -> 135 us (level)
  matrix products: 18 us -> 0 us
  local copies, waits for them, and re-layouts: 6.86 us -> 20.4 us
  Pallas kernels: 0 us -> 13.1 us
  other arithmetic: 5.17 us -> 0.2 us
  blocking collectives: 33.8 us -> 32.3 us
  starting transfers between devices: 46.1 us -> 44.7 us
    all_to_all x4 -> x2, starting transfers between devices: 40.4 us -> 16.6 us  [the longest x1 12.7 us: per_device(): lax.all_to_all(spread, RING, 0, 0, tiled=True).reshape(ring * 2, width)]
    dot_general x9 -> x0, matrix products: 16.5 us -> none  [the longest x1 5.7 us: per_device(): jnp.dot(hidden, w_fc2, preferred_element_type=jnp.float32)]
    ppermute x0 -> x4, starting transfers between devices: none -> 15.2 us  [the longest x1 8.92 us: per_device(): w1b = lax.ppermute(w_fc1, 'core', pair)]
    pallas_call x0 -> x4, Pallas kernels: none -> 13.1 us  [the longest x1 4.68 us: per_device(): call(mlp_kernel, [SMEM] + [VMEM] * 8, [shape((quarter, width + 128), BF16...]
    all_gather x2 -> x1, blocking collectives: 19.1 us -> 8.33 us  [per_device(): lax.all_gather(arrived, TP, axis=1, tiled=False).reshape(row_count, width)]
    unnamed x10 -> x28, local copies, waits for them, and re-layouts: 0.78 us -> 11.2 us
    psum x2, blocking collectives: 14.7 us -> 24 us  [the longest x1 17.7 us: per_device(): pooled = lax.psum(swap_quarters(pooled), TP)]
    ppermute x2 -> x4, starting transfers between devices: 5.77 us -> 12.9 us  [swap_quarters(): return lax.ppermute(values, ('x',) + TP, pairs)]
  transfers between devices with their start and end apart: 6 -> 10, of which waited for: 5 -> 4; matrix products, arithmetic and copies ran while one was open for 8% -> 11% of each run, Pallas kernels for 0% -> 6%
where the time goes in v2:
time: 135 us; the launch traced here: 134 us
  starting transfers between devices  44.7 us (33%)
  blocking collectives  32.3 us (24%)
  waiting for transfers between devices  20.6 us (15%)
  local copies, waits for them, and re-layouts  20.4 us (15%)
  Pallas kernels  13.1 us (10%)
  between operations  2.23 us (2%)
    psum x1, blocking collectives, per_device(): pooled = lax.psum(swap_quarters(pooled), TP)  17.7 us
    all_to_all x1, waiting for transfers between devices, per_device(): lax.all_to_all(spread, RING, 0, 0, tiled=True).reshape(ring * 2, width)  15.7 us
    ppermute x4, starting transfers between devices, swap_quarters(): return lax.ppermute(values, ('x',) + TP, pairs)  12.9 us
    all_to_all x1, starting transfers between devices, per_device(): lax.all_to_all(spread, RING, 0, 0, tiled=True).reshape(ring * 2, width)  12.7 us
    unnamed x28, local copies, waits for them, and re-layouts  11.2 us
    ppermute x1, starting transfers between devices, per_device(): w1b = lax.ppermute(w_fc1, 'core', pair)  8.92 us
    all_gather x1, blocking collectives, per_device(): lax.all_gather(arrived, TP, axis=1, tiled=False).reshape(row_count, width)  8.33 us
    psum x1, blocking collectives, per_device(): return (rows_out, lax.psum(partial[:2], TP))  6.25 us
  transfers between devices with their start and end apart: 10, of which 4 were waited for; matrix products, arithmetic and copies ran while one was open for 11% of the time, Pallas kernels for 6%

profile of v2, /device:TPU:1, one launch (start us, length us, event | category | flops | bytes accessed | tf_op | source)
XLA Modules:
  0.0 133.5 jit_solution(7368857199917724454)
XLA Ops:
  0.6 0.0 copy-start.3
  0.6 0.0 copy-start.8
  0.7 0.0 copy-start.9
  0.7 8.9 %collective-permute-start.2 = (bf16[1152,1076]{0,1:T(8,128)(2,1)}, bf16[1152,1076]{0,1:T(8,128)(2,1)}, u32[]{:S(2)}, u32[]{:S(2)}) collective-permute-start(bf16[1152,1076]{0,1:T(8,128)(2,1)} %param.15), channel_id=1, source_target_pairs={{0,1},{1,0},{2,3},{3,2},{4,5},{5,4},{6,7},{7,6},{8,9},{9,8},{10,11... | collective-permute-start | bytes 7437320 | tf_op jit(solution)/shard_map/ppermute | solution.py:172
  9.6 1.9 %collective-permute-start.3 = (bf16[1076,1152]{1,0:T(8,128)(2,1)}, bf16[1076,1152]{1,0:T(8,128)(2,1)}, u32[]{:S(2)}, u32[]{:S(2)}) collective-permute-start(bf16[1076,1152]{1,0:T(8,128)(2,1)} %w2a.1), channel_id=1, source_target_pairs={{0,1},{1,0},{2,3},{3,2},{4,5},{5,4},{6,7},{7,6},{8,9},{9,8},{10,11... | collective-permute-start | bytes 7437320 | tf_op jit(solution)/shard_map/ppermute | solution.py:173
  11.5 2.9 %copy.24.w_qkv = bf16[1152,864]{1,0:T(8,128)(2,1)S(1)} copy(bf16[1152,864]{0,1:T(8,128)(2,1)} %param.13) | data formatting | bytes 3981312 | tf_op args[3]
  14.4 0.1 pad_add_fusion.place
  14.5 0.0 copy-done.8
  14.5 3.4 %shard_map.113 = (bf16[128,1152]{1,0:T(8,128)(2,1)S(1)}, bf16[128,1152]{1,0:T(8,128)(2,1)S(1)}, bf16[128,1152]{1,0:T(8,128)(2,1)S(1)}, bf16[128,128]{1,0:T(8,128)(2,1)S(1)}) custom-call(s32[2]{0:T(128)S(1)} %pad_add_fusion.place, s32[1,2]{1,0:T(1,128)S(1)} %copy-done.8, s32[1,256]{1,0:T(1,128)S(1)} %copy-done.9, bf16[256,1152]{1,0:T(8,128)(2,1)S(1)} %copy-done.3, ...), custom_call_target="tpu_custom_call" | custom-call | tf_op jit(solution)/shard_map/pallas_call | solution.py:156
  17.9 0.0 copy-start.4
  17.9 2.4 %collective-permute-start = (bf16[128,1152]{1,0:T(8,128)(2,1)S(1)}, bf16[128,1152]{1,0:T(8,128)(2,1)S(1)}, u32[]{:S(2)}, u32[]{:S(2)}) collective-permute-start(bf16[128,1152]{1,0:T(8,128)(2,1)S(1)} %get-tuple-element.10), channel_id=1, source_target_pairs={{0,1},{1,0},{2,3},{3,2},{4,5},{5,4},{6,7},{7,6},{8,9},{9,8},{10,11... | collective-permute-start | bytes 884744 | tf_op jit(solution)/shard_map/ppermute | solution.py:169
  20.3 1.2 collective-permute-done
  21.5 0.1 add_convert_fusion.own_sum
  21.6 1.9 %collective-permute-start.1 = (bf16[128,1152]{1,0:T(8,128)(2,1)S(1)}, bf16[128,1152]{1,0:T(8,128)(2,1)S(1)}, u32[]{:S(2)}, u32[]{:S(2)}) collective-permute-start(bf16[128,1152]{1,0:T(8,128)(2,1)S(1)} %add_convert_fusion.own_sum), channel_id=1, source_target_pairs={{0,2},{2,0},{1,3},{3,1},{4,6},{6,4},{5,7},{7,5},{8,10},{10,8},{9,1... | collective-permute-start | bytes 884744 | tf_op jit(solution)/shard_map/ppermute | solution.py:171
  23.5 4.1 %copy.25.w1a = bf16[1152,1076]{1,0:T(8,128)(2,1)S(1)} copy(bf16[1152,1076]{0,1:T(8,128)(2,1)} %param.15) | data formatting | bytes 4958208 | tf_op args[5]
  27.6 0.0 copy-start.5
  27.6 0.0 collective-permute-done.2
  27.7 5.2 %copy.26.w1b = bf16[1152,1076]{1,0:T(8,128)(2,1)} copy(bf16[1152,1076]{0,1:T(8,128)(2,1)} %collective-permute-done.2) | data formatting | bytes 4958208 | tf_op jit(solution)/shard_map/ppermute | solution.py:172
  32.9 0.0 collective-permute-done.1.far_sum
  32.9 0.0 collective-permute-done.3.w2b
  32.9 1.7 %copy-done = bf16[1152,1076]{1,0:T(8,128)(2,1)S(1)} copy-done((bf16[1152,1076]{1,0:T(8,128)(2,1)S(1)}, bf16[1152,1076]{1,0:T(8,128)(2,1)}, u32[]{:S(2)}) %copy-start) | copy-done | bytes 2479128
  34.7 1.7 %copy-done.1 = bf16[1076,1152]{1,0:T(8,128)(2,1)S(1)} copy-done((bf16[1076,1152]{1,0:T(8,128)(2,1)S(1)}, bf16[1076,1152]{1,0:T(8,128)(2,1)}, u32[]{:S(2)}) %copy-start.1) | copy-done | bytes 2479128
  36.4 0.8 copy-done.7
  37.1 4.7 %shard_map.114 = (bf16[64,1280]{1,0:T(8,128)(2,1)}, bf16[64,1152]{1,0:T(8,128)(2,1)}) custom-call(s32[2]{0:T(128)S(1)} %pad_add_fusion.place, bf16[128,1152]{1,0:T(8,128)(2,1)S(1)} %copy-done.5, bf16[128,1152]{1,0:T(8,128)(2,1)S(1)} %add_convert_fusion.own_sum, bf16[128,1152]{1,0:T(8,128)(2,1)S(1)} %collective-permute-done.1.far_sum, ...), custom_call_target="tpu_custom_call" | custom-call | tf_op jit(solution)/shard_map/pallas_call | solution.py:177
  41.8 1.9 %collective-permute-start.4 = (bf16[64,1280]{1,0:T(8,128)(2,1)}, bf16[64,1280]{1,0:T(8,128)(2,1)S(1)}, u32[]{:S(2)}, u32[]{:S(2)}) collective-permute-start(bf16[64,1280]{1,0:T(8,128)(2,1)} %get-tuple-element.12), channel_id=1, source_target_pairs={{0,0},{1,4},{2,8},{3,12},{4,1},{5,5},{6,9},{7,13},{8,2},{9,6},{10,... | collective-permute-start | bytes 491528 | tf_op jit(solution)/shard_map/ppermute | solution.py:39
  43.7 6.0 %collective-permute-start.5 = (bf16[64,1152]{1,0:T(8,128)(2,1)}, bf16[64,1152]{1,0:T(8,128)(2,1)S(1)}, u32[]{:S(2)}, u32[]{:S(2)}) collective-permute-start(bf16[64,1152]{1,0:T(8,128)(2,1)} %get-tuple-element.13), channel_id=1, source_target_pairs={{0,8},{1,12},{2,0},{3,4},{4,9},{5,13},{6,1},{7,5},{8,10},{9,14},{1... | collective-permute-start | bytes 442376 | tf_op jit(solution)/shard_map/ppermute | solution.py:39
  49.8 1.9 %collective-permute-start.7 = (bf16[2,1152]{1,0:T(2,128)(2,1)S(1)}, bf16[2,1152]{1,0:T(2,128)(2,1)S(1)}, u32[]{:S(2)}, u32[]{:S(2)}) collective-permute-start(bf16[2,1152]{1,0:T(2,128)(2,1)S(1)} %copy-done.12), channel_id=1, source_target_pairs={{0,0},{1,4},{2,8},{3,12},{4,1},{5,5},{6,9},{7,13},{8,2},{9,6},{10,... | collective-permute-start | bytes 13832 | tf_op jit(solution)/shard_map/ppermute | solution.py:39
  51.7 3.0 %collective-permute-done.7 = bf16[2,1152]{1,0:T(2,128)(2,1)S(1)} collective-permute-done((bf16[2,1152]{1,0:T(2,128)(2,1)S(1)}, bf16[2,1152]{1,0:T(2,128)(2,1)S(1)}, u32[]{:S(2)}, u32[]{:S(2)}) %collective-permute-start.7) | collective-permute-done | bytes 4640 | tf_op jit(solution)/shard_map/ppermute | solution.py:39
  54.7 0.7 broadcast_in_dim.2
  55.4 12.7 %all-to-all-start.1 = ((bf16[32,2,1152]{2,1,0:T(2,128)(2,1)}), bf16[32,2,1152]{2,1,0:T(2,128)(2,1)S(1)}, u32[]{:S(2)}, u32[]{:S(2)}) async-start(bf16[32,2,1152]{2,1,0:T(2,128)(2,1)} %broadcast_in_dim.2), calls=%async_computation.1 | async-start | bytes 294912 | tf_op jit(solution)/shard_map/all_to_all | solution.py:175
  68.2 0.0 collective-permute-done.5.second
  68.2 0.0 copy-start.11
  68.2 0.0 collective-permute-done.4.first
  68.2 0.0 copy-start.10
  68.3 0.7 reshape.20
  69.0 15.7 %all-to-all-done.1 = bf16[32,2,1152]{2,1,0:T(2,128)(2,1)S(1)} async-done(((bf16[32,2,1152]{2,1,0:T(2,128)(2,1)}), bf16[32,2,1152]{2,1,0:T(2,128)(2,1)S(1)}, u32[]{:S(2)}, u32[]{:S(2)}) %all-to-all-start.1) | async-done | bytes 147488 | tf_op jit(solution)/shard_map/all_to_all | solution.py:175
  84.7 3.9 %all-to-all-start = ((bf16[32,2,1152]{2,1,0:T(2,128)(2,1)}), bf16[32,2,1152]{2,1,0:T(2,128)(2,1)S(1)}, u32[]{:S(2)}, u32[]{:S(2)}) async-start(bf16[32,2,1152]{2,1,0:T(2,128)(2,1)} %reshape.20), calls=%async_computation | async-start | bytes 294912 | tf_op jit(solution)/shard_map/all_to_all | solution.py:188
  88.6 2.4 %shard_map.115 = f32[8,1152]{1,0:T(8,128)} custom-call(bf16[64,1280]{1,0:T(8,128)(2,1)} %copy-done.10, bf16[64,1152]{1,0:T(8,128)(2,1)} %copy-done.11), custom_call_target="tpu_custom_call" | custom-call | tf_op jit(solution)/shard_map/pallas_call | solution.py:191
  91.0 3.0 %collective-permute-start.6 = (f32[8,1152]{1,0:T(8,128)}, f32[8,1152]{1,0:T(8,128)S(1)}, u32[]{:S(2)}, u32[]{:S(2)}) collective-permute-start(f32[8,1152]{1,0:T(8,128)} %shard_map.115), channel_id=1, source_target_pairs={{0,0},{1,4},{2,8},{3,12},{4,1},{5,5},{6,9},{7,13},{8,2},{9,6},{10,... | collective-permute-start | bytes 110600 | tf_op jit(solution)/shard_map/ppermute | solution.py:39
  95.4 0.7 reshape.24.texts
  96.1 0.7 collective-permute-done.6
  96.8 17.7 %psum.14.pooled_sum = f32[8,1152]{1,0:T(8,128)} all-reduce(f32[8,1152]{1,0:T(8,128)S(1)} %collective-permute-done.6), channel_id=1, replica_groups=mesh['yh'=2,'z'=16,'x'=4,'yl'=2,'core'=2] {'yl','core'}, use_global_device_ids=true, to_apply=%region_0.0 | all-reduce | flops 9216 | bytes 73728 | tf_op jit(solution)/shard_map/psum | solution.py:192
  114.5 2.6 %shard_map.116 = f32[8,1152]{1,0:T(8,128)} custom-call(s32[1]{0:T(128)} %bitcast.3.image_base, s32[1]{0:T(128)} %bitcast.4.text_base, s32[1,2]{1,0:T(1,128)} %counts.3, f32[1]{0:T(128)S(6)} %copy.31.multiplier, f32[1]{0:T(128)S(6)} %copy.32.shift, f32[8,1152]{1,0:T(8,128)} %psum.14.pooled_sum, bf16[64,1152]{1,0:T(8,128)(2,1)} %reshape.24.texts), custom_call_target="tpu_custom_call" | custom-call | tf_op jit(solution)/shard_map/pallas_call | solution.py:195
  117.2 0.8 slice.9
  117.9 6.3 %psum.15 = f32[2,1152]{1,0:T(2,128)} all-reduce(f32[2,1152]{1,0:T(2,128)S(1)} %slice.9), channel_id=1, replica_groups=mesh['yh'=2,'z'=16,'x'=4,'yl'=2,'core'=2] {'yl','core'}, use_global_device_ids=true, to_apply=%region_1.0 | all-reduce | flops 2304 | bytes 18432 | tf_op jit(solution)/shard_map/psum | solution.py:198
  124.2 0.0 all-to-all-done
  124.2 8.3 %all-gather = bf16[32,8,1152]{2,0,1:T(8,128)(2,1)S(1)} all-gather(bf16[32,2,1152]{2,0,1:T(8,128)(2,1)S(1)} %copy.27), channel_id=2, replica_groups=mesh['yh'=2,'z'=16,'x'=4,'yl'=2,'core'=2] {'yl','core'}, dimensions={1}, use_global_device_ids=true | all-gather | bytes 737280 | tf_op jit(solution)/shard_map/all_gather | solution.py:189
  132.5 1.0 copy.30
  (17 shorter events, 0.1 us)
Async XLA Ops:
  0.6 13.9 %copy-start.3 = (bf16[256,1152]{1,0:T(8,128)(2,1)S(1)}, bf16[256,1152]{1,0:T(8,128)(2,1)}, u32[]{:S(2)}) copy-start(bf16[256,1152]{1,0:T(8,128)(2,1)} %rows.1) | copy-start | bytes 1769476
  0.6 13.9 %copy-start.8 = (s32[1,2]{1,0:T(1,128)S(1)}, s32[1,2]{1,0:T(1,128)}, u32[]{:S(2)}) copy-start(s32[1,2]{1,0:T(1,128)} %counts.3) | copy-start | bytes 28
  0.7 13.8 %copy-start.9 = (s32[1,256]{1,0:T(1,128)S(1)}, s32[1,256]{1,0:T(1,128)}, u32[]{:S(2)}) copy-start(s32[1,256]{1,0:T(1,128)} %slots.1) | copy-start | bytes 3076
  0.7 13.8 %copy-start.2 = (bf16[288,1152]{1,0:T(8,128)(2,1)S(1)}, bf16[288,1152]{1,0:T(8,128)(2,1)}, u32[]{:S(2)}) copy-start(bf16[288,1152]{1,0:T(8,128)(2,1)} %w_out.1) | copy-start | bytes 1990660
  0.7 27.0 %collective-permute-start.2 = (bf16[1152,1076]{0,1:T(8,128)(2,1)}, bf16[1152,1076]{0,1:T(8,128)(2,1)}, u32[]{:S(2)}, u32[]{:S(2)}) collective-permute-start(bf16[1152,1076]{0,1:T(8,128)(2,1)} %param.15), channel_id=1, source_target_pairs={{0,1},{1,0},{2,3},{3,2},{4,5},{5,4},{6,7},{7,6},{8,9},{9,8},{10,11... | collective-permute-start | bytes 7437320 | tf_op jit(solution)/shard_map/ppermute | solution.py:172
  9.6 23.3 %collective-permute-start.3 = (bf16[1076,1152]{1,0:T(8,128)(2,1)}, bf16[1076,1152]{1,0:T(8,128)(2,1)}, u32[]{:S(2)}, u32[]{:S(2)}) collective-permute-start(bf16[1076,1152]{1,0:T(8,128)(2,1)} %w2a.1), channel_id=1, source_target_pairs={{0,1},{1,0},{2,3},{3,2},{4,5},{5,4},{6,7},{7,6},{8,9},{9,8},{10,11... | collective-permute-start | bytes 7437320 | tf_op jit(solution)/shard_map/ppermute | solution.py:173
  17.9 3.7 %copy-start.4 = (bf16[128,1152]{1,0:T(8,128)(2,1)}, bf16[128,1152]{1,0:T(8,128)(2,1)S(1)}, u32[]{:S(2)}) copy-start(bf16[128,1152]{1,0:T(8,128)(2,1)S(1)} %get-tuple-element.8.half) | copy-start | bytes 884740
  17.9 3.7 %copy-start.6 = (bf16[128,128]{1,0:T(8,128)(2,1)}, bf16[128,128]{1,0:T(8,128)(2,1)S(1)}, u32[]{:S(2)}) copy-start(bf16[128,128]{1,0:T(8,128)(2,1)S(1)} %get-tuple-element.11.member) | copy-start | bytes 98308
  17.9 3.6 %collective-permute-start = (bf16[128,1152]{1,0:T(8,128)(2,1)S(1)}, bf16[128,1152]{1,0:T(8,128)(2,1)S(1)}, u32[]{:S(2)}, u32[]{:S(2)}) collective-permute-start(bf16[128,1152]{1,0:T(8,128)(2,1)S(1)} %get-tuple-element.10), channel_id=1, source_target_pairs={{0,1},{1,0},{2,3},{3,2},{4,5},{5,4},{6,7},{7,6},{8,9},{9,8},{10,11... | collective-permute-start | bytes 884744 | tf_op jit(solution)/shard_map/ppermute | solution.py:169
  21.6 11.3 %collective-permute-start.1 = (bf16[128,1152]{1,0:T(8,128)(2,1)S(1)}, bf16[128,1152]{1,0:T(8,128)(2,1)S(1)}, u32[]{:S(2)}, u32[]{:S(2)}) collective-permute-start(bf16[128,1152]{1,0:T(8,128)(2,1)S(1)} %add_convert_fusion.own_sum), channel_id=1, source_target_pairs={{0,2},{2,0},{1,3},{3,1},{4,6},{6,4},{5,7},{7,5},{8,10},{10,8},{9,1... | collective-permute-start | bytes 884744 | tf_op jit(solution)/shard_map/ppermute | solution.py:171
  27.6 5.3 %copy-start.5 = (bf16[128,1152]{1,0:T(8,128)(2,1)S(1)}, bf16[128,1152]{1,0:T(8,128)(2,1)}, u32[]{:S(2)}) copy-start(bf16[128,1152]{1,0:T(8,128)(2,1)} %copy-done.4) | copy-start | bytes 884740
  32.9 1.8 %copy-start = (bf16[1152,1076]{1,0:T(8,128)(2,1)S(1)}, bf16[1152,1076]{1,0:T(8,128)(2,1)}, u32[]{:S(2)}) copy-start(bf16[1152,1076]{1,0:T(8,128)(2,1)} %copy.26.w1b) | copy-start | bytes 7437316
  34.7 1.7 %copy-start.1 = (bf16[1076,1152]{1,0:T(8,128)(2,1)S(1)}, bf16[1076,1152]{1,0:T(8,128)(2,1)}, u32[]{:S(2)}) copy-start(bf16[1076,1152]{1,0:T(8,128)(2,1)} %w2a.1) | copy-start | bytes 7437316
  36.4 0.8 copy-start.7
  37.1 12.6 %copy-start.12 = (bf16[2,1152]{1,0:T(2,128)(2,1)S(1)}, bf16[2,1152]{1,0:T(2,128)(2,1)}, u32[]{:S(2)}) copy-start(bf16[2,1152]{1,0:T(2,128)(2,1)} %param.17) | copy-start | bytes 13828
  41.8 26.4 %collective-permute-start.4 = (bf16[64,1280]{1,0:T(8,128)(2,1)}, bf16[64,1280]{1,0:T(8,128)(2,1)S(1)}, u32[]{:S(2)}, u32[]{:S(2)}) collective-permute-start(bf16[64,1280]{1,0:T(8,128)(2,1)} %get-tuple-element.12), channel_id=1, source_target_pairs={{0,0},{1,4},{2,8},{3,12},{4,1},{5,5},{6,9},{7,13},{8,2},{9,6},{10,... | collective-permute-start | bytes 491528 | tf_op jit(solution)/shard_map/ppermute | solution.py:39
  43.7 24.5 %collective-permute-start.5 = (bf16[64,1152]{1,0:T(8,128)(2,1)}, bf16[64,1152]{1,0:T(8,128)(2,1)S(1)}, u32[]{:S(2)}, u32[]{:S(2)}) collective-permute-start(bf16[64,1152]{1,0:T(8,128)(2,1)} %get-tuple-element.13), channel_id=1, source_target_pairs={{0,8},{1,12},{2,0},{3,4},{4,9},{5,13},{6,1},{7,5},{8,10},{9,14},{1... | collective-permute-start | bytes 442376 | tf_op jit(solution)/shard_map/ppermute | solution.py:39
  49.8 4.9 %collective-permute-start.7 = (bf16[2,1152]{1,0:T(2,128)(2,1)S(1)}, bf16[2,1152]{1,0:T(2,128)(2,1)S(1)}, u32[]{:S(2)}, u32[]{:S(2)}) collective-permute-start(bf16[2,1152]{1,0:T(2,128)(2,1)S(1)} %copy-done.12), channel_id=1, source_target_pairs={{0,0},{1,4},{2,8},{3,12},{4,1},{5,5},{6,9},{7,13},{8,2},{9,6},{10,... | collective-permute-start | bytes 13832 | tf_op jit(solution)/shard_map/ppermute | solution.py:39
  55.4 29.3 %all-to-all-start.1 = ((bf16[32,2,1152]{2,1,0:T(2,128)(2,1)}), bf16[32,2,1152]{2,1,0:T(2,128)(2,1)S(1)}, u32[]{:S(2)}, u32[]{:S(2)}) async-start(bf16[32,2,1152]{2,1,0:T(2,128)(2,1)} %broadcast_in_dim.2), calls=%async_computation.1 | async-start | bytes 294912 | tf_op jit(solution)/shard_map/all_to_all | solution.py:175
  68.2 20.4 %copy-start.11 = (bf16[64,1152]{1,0:T(8,128)(2,1)}, bf16[64,1152]{1,0:T(8,128)(2,1)S(1)}, u32[]{:S(2)}) copy-start(bf16[64,1152]{1,0:T(8,128)(2,1)S(1)} %collective-permute-done.5.second) | copy-start | bytes 442372
  68.2 20.4 %copy-start.10 = (bf16[64,1280]{1,0:T(8,128)(2,1)}, bf16[64,1280]{1,0:T(8,128)(2,1)S(1)}, u32[]{:S(2)}) copy-start(bf16[64,1280]{1,0:T(8,128)(2,1)S(1)} %collective-permute-done.4.first) | copy-start | bytes 491524
  84.7 39.4 %all-to-all-start = ((bf16[32,2,1152]{2,1,0:T(2,128)(2,1)}), bf16[32,2,1152]{2,1,0:T(2,128)(2,1)S(1)}, u32[]{:S(2)}, u32[]{:S(2)}) async-start(bf16[32,2,1152]{2,1,0:T(2,128)(2,1)} %reshape.20), calls=%async_computation | async-start | bytes 294912 | tf_op jit(solution)/shard_map/all_to_all | solution.py:188
  91.0 5.8 %collective-permute-start.6 = (f32[8,1152]{1,0:T(8,128)}, f32[8,1152]{1,0:T(8,128)S(1)}, u32[]{:S(2)}, u32[]{:S(2)}) collective-permute-start(f32[8,1152]{1,0:T(8,128)} %shard_map.115), channel_id=1, source_target_pairs={{0,0},{1,4},{2,8},{3,12},{4,1},{5,5},{6,9},{7,13},{8,2},{9,6},{10,... | collective-permute-start | bytes 110600 | tf_op jit(solution)/shard_map/ppermute | solution.py:39

commit v3 on v2

v3 whole, which is shorter than its diff:
```python
import functools
import math

import jax
import jax.numpy as jnp
from jax import lax
from jax.experimental import pallas as pl
from jax.experimental.pallas import tpu as pltpu
from jax.sharding import Mesh
from jax.sharding import PartitionSpec as P

HEAD_DIM = 72
N_YH, N_Z, N_X, N_YL, N_CORE = 2, 16, 4, 2, 2
DP = ("yh", "z", "x")
TP = ("yl", "core")
RING = ("yh", "z")
HIGH = lax.Precision.HIGHEST
F32, BF16, I32 = jnp.float32, jnp.bfloat16, jnp.int32
VMEM = pl.BlockSpec(memory_space=pltpu.VMEM)
HBM = pl.BlockSpec(memory_space=pltpu.HBM)
SMEM = pl.BlockSpec(memory_space=pltpu.SMEM)
CONTRACT_LAST = (((1,), (1,)), ((), ()))
CONTRACT_FIRST = (((0,), (0,)), ((), ()))
BIG = 28 * 2**20


def layer_norm(values):
    mean_val = jnp.mean(values, axis=-1, keepdims=True)
    centred = values - mean_val
    var_val = jnp.mean(centred * centred, axis=-1, keepdims=True)
    return centred * lax.rsqrt(var_val + 1e-06)


def swap_quarters(values, flip=0):
    pairs = [(x * N_X + t, (t ^ flip) * N_X + x) for x in range(N_X) for t in range(N_X)]
    return lax.ppermute(values, ("x",) + TP, pairs)


def attend_kernel(
    place, counts, slots, rows_hbm, w_qkv_hbm, w_out_hbm, keep, send, half, member, packed, part, rows, w_qkv, w_out, sems
):
    fetches = [
        pltpu.make_async_copy(source, target, sems.at[i])
        for i, (source, target) in enumerate(((rows_hbm, rows), (w_qkv_hbm, w_qkv), (w_out_hbm, w_out)))
    ]
    for fetch in fetches:
        fetch.start()
    n = rows.shape[0]
    core = place[0]
    slot = slots[...]
    peer = slot >> 1
    order = (peer & 1) * 128 + ((peer >> 1) & 1) * 64 + (peer >> 2) * 2 + (slot & 1)
    moved = jnp.where(lax.broadcasted_iota(I32, (n, n), 0) == order, 1.0, 0.0).astype(BF16)
    first, second = counts[0, 0], counts[0, 0] + counts[0, 1]

    def segment_of(position):
        return jnp.where(position >= first, 1.0, 0.0) + jnp.where(position >= second, 1.0, 0.0)

    seg_lanes = lax.dot_general(
        segment_of(lax.broadcasted_iota(I32, (8, n), 1)).astype(BF16), moved, CONTRACT_LAST, preferred_element_type=F32
    )
    seg_rows = jnp.dot(
        moved, segment_of(lax.broadcasted_iota(I32, (n, 128), 0)).astype(BF16), preferred_element_type=F32
    )
    same = seg_rows[:, :1] == seg_lanes[:1, :]
    fetches[0].wait()
    ordered = jnp.dot(moved, rows[...], preferred_element_type=F32)
    packed[...] = ordered.astype(BF16)
    normed = layer_norm(ordered).astype(BF16)
    fetches[1].wait()
    qkv = lax.dot_general(normed, w_qkv[...], CONTRACT_LAST, preferred_element_type=F32)
    heads = w_out.shape[0] // HEAD_DIM
    width = heads * HEAD_DIM
    outs = []
    for h in range(heads):
        q, k, v = (qkv[:, i * width + h * HEAD_DIM : i * width + (h + 1) * HEAD_DIM].astype(BF16) for i in range(3))
        scores = lax.dot_general(q, k, CONTRACT_LAST, preferred_element_type=F32) * (1.0 / math.sqrt(HEAD_DIM))
        scores = jnp.where(same, scores, -1e30)
        raised = jnp.exp(scores - jnp.max(scores, axis=-1, keepdims=True))
        total = jnp.sum(raised, axis=-1, keepdims=True)
        outs.append(jnp.dot(raised.astype(BF16), v, preferred_element_type=F32) / total)
    attended = jnp.concatenate(outs, axis=1).astype(BF16)
    fetches[2].wait()
    part[...] = jnp.dot(attended, w_out[...], preferred_element_type=F32).astype(BF16)
    mine, other = pl.multiple_of(core * 128, 128), pl.multiple_of(128 - core * 128, 128)
    keep[...] = part[pl.ds(mine, 128), :]
    send[...] = part[pl.ds(other, 128), :]
    half[...] = packed[pl.ds(mine, 128), :]
    images = lax.broadcasted_iota(I32, (n, 128), 1).astype(F32)
    packed[:, :128] = jnp.where(seg_rows == images, 1.0, 0.0).astype(BF16)
    member[...] = packed[pl.ds(mine, 128), :128]


def mlp_kernel(
    place, half, own_sum, far_sum, member, text, w1a, w1b, w2a, w2b, first_out, second_out, share_out, resid, part
):
    base = half[...].astype(F32) + own_sum[...].astype(F32) + far_sum[...].astype(F32)
    resid[...] = base.astype(BF16)
    normed = layer_norm(resid[...].astype(F32)).astype(BF16)
    total = None
    for w1, w2 in ((w1a, w2a), (w1b, w2b)):
        hidden = lax.dot_general(normed, w1[...], CONTRACT_LAST, preferred_element_type=F32)
        hidden = jax.nn.gelu(hidden, approximate=True).astype(BF16)
        piece = jnp.dot(hidden, w2[...], preferred_element_type=F32)
        total = piece if total is None else total + piece
    part[...] = total
    share_out[...] = total.astype(BF16)
    yl = place[1]
    mine, other = pl.multiple_of(yl * 64, 64), pl.multiple_of(64 - yl * 64, 64)
    width = half.shape[1]
    first_out[:64, :width] = (part[pl.ds(mine, 64), :] + resid[pl.ds(mine, 64), :].astype(F32)).astype(BF16)
    first_out[64:, :width] = jnp.concatenate([text[...].astype(F32), jnp.zeros((14, width), F32)], axis=0).astype(BF16)
    second_out[...] = part[pl.ds(other, 64), :].astype(BF16)


def pool_kernel(resid, own_share, far_share, member, pooled):
    layer = resid[...].astype(F32) + own_share[...].astype(F32) + far_share[...].astype(F32)
    normed = layer_norm(layer.astype(BF16).astype(F32))
    high = normed.astype(BF16)
    low = (normed - high.astype(F32)).astype(BF16)
    full = lax.dot_general(member[...], high, CONTRACT_FIRST, preferred_element_type=F32)
    full += lax.dot_general(member[...], low, CONTRACT_FIRST, preferred_element_type=F32)
    pooled[...] = full[:8]


def two_parts(values):
    high = values.astype(BF16).astype(F32)
    return jnp.concatenate([high, values - high], axis=0).astype(BF16)


def loss_kernel(where, counts, multiplier, shift, pooled_sum, texts, grad_out):
    row8 = lax.broadcasted_iota(I32, (8, 1), 0)
    count = jnp.where(row8 == 0, counts[0, 0], counts[0, 1]).astype(F32)
    pooled = pooled_sum[...] / count
    norm_img = jnp.sqrt(jnp.sum(pooled * pooled, axis=1, keepdims=True) + 1e-06)
    unit = pooled / norm_img
    text = texts[...]
    square = text.astype(F32) * text.astype(F32)
    high = square.astype(BF16)
    low = (square - high.astype(F32)).astype(BF16)
    ones = jnp.ones((16, text.shape[1]), BF16)
    total = lax.dot_general(ones, high, CONTRACT_LAST, preferred_element_type=F32)
    total += lax.dot_general(ones, low, CONTRACT_LAST, preferred_element_type=F32)
    per_norm = lax.rsqrt(total[:8] + 1e-06)
    cosine = lax.dot_general(two_parts(unit), text, CONTRACT_LAST, preferred_element_type=F32)
    logits = multiplier[0] * (cosine[:8] + cosine[8:]) * per_norm + shift[0]
    column = lax.broadcasted_iota(I32, logits.shape, 1)
    text_index = (column >> 1) * (2 * N_X) + (column & 1) + where[1]
    image_index = lax.broadcasted_iota(I32, logits.shape, 0) + where[0]
    slope = 1.0 / (1.0 + jnp.exp(-logits)) - jnp.where(text_index == image_index, 1.0, 0.0)
    grad = jnp.dot(two_parts(slope * per_norm), text, preferred_element_type=F32)
    grad = multiplier[0] * (grad[:8] + grad[8:])
    grad_out[...] = ((grad - unit * jnp.sum(unit * grad, axis=1, keepdims=True)) / norm_img)[:2]


def call(kernel, specs, outs, scratch=(), limit=None, flops=10**7, nbytes=10**6):
    many = isinstance(outs, list)
    return pl.pallas_call(
        kernel,
        in_specs=specs,
        out_specs=[VMEM] * len(outs) if many else VMEM,
        out_shape=outs,
        scratch_shapes=list(scratch),
        compiler_params=pltpu.CompilerParams(vmem_limit_bytes=limit),
        cost_estimate=pl.CostEstimate(flops=flops, bytes_accessed=nbytes, transcendentals=0),
    )


def per_device(rows_in, patch_counts, row_slots, w_qkv, w_out, w_fc1, w_fc2, text_embeds, multiplier, shift):
    row_count, width = rows_in.shape
    half_rows, quarter, ring = row_count // 2, row_count // 4, N_YH * N_Z
    shape = jax.ShapeDtypeStruct
    place = jnp.stack([lax.axis_index("core"), lax.axis_index("yl")]).astype(I32)
    pair = [(0, 1), (1, 0)]

    keep, send, half, member = call(
        attend_kernel,
        [SMEM, SMEM, VMEM, HBM, HBM, HBM],
        [
            shape((half_rows, width), BF16),
            shape((half_rows, width), BF16),
            shape((half_rows, width), BF16),
            shape((half_rows, 128), BF16),
        ],
        [
            pltpu.VMEM((row_count, width), BF16),
            pltpu.VMEM((row_count, width), BF16),
            pltpu.VMEM((row_count, width), BF16),
            pltpu.VMEM((w_qkv.shape[1], width), BF16),
            pltpu.VMEM(w_out.shape, BF16),
            pltpu.SemaphoreType.DMA((3,)),
        ],
        BIG,
        2 * 10**9,
        8 * 10**6,
    )(place, patch_counts, row_slots, rows_in, w_qkv.T, w_out)

    got = lax.ppermute(send, "core", pair)
    own_sum = (keep.astype(F32) + got.astype(F32)).astype(BF16)
    own_sum, far_w1, far_w2 = lax.optimization_barrier((own_sum, w_fc1.T, w_fc2))
    far_sum = lax.ppermute(own_sum, "yl", pair)
    far_w1 = lax.ppermute(far_w1, "core", pair)
    far_w2 = lax.ppermute(far_w2, "core", pair)

    first, second, share, resid = call(
        mlp_kernel,
        [SMEM] + [VMEM] * 9,
        [
            shape((quarter + 16, width), BF16),
            shape((quarter, width), BF16),
            shape((half_rows, width), BF16),
            shape((half_rows, width), BF16),
        ],
        [pltpu.VMEM((half_rows, width), F32)],
        BIG,
        4 * 10**9,
        16 * 10**6,
    )(place, half, own_sum, far_sum, member, text_embeds, w_fc1.T, far_w1, w_fc2, far_w2)

    first = swap_quarters(first)
    second = swap_quarters(second, 2)
    far_share = lax.ppermute(share, "yl", pair)
    layer = (first[:quarter].astype(F32) + second.astype(F32)).astype(BF16).reshape(ring, 2, width)
    text = jnp.broadcast_to(first[quarter : quarter + 2][None], layer.shape)
    arrived = lax.all_to_all(jnp.concatenate([layer, text], axis=1), RING, 0, 0, tiled=True)

    pooled = call(pool_kernel, [VMEM] * 4, shape((8, width), F32))(resid, share, far_share, member)
    pooled = lax.psum(pooled, "core")
    where = jnp.stack([lax.axis_index(DP) * 2, lax.axis_index(TP) * 2]).astype(I32)
    grad = call(loss_kernel, [SMEM] * 4 + [VMEM] * 2, shape((2, width), F32))(
        where, patch_counts, multiplier, shift, pooled, arrived[:, 2:].reshape(quarter, width)
    )

    high = grad.astype(BF16)
    low = (grad - high.astype(F32)).astype(BF16)
    bundle = jnp.concatenate([arrived[:, :2], high[None], low[None]], axis=0)
    bundle = lax.all_gather(bundle, TP, axis=1, tiled=False)
    rows_out = bundle[:ring].reshape(row_count, width)
    return rows_out, jnp.sum(bundle[ring:].astype(F32), axis=(0, 1))


def solution(mesh):
    fine = Mesh(mesh.devices.reshape(N_YH, N_Z, N_X, N_YL, N_CORE), DP + TP)
    placed = (
        P(DP, None),
        P(DP, None),
        P(DP, None),
        P(None, TP),
        P(TP, None),
        P(None, TP),
        P(TP, None),
        P(DP, None),
        P(),
        P(),
    )
    return jax.shard_map(per_device, mesh=fine, in_specs=placed, out_specs=(P(DP, None), P(DP, None)), check_vma=False)
```

time: 135 us -> 107 us (0.79)
  blocking collectives: 32.3 us -> 19.3 us
  local copies, waits for them, and re-layouts: 20.4 us -> 8.63 us
  other arithmetic: 0.2 us -> 3.5 us
  starting transfers between devices: 44.7 us -> 42.1 us
  waiting for transfers between devices: 20.6 us -> 18.5 us
    psum x2 -> x1, blocking collectives: 24 us -> 5.62 us  [per_device(): pooled = lax.psum(pooled, 'core')]
    all_to_all x2 -> x1, waiting for transfers between devices: 15.7 us -> 0.01 us  [per_device(): lax.all_to_all(jnp.concatenate([layer, text], axis=1), RING, 0, 0, tiled=...]
    ppermute x1, waiting for transfers between devices: 0.01 us -> 8.19 us  [per_device(): far_sum = lax.ppermute(own_sum, 'yl', pair)]
    ppermute x2 -> x3, waiting for transfers between devices: 0.01 us -> 6.58 us  [the longest x1 6.57 us: per_device(): far_share = lax.ppermute(share, 'yl', pair)]
    ppermute x1, starting transfers between devices: 2.4 us -> 8.79 us  [per_device(): got = lax.ppermute(send, 'core', pair)]
    ppermute x4 -> x2, starting transfers between devices: 12.9 us -> 6.81 us  [swap_quarters(): return lax.ppermute(values, ('x',) + TP, pairs)]
    all_gather x1, blocking collectives: 8.33 us -> 13.7 us  [per_device(): bundle = lax.all_gather(bundle, TP, axis=1, tiled=False)]
    ppermute x1 -> x0, local copies, waits for them, and re-layouts: 5.24 us -> none  [per_device(): w1b = lax.ppermute(w_fc1, 'core', pair)]
  transfers between devices with their start and end apart: 10 -> 8, of which waited for: 4 -> 4; matrix products, arithmetic and copies ran while one was open for 11% -> 1% of each run, Pallas kernels for 6% -> 2%
where the time goes in v3:
time: 107 us
  starting transfers between devices  42.1 us (39%)
  blocking collectives  19.3 us (18%)
  waiting for transfers between devices  18.5 us (17%)
  Pallas kernels  12.3 us (11%)
  local copies, waits for them, and re-layouts  8.63 us (8%)
  other arithmetic  3.5 us (3%)
  between operations  2.14 us (2%)
    all_to_all x1, starting transfers between devices, per_device(): lax.all_to_all(jnp.concatenate([layer, text], axis=1), RING, 0, 0, tiled=...  14.7 us
    all_gather x1, blocking collectives, per_device(): bundle = lax.all_gather(bundle, TP, axis=1, tiled=False)  13.7 us
    ppermute x1, starting transfers between devices, per_device(): got = lax.ppermute(send, 'core', pair)  8.79 us
    ppermute x1, waiting for transfers between devices, per_device(): far_sum = lax.ppermute(own_sum, 'yl', pair)  8.19 us
    unnamed x25, local copies, waits for them, and re-layouts  7.47 us
    ppermute x2, starting transfers between devices, swap_quarters(): return lax.ppermute(values, ('x',) + TP, pairs)  6.81 us
    ppermute x1, waiting for transfers between devices, per_device(): far_share = lax.ppermute(share, 'yl', pair)  6.57 us
    psum x1, blocking collectives, per_device(): pooled = lax.psum(pooled, 'core')  5.62 us
  transfers between devices with their start and end apart: 8, of which 4 were waited for; matrix products, arithmetic and copies ran while one was open for 1% of the time, Pallas kernels for 2%

profile of v3, /device:TPU:1, one launch (start us, length us, event | category | flops | bytes accessed | tf_op | source)
XLA Modules:
  0.0 106.5 jit_solution(1608140192048060534)
XLA Ops:
  0.6 0.1 pad_add_fusion.place
  0.7 0.7 copy-done.3
  1.4 1.6 %copy-done.6 = bf16[1152,864]{0,1:T(8,128)(2,1)S(1)} copy-done((bf16[1152,864]{0,1:T(8,128)(2,1)S(1)}, bf16[1152,864]{0,1:T(8,128)(2,1)}, u32[]{:S(2)}) %copy-start.6) | copy-done | bytes 1990680
  2.9 1.1 %copy-done.7 = bf16[288,1152]{1,0:T(8,128)(2,1)S(1)} copy-done((bf16[288,1152]{1,0:T(8,128)(2,1)S(1)}, bf16[288,1152]{1,0:T(8,128)(2,1)}, u32[]{:S(2)}) %copy-start.7) | copy-done | bytes 663576
  4.0 1.1 copy-done.8
  5.1 0.7 copy-done.10
  5.8 4.5 %shard_map.113 = (bf16[128,1152]{1,0:T(8,128)(2,1)S(1)}, bf16[128,1152]{1,0:T(8,128)(2,1)S(1)}, bf16[128,1152]{1,0:T(8,128)(2,1)S(1)}, bf16[128,128]{1,0:T(8,128)(2,1)S(1)}) custom-call(s32[2]{0:T(128)S(1)} %pad_add_fusion.place, s32[1,2]{1,0:T(1,128)S(1)} %copy-done.3, s32[1,256]{1,0:T(1,128)S(1)} %copy-done.10, bf16[256,1152]{1,0:T(8,128)(2,1)S(1)} %copy-done.8, ...), custom_call_target="tpu_custom_call" | custom-call | flops 2000000000 | bytes 8000000 | tf_op jit(solution)/shard_map/pallas_call | solution.py:176
  10.2 0.0 copy-start.2
  10.2 8.8 %collective-permute-start = (bf16[128,1152]{1,0:T(8,128)(2,1)S(1)}, bf16[128,1152]{1,0:T(8,128)(2,1)S(1)}, u32[]{:S(2)}, u32[]{:S(2)}) collective-permute-start(bf16[128,1152]{1,0:T(8,128)(2,1)S(1)} %get-tuple-element.15), channel_id=1, source_target_pairs={{0,1},{1,0},{2,3},{3,2},{4,5},{5,4},{6,7},{7,6},{8,9},{9,8},{10,11... | collective-permute-start | bytes 884744 | tf_op jit(solution)/shard_map/ppermute | solution.py:198
  19.0 1.2 %collective-permute-done = bf16[128,1152]{1,0:T(8,128)(2,1)S(1)} collective-permute-done((bf16[128,1152]{1,0:T(8,128)(2,1)S(1)}, bf16[128,1152]{1,0:T(8,128)(2,1)S(1)}, u32[]{:S(2)}, u32[]{:S(2)}) %collective-permute-start) | collective-permute-done | bytes 294944 | tf_op jit(solution)/shard_map/ppermute | solution.py:198
  20.2 0.1 add_convert_fusion.own_sum
  20.3 0.0 copy-done.4
  20.3 2.3 %collective-permute-start.2 = (bf16[1076,1152]{1,0:T(8,128)(2,1)S(1)}, bf16[1076,1152]{1,0:T(8,128)(2,1)S(1)}, u32[]{:S(2)}, u32[]{:S(2)}) collective-permute-start(bf16[1076,1152]{1,0:T(8,128)(2,1)S(1)} %bitcast.13), channel_id=1, source_target_pairs={{0,1},{1,0},{2,3},{3,2},{4,5},{5,4},{6,7},{7,6},{8,9},{9,8},{10,11... | collective-permute-start | bytes 7437320 | tf_op jit(solution)/shard_map/ppermute | solution.py:202
  22.6 0.0 copy-done.5
  22.6 2.0 %collective-permute-start.3 = (bf16[1076,1152]{1,0:T(8,128)(2,1)S(1)}, bf16[1076,1152]{1,0:T(8,128)(2,1)S(1)}, u32[]{:S(2)}, u32[]{:S(2)}) collective-permute-start(bf16[1076,1152]{1,0:T(8,128)(2,1)S(1)} %copy-done.5), channel_id=1, source_target_pairs={{0,1},{1,0},{2,3},{3,2},{4,5},{5,4},{6,7},{7,6},{8,9},{9,8},{10,11... | collective-permute-start | bytes 7437320 | tf_op jit(solution)/shard_map/ppermute | solution.py:203
  24.7 1.9 %collective-permute-start.1 = (bf16[128,1152]{1,0:T(8,128)(2,1)S(1)}, bf16[128,1152]{1,0:T(8,128)(2,1)S(1)}, u32[]{:S(2)}, u32[]{:S(2)}) collective-permute-start(bf16[128,1152]{1,0:T(8,128)(2,1)S(1)} %add_convert_fusion.own_sum), channel_id=1, source_target_pairs={{0,2},{2,0},{1,3},{3,1},{4,6},{6,4},{5,7},{7,5},{8,10},{10,8},{9,1... | collective-permute-start | bytes 884744 | tf_op jit(solution)/shard_map/ppermute | solution.py:201
  26.6 8.2 %collective-permute-done.1.far_sum = bf16[128,1152]{1,0:T(8,128)(2,1)S(1)} collective-permute-done((bf16[128,1152]{1,0:T(8,128)(2,1)S(1)}, bf16[128,1152]{1,0:T(8,128)(2,1)S(1)}, u32[]{:S(2)}, u32[]{:S(2)}) %collective-permute-start.1) | collective-permute-done | bytes 294944 | tf_op jit(solution)/shard_map/ppermute | solution.py:201
  34.8 0.0 collective-permute-done.2.w1b
  34.8 0.0 collective-permute-done.3.w2b
  34.8 0.0 copy-done.9
  34.8 3.4 %shard_map.114 = (bf16[80,1152]{1,0:T(8,128)(2,1)S(1)}, bf16[64,1152]{1,0:T(8,128)(2,1)S(1)}, bf16[128,1152]{1,0:T(8,128)(2,1)S(1)}, bf16[128,1152]{1,0:T(8,128)(2,1)S(1)}) custom-call(s32[2]{0:T(128)S(1)} %pad_add_fusion.place, bf16[128,1152]{1,0:T(8,128)(2,1)S(1)} %get-tuple-element.13.half, bf16[128,1152]{1,0:T(8,128)(2,1)S(1)} %add_convert_fusion.own_sum, ...), custom_call_target="tpu_custom_call" | custom-call | flops 4000000000 | bytes 16000000 | tf_op jit(solution)/shard_map/pallas_call | solution.py:205
  38.2 0.0 copy-done.2
  38.2 0.0 copy-start.1
  38.2 0.7 copy-done.1
  38.9 1.9 %collective-permute-start.4 = (bf16[80,1152]{1,0:T(8,128)(2,1)S(1)}, bf16[80,1152]{1,0:T(8,128)(2,1)S(1)}, u32[]{:S(2)}, u32[]{:S(2)}) collective-permute-start(bf16[80,1152]{1,0:T(8,128)(2,1)S(1)} %get-tuple-element.20), channel_id=1, source_target_pairs={{0,0},{1,4},{2,8},{3,12},{4,1},{5,5},{6,9},{7,13},{8,2},{9,6},{10,... | collective-permute-start | bytes 552968 | tf_op jit(solution)/shard_map/ppermute | solution.py:36
  40.8 4.9 %collective-permute-start.5 = (bf16[64,1152]{1,0:T(8,128)(2,1)S(1)}, bf16[64,1152]{1,0:T(8,128)(2,1)S(1)}, u32[]{:S(2)}, u32[]{:S(2)}) collective-permute-start(bf16[64,1152]{1,0:T(8,128)(2,1)S(1)} %get-tuple-element.21), channel_id=1, source_target_pairs={{0,8},{1,12},{2,0},{3,4},{4,9},{5,13},{6,1},{7,5},{8,10},{9,14},{1... | collective-permute-start | bytes 442376 | tf_op jit(solution)/shard_map/ppermute | solution.py:36
  45.7 2.6 %collective-permute-done.5 = bf16[64,1152]{1,0:T(8,128)(2,1)S(1)} collective-permute-done((bf16[64,1152]{1,0:T(8,128)(2,1)S(1)}, bf16[64,1152]{1,0:T(8,128)(2,1)S(1)}, u32[]{:S(2)}, u32[]{:S(2)}) %collective-permute-start.5) | collective-permute-done | bytes 147488 | tf_op jit(solution)/shard_map/ppermute | solution.py:36
  48.3 0.0 collective-permute-done.4
  48.4 0.1 reshape.14
  48.4 0.1 broadcast_in_dim.12
  48.5 1.0 pad_maximum_fusion
  49.5 14.7 %all-to-all-start = ((bf16[32,4,1152]{2,1,0:T(4,128)(2,1)}), bf16[32,4,1152]{2,1,0:T(4,128)(2,1)S(1)}, u32[]{:S(2)}, u32[]{:S(2)}) async-start(bf16[32,4,1152]{2,1,0:T(4,128)(2,1)} %pad_maximum_fusion), calls=%async_computation | async-start | bytes 589824 | tf_op jit(solution)/shard_map/all_to_all | solution.py:225
  64.3 5.5 %collective-permute-start.6 = (bf16[128,1152]{1,0:T(8,128)(2,1)S(1)}, bf16[128,1152]{1,0:T(8,128)(2,1)S(1)}, u32[]{:S(2)}, u32[]{:S(2)}) collective-permute-start(bf16[128,1152]{1,0:T(8,128)(2,1)S(1)} %get-tuple-element.23.own_share), channel_id=1, source_target_pairs={{0,2},{2,0},{1,3},{3,1},{4,6},{6,4},{5,7},{7,5},{8,10},{10,8},{9,1... | collective-permute-start | bytes 884744 | tf_op jit(solution)/shard_map/ppermute | solution.py:222
  71.2 0.6 pad_add_fusion.1.where
  71.7 6.6 %collective-permute-done.6.far_share = bf16[128,1152]{1,0:T(8,128)(2,1)S(1)} collective-permute-done((bf16[128,1152]{1,0:T(8,128)(2,1)S(1)}, bf16[128,1152]{1,0:T(8,128)(2,1)S(1)}, u32[]{:S(2)}, u32[]{:S(2)}) %collective-permute-start.6) | collective-permute-done | bytes 294944 | tf_op jit(solution)/shard_map/ppermute | solution.py:222
  78.3 0.7 copy-done.11
  79.0 2.4 %shard_map.115 = f32[8,1152]{1,0:T(8,128)} custom-call(bf16[128,1152]{1,0:T(8,128)(2,1)} %copy-done.1, bf16[128,1152]{1,0:T(8,128)(2,1)} %copy-done, bf16[128,1152]{1,0:T(8,128)(2,1)} %copy-done.11, bf16[128,128]{1,0:T(8,128)(2,1)} %copy-done.2), custom_call_target="tpu_custom_call" | custom-call | flops 10000000 | bytes 1000000 | tf_op jit(solution)/shard_map/pallas_call | solution.py:227
  81.4 5.6 %psum.7.pooled_sum = f32[8,1152]{1,0:T(8,128)} all-reduce(f32[8,1152]{1,0:T(8,128)} %shard_map.115), channel_id=1, replica_groups=mesh['yh'=2,'z'=16,'x'=4,'yl'=2,'core'=2] {'core'}, use_global_device_ids=true, to_apply=%region_0.0 | all-reduce | flops 9216 | bytes 73728 | tf_op jit(solution)/shard_map/psum | solution.py:228
  87.0 0.0 all-to-all-done
  87.0 0.2 fusion.1
  87.2 0.7 reshape.15.texts
  87.9 2.1 %shard_map.116 = f32[2,1152]{1,0:T(2,128)} custom-call(s32[2]{0:T(128)} %pad_add_fusion.1.where, s32[1,2]{1,0:T(1,128)} %counts.3, f32[1]{0:T(128)S(6)} %copy.32.multiplier, f32[1]{0:T(128)S(6)} %copy.33.shift, f32[8,1152]{1,0:T(8,128)} %psum.7.pooled_sum, bf16[64,1152]{1,0:T(8,128)(2,1)} %reshape.15.texts), custom_call_target="tpu_custom_call" | custom-call | flops 10000000 | bytes 1000000 | tf_op jit(solution)/shard_map/pallas_call | solution.py:230
  90.0 0.8 convert_bitcast_fusion
  90.8 0.2 pad_maximum_fusion.1
  91.1 13.7 %all-gather = bf16[34,8,1152]{2,0,1:T(8,128)(2,1)S(1)} all-gather(bf16[34,2,1152]{2,0,1:T(8,128)(2,1)S(1)} %copy.25), channel_id=2, replica_groups=mesh['yh'=2,'z'=16,'x'=4,'yl'=2,'core'=2] {'yl','core'}, dimensions={1}, use_global_device_ids=true | all-gather | bytes 783360 | tf_op jit(solution)/shard_map/all_gather | solution.py:237
  104.7 0.1 convert_reduce_fusion
  104.9 1.0 copy.31
  105.9 0.6 reduce_sum.9
  (16 shorter events, 0.2 us)
Async XLA Ops:
  0.7 0.7 copy-start.3
  1.4 1.6 %copy-start.6 = (bf16[1152,864]{0,1:T(8,128)(2,1)S(1)}, bf16[1152,864]{0,1:T(8,128)(2,1)}, u32[]{:S(2)}) copy-start(bf16[1152,864]{0,1:T(8,128)(2,1)} %param.13) | copy-start | bytes 5971972
  2.9 1.1 %copy-start.7 = (bf16[288,1152]{1,0:T(8,128)(2,1)S(1)}, bf16[288,1152]{1,0:T(8,128)(2,1)}, u32[]{:S(2)}) copy-start(bf16[288,1152]{1,0:T(8,128)(2,1)} %w_out_hbm.1) | copy-start | bytes 1990660
  4.0 1.1 copy-start.8
  5.1 0.7 copy-start.10
  5.8 14.5 %copy-start.4 = (bf16[1152,1076]{0,1:T(8,128)(2,1)S(1)}, bf16[1152,1076]{0,1:T(8,128)(2,1)}, u32[]{:S(2)}) copy-start(bf16[1152,1076]{0,1:T(8,128)(2,1)} %param.15) | copy-start | bytes 7437316
  5.8 16.8 %copy-start.5 = (bf16[1076,1152]{1,0:T(8,128)(2,1)S(1)}, bf16[1076,1152]{1,0:T(8,128)(2,1)}, u32[]{:S(2)}) copy-start(bf16[1076,1152]{1,0:T(8,128)(2,1)} %w2a.1) | copy-start | bytes 7437316
  5.8 29.0 %copy-start.9 = (bf16[2,1152]{1,0:T(2,128)(2,1)S(1)}, bf16[2,1152]{1,0:T(2,128)(2,1)}, u32[]{:S(2)}) copy-start(bf16[2,1152]{1,0:T(2,128)(2,1)} %text.1) | copy-start | bytes 13828
  10.2 28.0 %copy-start.2 = (bf16[128,128]{1,0:T(8,128)(2,1)}, bf16[128,128]{1,0:T(8,128)(2,1)S(1)}, u32[]{:S(2)}) copy-start(bf16[128,128]{1,0:T(8,128)(2,1)S(1)} %get-tuple-element.17.member) | copy-start | bytes 98308
  10.2 10.0 %collective-permute-start = (bf16[128,1152]{1,0:T(8,128)(2,1)S(1)}, bf16[128,1152]{1,0:T(8,128)(2,1)S(1)}, u32[]{:S(2)}, u32[]{:S(2)}) collective-permute-start(bf16[128,1152]{1,0:T(8,128)(2,1)S(1)} %get-tuple-element.15), channel_id=1, source_target_pairs={{0,1},{1,0},{2,3},{3,2},{4,5},{5,4},{6,7},{7,6},{8,9},{9,8},{10,11... | collective-permute-start | bytes 884744 | tf_op jit(solution)/shard_map/ppermute | solution.py:198
  20.3 14.5 %collective-permute-start.2 = (bf16[1076,1152]{1,0:T(8,128)(2,1)S(1)}, bf16[1076,1152]{1,0:T(8,128)(2,1)S(1)}, u32[]{:S(2)}, u32[]{:S(2)}) collective-permute-start(bf16[1076,1152]{1,0:T(8,128)(2,1)S(1)} %bitcast.13), channel_id=1, source_target_pairs={{0,1},{1,0},{2,3},{3,2},{4,5},{5,4},{6,7},{7,6},{8,9},{9,8},{10,11... | collective-permute-start | bytes 7437320 | tf_op jit(solution)/shard_map/ppermute | solution.py:202
  22.6 12.2 %collective-permute-start.3 = (bf16[1076,1152]{1,0:T(8,128)(2,1)S(1)}, bf16[1076,1152]{1,0:T(8,128)(2,1)S(1)}, u32[]{:S(2)}, u32[]{:S(2)}) collective-permute-start(bf16[1076,1152]{1,0:T(8,128)(2,1)S(1)} %copy-done.5), channel_id=1, source_target_pairs={{0,1},{1,0},{2,3},{3,2},{4,5},{5,4},{6,7},{7,6},{8,9},{9,8},{10,11... | collective-permute-start | bytes 7437320 | tf_op jit(solution)/shard_map/ppermute | solution.py:203
  24.7 10.1 %collective-permute-start.1 = (bf16[128,1152]{1,0:T(8,128)(2,1)S(1)}, bf16[128,1152]{1,0:T(8,128)(2,1)S(1)}, u32[]{:S(2)}, u32[]{:S(2)}) collective-permute-start(bf16[128,1152]{1,0:T(8,128)(2,1)S(1)} %add_convert_fusion.own_sum), channel_id=1, source_target_pairs={{0,2},{2,0},{1,3},{3,1},{4,6},{6,4},{5,7},{7,5},{8,10},{10,8},{9,1... | collective-permute-start | bytes 884744 | tf_op jit(solution)/shard_map/ppermute | solution.py:201
  38.2 0.7 copy-start.1
  38.9 39.4 %copy-start = (bf16[128,1152]{1,0:T(8,128)(2,1)}, bf16[128,1152]{1,0:T(8,128)(2,1)S(1)}, u32[]{:S(2)}) copy-start(bf16[128,1152]{1,0:T(8,128)(2,1)S(1)} %get-tuple-element.23.own_share) | copy-start | bytes 884740
  38.9 9.4 %collective-permute-start.4 = (bf16[80,1152]{1,0:T(8,128)(2,1)S(1)}, bf16[80,1152]{1,0:T(8,128)(2,1)S(1)}, u32[]{:S(2)}, u32[]{:S(2)}) collective-permute-start(bf16[80,1152]{1,0:T(8,128)(2,1)S(1)} %get-tuple-element.20), channel_id=1, source_target_pairs={{0,0},{1,4},{2,8},{3,12},{4,1},{5,5},{6,9},{7,13},{8,2},{9,6},{10,... | collective-permute-start | bytes 552968 | tf_op jit(solution)/shard_map/ppermute | solution.py:36
  40.8 7.5 %collective-permute-start.5 = (bf16[64,1152]{1,0:T(8,128)(2,1)S(1)}, bf16[64,1152]{1,0:T(8,128)(2,1)S(1)}, u32[]{:S(2)}, u32[]{:S(2)}) collective-permute-start(bf16[64,1152]{1,0:T(8,128)(2,1)S(1)} %get-tuple-element.21), channel_id=1, source_target_pairs={{0,8},{1,12},{2,0},{3,4},{4,9},{5,13},{6,1},{7,5},{8,10},{9,14},{1... | collective-permute-start | bytes 442376 | tf_op jit(solution)/shard_map/ppermute | solution.py:36
  49.5 37.5 %all-to-all-start = ((bf16[32,4,1152]{2,1,0:T(4,128)(2,1)}), bf16[32,4,1152]{2,1,0:T(4,128)(2,1)S(1)}, u32[]{:S(2)}, u32[]{:S(2)}) async-start(bf16[32,4,1152]{2,1,0:T(4,128)(2,1)} %pad_maximum_fusion), calls=%async_computation | async-start | bytes 589824 | tf_op jit(solution)/shard_map/all_to_all | solution.py:225
  64.3 14.0 %collective-permute-start.6 = (bf16[128,1152]{1,0:T(8,128)(2,1)S(1)}, bf16[128,1152]{1,0:T(8,128)(2,1)S(1)}, u32[]{:S(2)}, u32[]{:S(2)}) collective-permute-start(bf16[128,1152]{1,0:T(8,128)(2,1)S(1)} %get-tuple-element.23.own_share), channel_id=1, source_target_pairs={{0,2},{2,0},{1,3},{3,1},{4,6},{6,4},{5,7},{7,5},{8,10},{10,8},{9,1... | collective-permute-start | bytes 884744 | tf_op jit(solution)/shard_map/ppermute | solution.py:222
  78.3 0.7 copy-start.11

commit v4 on v3

--- a/solution.py
+++ b/solution.py
@@ -22,6 +22,12 @@
 CONTRACT_LAST = (((1,), (1,)), ((), ()))
 CONTRACT_FIRST = (((0,), (0,)), ((), ()))
 BIG = 28 * 2**20
+SMALL = 12 * 2**20
+ATTEND_LIMIT = 61 * 2**20
+NEAR_LIMIT = 40 * 2**20
+NEAR_FLOPS = 50 * 10**9
+ADD_FLOPS = 50 * 10**9
+POOL_FLOPS = 50 * 10**9
 
 
 def layer_norm(values):
@@ -37,21 +43,20 @@
 
 
 def attend_kernel(
-    place, counts, slots, rows_hbm, w_qkv_hbm, w_out_hbm, keep, send, half, member, packed, part, rows, w_qkv, w_out, sems
+    counts, slots, rows_hbm, w_qkv_hbm, w_out_hbm, keep, send, half, member, packed, part, rows, w_qkv, w_out, sems
 ):
-    fetches = [
-        pltpu.make_async_copy(source, target, sems.at[i])
-        for i, (source, target) in enumerate(((rows_hbm, rows), (w_qkv_hbm, w_qkv), (w_out_hbm, w_out)))
-    ]
+    n, width = rows.shape[0], w_out.shape[0]
+    thirds = [pl.ds(i * width, width) for i in range(3)]
+    pieces = [(rows_hbm, rows)] + [(w_qkv_hbm.at[third], w_qkv.at[third]) for third in thirds] + [(w_out_hbm, w_out)]
+    fetches = [pltpu.make_async_copy(source, target, sems.at[i]) for i, (source, target) in enumerate(pieces)]
     for fetch in fetches:
         fetch.start()
-    n = rows.shape[0]
-    core = place[0]
+    core = lax.axis_index("core")
     slot = slots[...]
     peer = slot >> 1
     order = (peer & 1) * 128 + ((peer >> 1) & 1) * 64 + (peer >> 2) * 2 + (slot & 1)
     moved = jnp.where(lax.broadcasted_iota(I32, (n, n), 0) == order, 1.0, 0.0).astype(BF16)
-    first, second = counts[0, 0], counts[0, 0] + counts[0, 1]
+    first, second = counts[:, 0:1], counts[:, 0:1] + counts[:, 1:2]
 
     def segment_of(position):
         return jnp.where(position >= first, 1.0, 0.0) + jnp.where(position >= second, 1.0, 0.0)
@@ -67,20 +72,20 @@
     ordered = jnp.dot(moved, rows[...], preferred_element_type=F32)
     packed[...] = ordered.astype(BF16)
     normed = layer_norm(ordered).astype(BF16)
-    fetches[1].wait()
-    qkv = lax.dot_general(normed, w_qkv[...], CONTRACT_LAST, preferred_element_type=F32)
-    heads = w_out.shape[0] // HEAD_DIM
-    width = heads * HEAD_DIM
+    qkv = []
+    for i, third in enumerate(thirds):
+        fetches[1 + i].wait()
+        qkv.append(lax.dot_general(normed, w_qkv[third, :], CONTRACT_LAST, preferred_element_type=F32))
     outs = []
-    for h in range(heads):
-        q, k, v = (qkv[:, i * width + h * HEAD_DIM : i * width + (h + 1) * HEAD_DIM].astype(BF16) for i in range(3))
+    for h in range(width // HEAD_DIM):
+        q, k, v = (piece[:, h * HEAD_DIM : (h + 1) * HEAD_DIM].astype(BF16) for piece in qkv)
         scores = lax.dot_general(q, k, CONTRACT_LAST, preferred_element_type=F32) * (1.0 / math.sqrt(HEAD_DIM))
         scores = jnp.where(same, scores, -1e30)
         raised = jnp.exp(scores - jnp.max(scores, axis=-1, keepdims=True))
         total = jnp.sum(raised, axis=-1, keepdims=True)
         outs.append(jnp.dot(raised.astype(BF16), v, preferred_element_type=F32) / total)
     attended = jnp.concatenate(outs, axis=1).astype(BF16)
-    fetches[2].wait()
+    fetches[4].wait()
     part[...] = jnp.dot(attended, w_out[...], preferred_element_type=F32).astype(BF16)
     mine, other = pl.multiple_of(core * 128, 128), pl.multiple_of(128 - core * 128, 128)
     keep[...] = part[pl.ds(mine, 128), :]
@@ -91,26 +96,42 @@
     member[...] = packed[pl.ds(mine, 128), :128]
 
 
-def mlp_kernel(
-    place, half, own_sum, far_sum, member, text, w1a, w1b, w2a, w2b, first_out, second_out, share_out, resid, part
-):
+def add_kernel(own, far, out):
+    out[...] = (own[...].astype(F32) + far[...].astype(F32)).astype(BF16)
+
+
+def mlp_share(normed, w1, w2):
+    hidden = lax.dot_general(normed, w1, CONTRACT_LAST, preferred_element_type=F32)
+    hidden = jax.nn.gelu(hidden, approximate=True).astype(BF16)
+    return jnp.dot(hidden, w2, preferred_element_type=F32)
+
+
+def near_kernel(half, own_sum, far_sum, w1_hbm, w2_hbm, resid, normed, part, w1, w2, sems):
+    fetches = [
+        pltpu.make_async_copy(source, target, sems.at[i])
+        for i, (source, target) in enumerate(((w1_hbm, w1), (w2_hbm, w2)))
+    ]
+    for fetch in fetches:
+        fetch.start()
     base = half[...].astype(F32) + own_sum[...].astype(F32) + far_sum[...].astype(F32)
     resid[...] = base.astype(BF16)
-    normed = layer_norm(resid[...].astype(F32)).astype(BF16)
-    total = None
-    for w1, w2 in ((w1a, w2a), (w1b, w2b)):
-        hidden = lax.dot_general(normed, w1[...], CONTRACT_LAST, preferred_element_type=F32)
-        hidden = jax.nn.gelu(hidden, approximate=True).astype(BF16)
-        piece = jnp.dot(hidden, w2[...], preferred_element_type=F32)
-        total = piece if total is None else total + piece
-    part[...] = total
-    share_out[...] = total.astype(BF16)
-    yl = place[1]
+    normed[...] = layer_norm(resid[...].astype(F32)).astype(BF16)
+    fetches[0].wait()
+    hidden = lax.dot_general(normed[...], w1[...], CONTRACT_LAST, preferred_element_type=F32)
+    hidden = jax.nn.gelu(hidden, approximate=True).astype(BF16)
+    fetches[1].wait()
+    part[...] = jnp.dot(hidden, w2[...], preferred_element_type=F32)
+
+
+def far_kernel(resid, normed, part, text, w1, w2, first_out, second_out, share_out, total):
+    total[...] = part[...] + mlp_share(normed[...], w1[...], w2[...])
+    share_out[...] = total[...].astype(BF16)
+    yl = lax.axis_index("yl")
     mine, other = pl.multiple_of(yl * 64, 64), pl.multiple_of(64 - yl * 64, 64)
-    width = half.shape[1]
-    first_out[:64, :width] = (part[pl.ds(mine, 64), :] + resid[pl.ds(mine, 64), :].astype(F32)).astype(BF16)
-    first_out[64:, :width] = jnp.concatenate([text[...].astype(F32), jnp.zeros((14, width), F32)], axis=0).astype(BF16)
-    second_out[...] = part[pl.ds(other, 64), :].astype(BF16)
+    width = resid.shape[1]
+    first_out[:64, :] = (total[pl.ds(mine, 64), :] + resid[pl.ds(mine, 64), :].astype(F32)).astype(BF16)
+    first_out[64:, :] = jnp.concatenate([text[...].astype(F32), jnp.zeros((14, width), F32)], axis=0).astype(BF16)
+    second_out[...] = total[pl.ds(other, 64), :].astype(BF16)
 
 
 def pool_kernel(resid, own_share, far_share, member, pooled):
@@ -128,10 +149,10 @@
     return jnp.concatenate([high, values - high], axis=0).astype(BF16)
 
 
-def loss_kernel(where, counts, multiplier, shift, pooled_sum, texts, grad_out):
+def loss_kernel(where, counts, multiplier, shift, pooled_own, pooled_far, texts, grad_out):
     row8 = lax.broadcasted_iota(I32, (8, 1), 0)
     count = jnp.where(row8 == 0, counts[0, 0], counts[0, 1]).astype(F32)
-    pooled = pooled_sum[...] / count
+    pooled = (pooled_own[...] + pooled_far[...]) / count
     norm_img = jnp.sqrt(jnp.sum(pooled * pooled, axis=1, keepdims=True) + 1e-06)
     unit = pooled / norm_img
     text = texts[...]
@@ -150,7 +171,7 @@
     slope = 1.0 / (1.0 + jnp.exp(-logits)) - jnp.where(text_index == image_index, 1.0, 0.0)
     grad = jnp.dot(two_parts(slope * per_norm), text, preferred_element_type=F32)
     grad = multiplier[0] * (grad[:8] + grad[8:])
-    grad_out[...] = ((grad - unit * jnp.sum(unit * grad, axis=1, keepdims=True)) / norm_img)[:2]
+    grad_out[...] = ((grad - unit * jnp.sum(unit * grad, axis=1, keepdims=True)) / norm_img)[:2].astype(BF16)
 
 
 def call(kernel, specs, outs, scratch=(), limit=None, flops=10**7, nbytes=10**6):
@@ -170,12 +191,11 @@
     row_count, width = rows_in.shape
     half_rows, quarter, ring = row_count // 2, row_count // 4, N_YH * N_Z
     shape = jax.ShapeDtypeStruct
-    place = jnp.stack([lax.axis_index("core"), lax.axis_index("yl")]).astype(I32)
     pair = [(0, 1), (1, 0)]
 
     keep, send, half, member = call(
         attend_kernel,
-        [SMEM, SMEM, VMEM, HBM, HBM, HBM],
+        [VMEM, VMEM, HBM, HBM, HBM],
         [
             shape((half_rows, width), BF16),
             shape((half_rows, width), BF16),
@@ -188,34 +208,39 @@
             pltpu.VMEM((row_count, width), BF16),
             pltpu.VMEM((w_qkv.shape[1], width), BF16),
             pltpu.VMEM(w_out.shape, BF16),
-            pltpu.SemaphoreType.DMA((3,)),
+            pltpu.SemaphoreType.DMA((5,)),
         ],
-        BIG,
+        ATTEND_LIMIT,
         2 * 10**9,
         8 * 10**6,
-    )(place, patch_counts, row_slots, rows_in, w_qkv.T, w_out)
+    )(patch_counts, row_slots, rows_in, w_qkv.T, w_out)
 
     got = lax.ppermute(send, "core", pair)
-    own_sum = (keep.astype(F32) + got.astype(F32)).astype(BF16)
+    own_sum = call(add_kernel, [VMEM] * 2, shape((half_rows, width), BF16), limit=SMALL, flops=ADD_FLOPS)(keep, got)
     own_sum, far_w1, far_w2 = lax.optimization_barrier((own_sum, w_fc1.T, w_fc2))
     far_sum = lax.ppermute(own_sum, "yl", pair)
     far_w1 = lax.ppermute(far_w1, "core", pair)
     far_w2 = lax.ppermute(far_w2, "core", pair)
 
-    first, second, share, resid = call(
-        mlp_kernel,
-        [SMEM] + [VMEM] * 9,
-        [
-            shape((quarter + 16, width), BF16),
-            shape((quarter, width), BF16),
-            shape((half_rows, width), BF16),
-            shape((half_rows, width), BF16),
-        ],
+    hidden = w_fc2.shape[0]
+    resid, normed, part = call(
+        near_kernel,
+        [VMEM, VMEM, VMEM, HBM, HBM],
+        [shape((half_rows, width), BF16), shape((half_rows, width), BF16), shape((half_rows, width), F32)],
+        [pltpu.VMEM((hidden, width), BF16), pltpu.VMEM((hidden, width), BF16), pltpu.SemaphoreType.DMA((2,))],
+        NEAR_LIMIT,
+        NEAR_FLOPS,
+        16 * 10**6,
+    )(half, own_sum, far_sum, w_fc1.T, w_fc2)
+    first, second, share = call(
+        far_kernel,
+        [VMEM] * 6,
+        [shape((quarter + 16, width), BF16), shape((quarter, width), BF16), shape((half_rows, width), BF16)],
         [pltpu.VMEM((half_rows, width), F32)],
         BIG,
         4 * 10**9,
         16 * 10**6,
-    )(place, half, own_sum, far_sum, member, text_embeds, w_fc1.T, far_w1, w_fc2, far_w2)
+    )(resid, normed, part, text_embeds, far_w1, far_w2)
 
     first = swap_quarters(first)
     second = swap_quarters(second, 2)
@@ -224,19 +249,17 @@
     text = jnp.broadcast_to(first[quarter : quarter + 2][None], layer.shape)
     arrived = lax.all_to_all(jnp.concatenate([layer, text], axis=1), RING, 0, 0, tiled=True)
 
-    pooled = call(pool_kernel, [VMEM] * 4, shape((8, width), F32))(resid, share, far_share, member)
-    pooled = lax.psum(pooled, "core")
+    pooled = call(pool_kernel, [VMEM] * 4, shape((8, width), F32), limit=SMALL, flops=POOL_FLOPS)(resid, share, far_share, member)
+    pooled_far = lax.ppermute(pooled, "core", pair)
     where = jnp.stack([lax.axis_index(DP) * 2, lax.axis_index(TP) * 2]).astype(I32)
-    grad = call(loss_kernel, [SMEM] * 4 + [VMEM] * 2, shape((2, width), F32))(
-        where, patch_counts, multiplier, shift, pooled, arrived[:, 2:].reshape(quarter, width)
-    )
-
-    high = grad.astype(BF16)
-    low = (grad - high.astype(F32)).astype(BF16)
-    bundle = jnp.concatenate([arrived[:, :2], high[None], low[None]], axis=0)
+    grad = call(loss_kernel, [SMEM] * 4 + [VMEM] * 3, shape((2, width), BF16), limit=SMALL)(
+        where, patch_counts, multiplier, shift, pooled, pooled_far, arrived[:, 2:].reshape(quarter, width)
+    )
+
+    bundle = jnp.concatenate([arrived[:, :2], grad[None]], axis=0)
     bundle = lax.all_gather(bundle, TP, axis=1, tiled=False)
     rows_out = bundle[:ring].reshape(row_count, width)
-    return rows_out, jnp.sum(bundle[ring:].astype(F32), axis=(0, 1))
+    return rows_out, jnp.sum(bundle[ring].astype(F32), axis=0)
 
 
 def solution(mesh):

time: 107 us -> 98.7 us (0.922)
  local copies, waits for them, and re-layouts: 8.63 us -> 2.49 us
  blocking collectives: 19.3 us -> 15.1 us
  waiting for transfers between devices: 18.5 us -> 21.5 us
  other arithmetic: 3.5 us -> 2.05 us
    all_to_all x1, waiting for transfers between devices: 0.01 us -> 16.3 us  [per_device(): lax.all_to_all(jnp.concatenate([layer, text], axis=1), RING, 0, 0, tiled=...]
    ppermute x1, waiting for transfers between devices: 6.57 us -> 0.01 us  [per_device(): far_share = lax.ppermute(share, 'yl', pair)]
    psum x1 -> x0, blocking collectives: 5.62 us -> none  [per_device(): pooled = lax.psum(pooled, 'core')]
    unnamed x25 -> x15, local copies, waits for them, and re-layouts: 7.47 us -> 1.98 us
    ppermute x1, waiting for transfers between devices: 8.19 us -> 3.82 us  [per_device(): far_sum = lax.ppermute(own_sum, 'yl', pair)]
    ppermute x0 -> x1, starting transfers between devices: none -> 4.13 us  [per_device(): pooled_far = lax.ppermute(pooled, 'core', pair)]
    ppermute x1, starting transfers between devices: 5.54 us -> 1.91 us  [per_device(): far_share = lax.ppermute(share, 'yl', pair)]
    ppermute x2, waiting for transfers between devices: 2.57 us -> 0.01 us  [swap_quarters(): return lax.ppermute(values, ('x',) + TP, pairs)]
  transfers between devices with their start and end apart: 8 -> 9, of which waited for: 4 -> 3; matrix products, arithmetic and copies ran while one was open for 1% -> 2% of each run, Pallas kernels for 2% -> 3%
where the time goes in v4:
time: 98.7 us; the launch traced here: 98.3 us
  starting transfers between devices  42.3 us (43%)
  waiting for transfers between devices  21.5 us (22%)
  blocking collectives  15.1 us (15%)
  Pallas kernels  12.6 us (13%)
  local copies, waits for them, and re-layouts  2.49 us (3%)
  between operations  2.23 us (2%)
  other arithmetic  2.05 us (2%)
    all_to_all x1, waiting for transfers between devices, per_device(): lax.all_to_all(jnp.concatenate([layer, text], axis=1), RING, 0, 0, tiled=...  16.3 us
    all_gather x1, blocking collectives, per_device(): bundle = lax.all_gather(bundle, TP, axis=1, tiled=False)  15.1 us
    all_to_all x1, starting transfers between devices, per_device(): lax.all_to_all(jnp.concatenate([layer, text], axis=1), RING, 0, 0, tiled=...  13.5 us
    ppermute x1, starting transfers between devices, per_device(): got = lax.ppermute(send, 'core', pair)  8.78 us
    ppermute x2, starting transfers between devices, swap_quarters(): return lax.ppermute(values, ('x',) + TP, pairs)  7.46 us
    pallas_call x1, Pallas kernels, per_device(): call(attend_kernel, [VMEM, VMEM, HBM, HBM, HBM], [shape((half_rows, width...  6.57 us
    ppermute x1, starting transfers between devices, per_device(): pooled_far = lax.ppermute(pooled, 'core', pair)  4.13 us
    ppermute x1, waiting for transfers between devices, per_device(): far_sum = lax.ppermute(own_sum, 'yl', pair)  3.82 us
  transfers between devices with their start and end apart: 9, of which 3 were waited for; matrix products, arithmetic and copies ran while one was open for 2% of the time, Pallas kernels for 3%

profile of v4, /device:TPU:1, one launch (start us, length us, event | category | flops | bytes accessed | tf_op | source)
XLA Modules:
  0.0 98.3 jit_solution(10354975561781262003)
XLA Ops:
  0.6 6.6 %shard_map.113 = (bf16[128,1152]{1,0:T(8,128)(2,1)}, bf16[128,1152]{1,0:T(8,128)(2,1)}, bf16[128,1152]{1,0:T(8,128)(2,1)}, bf16[128,128]{1,0:T(8,128)(2,1)}) custom-call(s32[1,2]{1,0:T(1,128)} %counts.3, s32[1,256]{1,0:T(1,128)} %slots.1, bf16[256,1152]{1,0:T(8,128)(2,1)} %rows_hbm.1, bf16[864,1152]{1,0:T(8,128)(2,1)} %bitcast.12, bf16[288,1152]{1,0:T(8,128)(2,1)} %w_out_hbm.1), custom_call_target="tpu_custom_call" | custom-call | flops 2000000000 | bytes 8000000 | tf_op jit(solution)/shard_map/pallas_call | solution.py:196
  7.2 8.8 %collective-permute-start = (bf16[128,1152]{1,0:T(8,128)(2,1)}, bf16[128,1152]{1,0:T(8,128)(2,1)S(1)}, u32[]{:S(2)}, u32[]{:S(2)}) collective-permute-start(bf16[128,1152]{1,0:T(8,128)(2,1)} %get-tuple-element.17), channel_id=1, source_target_pairs={{0,1},{1,0},{2,3},{3,2},{4,5},{5,4},{6,7},{7,6},{8,9},{9,8},{10,11... | collective-permute-start | bytes 884744 | tf_op jit(solution)/shard_map/ppermute | solution.py:218
  16.0 1.4 %collective-permute-done.far = bf16[128,1152]{1,0:T(8,128)(2,1)S(1)} collective-permute-done((bf16[128,1152]{1,0:T(8,128)(2,1)}, bf16[128,1152]{1,0:T(8,128)(2,1)S(1)}, u32[]{:S(2)}, u32[]{:S(2)}) %collective-permute-start) | collective-permute-done | bytes 294944 | tf_op jit(solution)/shard_map/ppermute | solution.py:218
  17.4 0.0 copy-start.5
  17.4 1.0 copy-done.5
  18.4 0.0 copy-start.1
  18.4 0.0 copy-start.2
  18.4 0.0 copy-start.4
  18.4 0.1 shard_map.114.own_sum
  18.4 2.2 %collective-permute-start.1 = (bf16[128,1152]{1,0:T(8,128)(2,1)S(1)}, bf16[128,1152]{1,0:T(8,128)(2,1)S(1)}, u32[]{:S(2)}, u32[]{:S(2)}) collective-permute-start(bf16[128,1152]{1,0:T(8,128)(2,1)S(1)} %shard_map.114.own_sum), channel_id=1, source_target_pairs={{0,2},{2,0},{1,3},{3,1},{4,6},{6,4},{5,7},{7,5},{8,10},{10,8},{9,1... | collective-permute-start | bytes 884744 | tf_op jit(solution)/shard_map/ppermute | solution.py:221
  20.6 0.0 copy-done.1
  20.6 2.3 %collective-permute-start.2 = (bf16[1076,1152]{1,0:T(8,128)(2,1)S(1)}, bf16[1076,1152]{1,0:T(8,128)(2,1)S(1)}, u32[]{:S(2)}, u32[]{:S(2)}) collective-permute-start(bf16[1076,1152]{1,0:T(8,128)(2,1)S(1)} %bitcast.9), channel_id=1, source_target_pairs={{0,1},{1,0},{2,3},{3,2},{4,5},{5,4},{6,7},{7,6},{8,9},{9,8},{10,11... | collective-permute-start | bytes 7437320 | tf_op jit(solution)/shard_map/ppermute | solution.py:222
  22.9 0.0 copy-done.2
  22.9 2.0 %collective-permute-start.3 = (bf16[1076,1152]{1,0:T(8,128)(2,1)S(1)}, bf16[1076,1152]{1,0:T(8,128)(2,1)S(1)}, u32[]{:S(2)}, u32[]{:S(2)}) collective-permute-start(bf16[1076,1152]{1,0:T(8,128)(2,1)S(1)} %copy-done.2), channel_id=1, source_target_pairs={{0,1},{1,0},{2,3},{3,2},{4,5},{5,4},{6,7},{7,6},{8,9},{9,8},{10,11... | collective-permute-start | bytes 7437320 | tf_op jit(solution)/shard_map/ppermute | solution.py:223
  25.0 3.8 %collective-permute-done.1.far_sum = bf16[128,1152]{1,0:T(8,128)(2,1)S(1)} collective-permute-done((bf16[128,1152]{1,0:T(8,128)(2,1)S(1)}, bf16[128,1152]{1,0:T(8,128)(2,1)S(1)}, u32[]{:S(2)}, u32[]{:S(2)}) %collective-permute-start.1) | collective-permute-done | bytes 294944 | tf_op jit(solution)/shard_map/ppermute | solution.py:221
  28.8 0.0 copy-done.4
  28.8 2.7 %shard_map.115 = (bf16[128,1152]{1,0:T(8,128)(2,1)S(1)}, bf16[128,1152]{1,0:T(8,128)(2,1)S(1)}, f32[128,1152]{1,0:T(8,128)S(1)}) custom-call(bf16[128,1152]{1,0:T(8,128)(2,1)S(1)} %copy-done.4, bf16[128,1152]{1,0:T(8,128)(2,1)S(1)} %shard_map.114.own_sum, bf16[128,1152]{1,0:T(8,128)(2,1)S(1)} %collective-permute-done.1.far_sum, ...), custom_call_target="tpu_custom_call" | custom-call | flops 49999998976 | bytes 16000000 | tf_op jit(solution)/shard_map/pallas_call | solution.py:226
  31.5 0.0 collective-permute-done.2.w1
  31.5 0.0 collective-permute-done.3.w2
  31.6 0.0 copy-done.3
  31.6 0.0 copy-start.6
  31.6 1.5 %shard_map.116 = (bf16[80,1152]{1,0:T(8,128)(2,1)S(1)}, bf16[64,1152]{1,0:T(8,128)(2,1)S(1)}, bf16[128,1152]{1,0:T(8,128)(2,1)S(1)}) custom-call(bf16[128,1152]{1,0:T(8,128)(2,1)S(1)} %get-tuple-element.19.resid, bf16[128,1152]{1,0:T(8,128)(2,1)S(1)} %get-tuple-element.20.normed, f32[128,1152]{1,0:T(8,128)S(1)} %get-tuple-element.21.part, ...), custom_call_target="tpu_custom_call" | custom-call | flops 4000000000 | bytes 16000000 | tf_op jit(solution)/shard_map/pallas_call | solution.py:235
  33.1 1.9 %collective-permute-start.4 = (bf16[80,1152]{1,0:T(8,128)(2,1)S(1)}, bf16[80,1152]{1,0:T(8,128)(2,1)S(1)}, u32[]{:S(2)}, u32[]{:S(2)}) collective-permute-start(bf16[80,1152]{1,0:T(8,128)(2,1)S(1)} %get-tuple-element.24), channel_id=1, source_target_pairs={{0,0},{1,4},{2,8},{3,12},{4,1},{5,5},{6,9},{7,13},{8,2},{9,6},{10,... | collective-permute-start | bytes 552968 | tf_op jit(solution)/shard_map/ppermute | solution.py:42
  35.0 5.5 %collective-permute-start.5 = (bf16[64,1152]{1,0:T(8,128)(2,1)S(1)}, bf16[64,1152]{1,0:T(8,128)(2,1)S(1)}, u32[]{:S(2)}, u32[]{:S(2)}) collective-permute-start(bf16[64,1152]{1,0:T(8,128)(2,1)S(1)} %get-tuple-element.25), channel_id=1, source_target_pairs={{0,8},{1,12},{2,0},{3,4},{4,9},{5,13},{6,1},{7,5},{8,10},{9,14},{1... | collective-permute-start | bytes 442376 | tf_op jit(solution)/shard_map/ppermute | solution.py:42
  41.9 0.1 pad_add_fusion.where
  42.0 1.9 %collective-permute-start.6 = (bf16[128,1152]{1,0:T(8,128)(2,1)S(1)}, bf16[128,1152]{1,0:T(8,128)(2,1)S(1)}, u32[]{:S(2)}, u32[]{:S(2)}) collective-permute-start(bf16[128,1152]{1,0:T(8,128)(2,1)S(1)} %get-tuple-element.26.own_share), channel_id=1, source_target_pairs={{0,2},{2,0},{1,3},{3,1},{4,6},{6,4},{5,7},{7,5},{8,10},{10,8},{9,1... | collective-permute-start | bytes 884744 | tf_op jit(solution)/shard_map/ppermute | solution.py:247
  43.9 0.0 collective-permute-done.5
  43.9 0.0 collective-permute-done.4
  44.0 0.1 reshape.15
  44.0 0.1 broadcast_in_dim.4
  44.1 1.0 %pad_maximum_fusion = bf16[32,4,1152]{2,1,0:T(4,128)(2,1)} fusion(bf16[32,2,1152]{2,1,0:T(2,128)(2,1)S(1)} %broadcast_in_dim.4, bf16[32,2,1152]{2,1,0:T(2,128)(2,1)S(1)} %reshape.15), kind=kLoop, calls=%fused_computation.1 | loop fusion | flops 589824 | bytes 589824 | tf_op jit(solution)/shard_map/concatenate | solution.py:250
  45.2 13.5 %all-to-all-start = ((bf16[32,4,1152]{2,1,0:T(4,128)(2,1)}), bf16[32,4,1152]{2,1,0:T(4,128)(2,1)S(1)}, u32[]{:S(2)}, u32[]{:S(2)}) async-start(bf16[32,4,1152]{2,1,0:T(4,128)(2,1)} %pad_maximum_fusion), calls=%async_computation | async-start | bytes 589824 | tf_op jit(solution)/shard_map/all_to_all | solution.py:250
  58.7 0.0 collective-permute-done.6.far_share
  58.7 0.0 copy-done.6
  58.7 0.0 copy-start
  58.7 0.6 shard_map.117.pooled_own
  59.4 4.1 %collective-permute-start.7 = (f32[8,1152]{1,0:T(8,128)S(1)}, f32[8,1152]{1,0:T(8,128)S(1)}, u32[]{:S(2)}, u32[]{:S(2)}) collective-permute-start(f32[8,1152]{1,0:T(8,128)S(1)} %shard_map.117.pooled_own), channel_id=1, source_target_pairs={{0,1},{1,0},{2,3},{3,2},{4,5},{5,4},{6,7},{7,6},{8,9},{9,8},{10,11... | collective-permute-start | bytes 110600 | tf_op jit(solution)/shard_map/ppermute | solution.py:253
  63.5 16.3 %all-to-all-done = bf16[32,4,1152]{2,1,0:T(4,128)(2,1)S(1)} async-done(((bf16[32,4,1152]{2,1,0:T(4,128)(2,1)}), bf16[32,4,1152]{2,1,0:T(4,128)(2,1)S(1)}, u32[]{:S(2)}, u32[]{:S(2)}) %all-to-all-start) | async-done | bytes 294944 | tf_op jit(solution)/shard_map/all_to_all | solution.py:250
  79.8 0.2 fusion.1
  80.0 0.1 reshape.16.texts
  80.1 0.0 collective-permute-done.7.pooled_far
  80.1 0.0 copy-done
  80.1 1.1 %shard_map.118 = bf16[2,1152]{1,0:T(2,128)(2,1)S(1)} custom-call(s32[2]{0:T(128)S(1)} %pad_add_fusion.where, s32[1,2]{1,0:T(1,128)S(1)} %copy-done, f32[1]{0:T(128)S(6)} %copy.25.multiplier, f32[1]{0:T(128)S(6)} %copy.26.shift, f32[8,1152]{1,0:T(8,128)S(1)} %shard_map.117.pooled_own, f32[8,1152]{1,0:T(8,128)S(1)} %collective-permute-done.7.pooled_far, ...), custom_call_target="tpu_custom_call" | custom-call | flops 10000000 | bytes 1000000 | tf_op jit(solution)/shard_map/pallas_call | solution.py:255
  81.2 0.2 pad_maximum_fusion.1
  81.4 15.1 %all-gather = bf16[33,8,1152]{2,0,1:T(8,128)(2,1)S(1)} all-gather(bf16[33,2,1152]{2,0,1:T(8,128)(2,1)S(1)} %copy.19), channel_id=2, replica_groups=mesh['yh'=2,'z'=16,'x'=4,'yl'=2,'core'=2] {'yl','core'}, dimensions={1}, use_global_device_ids=true | all-gather | bytes 760320 | tf_op jit(solution)/shard_map/all_gather | solution.py:260
  96.5 0.1 fusion
  96.6 1.0 %copy.24 = bf16[32,8,1152]{2,1,0:T(8,128)(2,1)} copy(bf16[32,8,1152]{2,0,1:T(8,128)(2,1)S(1)} %slice.30) | data formatting | bytes 1179648
  97.7 0.6 reduce.1
  (6 shorter events, 0.1 us)
Async XLA Ops:
  7.2 10.2 %collective-permute-start = (bf16[128,1152]{1,0:T(8,128)(2,1)}, bf16[128,1152]{1,0:T(8,128)(2,1)S(1)}, u32[]{:S(2)}, u32[]{:S(2)}) collective-permute-start(bf16[128,1152]{1,0:T(8,128)(2,1)} %get-tuple-element.17), channel_id=1, source_target_pairs={{0,1},{1,0},{2,3},{3,2},{4,5},{5,4},{6,7},{7,6},{8,9},{9,8},{10,11... | collective-permute-start | bytes 884744 | tf_op jit(solution)/shard_map/ppermute | solution.py:218
  17.4 1.0 copy-start.5
  18.4 2.3 %copy-start.1 = (bf16[1152,1076]{0,1:T(8,128)(2,1)S(1)}, bf16[1152,1076]{0,1:T(8,128)(2,1)}, u32[]{:S(2)}) copy-start(bf16[1152,1076]{0,1:T(8,128)(2,1)} %param.15) | copy-start | bytes 7437316
  18.4 4.6 %copy-start.2 = (bf16[1076,1152]{1,0:T(8,128)(2,1)S(1)}, bf16[1076,1152]{1,0:T(8,128)(2,1)}, u32[]{:S(2)}) copy-start(bf16[1076,1152]{1,0:T(8,128)(2,1)} %w2_hbm.1) | copy-start | bytes 7437316
  18.4 10.5 %copy-start.4 = (bf16[128,1152]{1,0:T(8,128)(2,1)S(1)}, bf16[128,1152]{1,0:T(8,128)(2,1)}, u32[]{:S(2)}) copy-start(bf16[128,1152]{1,0:T(8,128)(2,1)} %get-tuple-element.15.half) | copy-start | bytes 884740
  18.4 10.4 %collective-permute-start.1 = (bf16[128,1152]{1,0:T(8,128)(2,1)S(1)}, bf16[128,1152]{1,0:T(8,128)(2,1)S(1)}, u32[]{:S(2)}, u32[]{:S(2)}) collective-permute-start(bf16[128,1152]{1,0:T(8,128)(2,1)S(1)} %shard_map.114.own_sum), channel_id=1, source_target_pairs={{0,2},{2,0},{1,3},{3,1},{4,6},{6,4},{5,7},{7,5},{8,10},{10,8},{9,1... | collective-permute-start | bytes 884744 | tf_op jit(solution)/shard_map/ppermute | solution.py:221
  20.6 10.9 %collective-permute-start.2 = (bf16[1076,1152]{1,0:T(8,128)(2,1)S(1)}, bf16[1076,1152]{1,0:T(8,128)(2,1)S(1)}, u32[]{:S(2)}, u32[]{:S(2)}) collective-permute-start(bf16[1076,1152]{1,0:T(8,128)(2,1)S(1)} %bitcast.9), channel_id=1, source_target_pairs={{0,1},{1,0},{2,3},{3,2},{4,5},{5,4},{6,7},{7,6},{8,9},{9,8},{10,11... | collective-permute-start | bytes 7437320 | tf_op jit(solution)/shard_map/ppermute | solution.py:222
  22.9 8.6 %collective-permute-start.3 = (bf16[1076,1152]{1,0:T(8,128)(2,1)S(1)}, bf16[1076,1152]{1,0:T(8,128)(2,1)S(1)}, u32[]{:S(2)}, u32[]{:S(2)}) collective-permute-start(bf16[1076,1152]{1,0:T(8,128)(2,1)S(1)} %copy-done.2), channel_id=1, source_target_pairs={{0,1},{1,0},{2,3},{3,2},{4,5},{5,4},{6,7},{7,6},{8,9},{9,8},{10,11... | collective-permute-start | bytes 7437320 | tf_op jit(solution)/shard_map/ppermute | solution.py:223
  28.8 2.7 %copy-start.3 = (bf16[2,1152]{1,0:T(2,128)(2,1)S(1)}, bf16[2,1152]{1,0:T(2,128)(2,1)}, u32[]{:S(2)}) copy-start(bf16[2,1152]{1,0:T(2,128)(2,1)} %text.1) | copy-start | bytes 13828
  31.6 27.2 %copy-start.6 = (bf16[128,128]{1,0:T(8,128)(2,1)S(1)}, bf16[128,128]{1,0:T(8,128)(2,1)}, u32[]{:S(2)}) copy-start(bf16[128,128]{1,0:T(8,128)(2,1)} %get-tuple-element.27.member) | copy-start | bytes 98308
  33.1 10.8 %collective-permute-start.4 = (bf16[80,1152]{1,0:T(8,128)(2,1)S(1)}, bf16[80,1152]{1,0:T(8,128)(2,1)S(1)}, u32[]{:S(2)}, u32[]{:S(2)}) collective-permute-start(bf16[80,1152]{1,0:T(8,128)(2,1)S(1)} %get-tuple-element.24), channel_id=1, source_target_pairs={{0,0},{1,4},{2,8},{3,12},{4,1},{5,5},{6,9},{7,13},{8,2},{9,6},{10,... | collective-permute-start | bytes 552968 | tf_op jit(solution)/shard_map/ppermute | solution.py:42
  35.0 8.8 %collective-permute-start.5 = (bf16[64,1152]{1,0:T(8,128)(2,1)S(1)}, bf16[64,1152]{1,0:T(8,128)(2,1)S(1)}, u32[]{:S(2)}, u32[]{:S(2)}) collective-permute-start(bf16[64,1152]{1,0:T(8,128)(2,1)S(1)} %get-tuple-element.25), channel_id=1, source_target_pairs={{0,8},{1,12},{2,0},{3,4},{4,9},{5,13},{6,1},{7,5},{8,10},{9,14},{1... | collective-permute-start | bytes 442376 | tf_op jit(solution)/shard_map/ppermute | solution.py:42
  42.0 16.7 %collective-permute-start.6 = (bf16[128,1152]{1,0:T(8,128)(2,1)S(1)}, bf16[128,1152]{1,0:T(8,128)(2,1)S(1)}, u32[]{:S(2)}, u32[]{:S(2)}) collective-permute-start(bf16[128,1152]{1,0:T(8,128)(2,1)S(1)} %get-tuple-element.26.own_share), channel_id=1, source_target_pairs={{0,2},{2,0},{1,3},{3,1},{4,6},{6,4},{5,7},{7,5},{8,10},{10,8},{9,1... | collective-permute-start | bytes 884744 | tf_op jit(solution)/shard_map/ppermute | solution.py:247
  45.2 34.6 %all-to-all-start = ((bf16[32,4,1152]{2,1,0:T(4,128)(2,1)}), bf16[32,4,1152]{2,1,0:T(4,128)(2,1)S(1)}, u32[]{:S(2)}, u32[]{:S(2)}) async-start(bf16[32,4,1152]{2,1,0:T(4,128)(2,1)} %pad_maximum_fusion), calls=%async_computation | async-start | bytes 589824 | tf_op jit(solution)/shard_map/all_to_all | solution.py:250
  58.7 21.3 %copy-start = (s32[1,2]{1,0:T(1,128)S(1)}, s32[1,2]{1,0:T(1,128)}, u32[]{:S(2)}) copy-start(s32[1,2]{1,0:T(1,128)} %counts.3) | copy-start | bytes 28
  59.4 20.7 %collective-permute-start.7 = (f32[8,1152]{1,0:T(8,128)S(1)}, f32[8,1152]{1,0:T(8,128)S(1)}, u32[]{:S(2)}, u32[]{:S(2)}) collective-permute-start(f32[8,1152]{1,0:T(8,128)S(1)} %shard_map.117.pooled_own), channel_id=1, source_target_pairs={{0,1},{1,0},{2,3},{3,2},{4,5},{5,4},{6,7},{7,6},{8,9},{9,8},{10,11... | collective-permute-start | bytes 110600 | tf_op jit(solution)/shard_map/ppermute | solution.py:253

commit v5 on v4

--- a/solution.py
+++ b/solution.py
@@ -10,10 +10,11 @@
 from jax.sharding import PartitionSpec as P
 
 HEAD_DIM = 72
-N_YH, N_Z, N_X, N_YL, N_CORE = 2, 16, 4, 2, 2
-DP = ("yh", "z", "x")
+N_YH, N_Z, N_XH, N_XL, N_YL, N_CORE = 2, 16, 2, 2, 2, 2
+DP = ("yh", "z", "xh", "xl")
 TP = ("yl", "core")
-RING = ("yh", "z")
+QUARTER = ("yh", "xh")
+RING = ("z", "xl")
 HIGH = lax.Precision.HIGHEST
 F32, BF16, I32 = jnp.float32, jnp.bfloat16, jnp.int32
 VMEM = pl.BlockSpec(memory_space=pltpu.VMEM)
@@ -23,10 +24,10 @@
 CONTRACT_FIRST = (((0,), (0,)), ((), ()))
 BIG = 28 * 2**20
 SMALL = 12 * 2**20
-ATTEND_LIMIT = 61 * 2**20
-NEAR_LIMIT = 40 * 2**20
+ATTEND_LIMIT = 28 * 2**20
+NEAR_LIMIT = 28 * 2**20
 NEAR_FLOPS = 50 * 10**9
-ADD_FLOPS = 50 * 10**9
+ADD_FLOPS = 500 * 10**9
 POOL_FLOPS = 50 * 10**9
 
 
@@ -38,8 +39,8 @@
 
 
 def swap_quarters(values, flip=0):
-    pairs = [(x * N_X + t, (t ^ flip) * N_X + x) for x in range(N_X) for t in range(N_X)]
-    return lax.ppermute(values, ("x",) + TP, pairs)
+    pairs = [(q * 4 + t, (t ^ flip) * 4 + q) for q in range(4) for t in range(4)]
+    return lax.ppermute(values, QUARTER + TP, pairs)
 
 
 def attend_kernel(
@@ -54,7 +55,7 @@
     core = lax.axis_index("core")
     slot = slots[...]
     peer = slot >> 1
-    order = (peer & 1) * 128 + ((peer >> 1) & 1) * 64 + (peer >> 2) * 2 + (slot & 1)
+    order = ((peer >> 1) & 1) * 128 + (peer >> 6) * 64 + ((peer >> 2) & 15) * 4 + (peer & 1) * 2 + (slot & 1)
     moved = jnp.where(lax.broadcasted_iota(I32, (n, n), 0) == order, 1.0, 0.0).astype(BF16)
     first, second = counts[:, 0:1], counts[:, 0:1] + counts[:, 1:2]
 
@@ -106,21 +107,11 @@
     return jnp.dot(hidden, w2, preferred_element_type=F32)
 
 
-def near_kernel(half, own_sum, far_sum, w1_hbm, w2_hbm, resid, normed, part, w1, w2, sems):
-    fetches = [
-        pltpu.make_async_copy(source, target, sems.at[i])
-        for i, (source, target) in enumerate(((w1_hbm, w1), (w2_hbm, w2)))
-    ]
-    for fetch in fetches:
-        fetch.start()
+def near_kernel(half, own_sum, far_sum, w1, w2, resid, normed, part):
     base = half[...].astype(F32) + own_sum[...].astype(F32) + far_sum[...].astype(F32)
     resid[...] = base.astype(BF16)
     normed[...] = layer_norm(resid[...].astype(F32)).astype(BF16)
-    fetches[0].wait()
-    hidden = lax.dot_general(normed[...], w1[...], CONTRACT_LAST, preferred_element_type=F32)
-    hidden = jax.nn.gelu(hidden, approximate=True).astype(BF16)
-    fetches[1].wait()
-    part[...] = jnp.dot(hidden, w2[...], preferred_element_type=F32)
+    part[...] = mlp_share(normed[...], w1[...], w2[...])
 
 
 def far_kernel(resid, normed, part, text, w1, w2, first_out, second_out, share_out, total):
@@ -166,7 +157,7 @@
     cosine = lax.dot_general(two_parts(unit), text, CONTRACT_LAST, preferred_element_type=F32)
     logits = multiplier[0] * (cosine[:8] + cosine[8:]) * per_norm + shift[0]
     column = lax.broadcasted_iota(I32, logits.shape, 1)
-    text_index = (column >> 1) * (2 * N_X) + (column & 1) + where[1]
+    text_index = (column >> 2) * (4 * N_XH) + (column & 3) + where[1]
     image_index = lax.broadcasted_iota(I32, logits.shape, 0) + where[0]
     slope = 1.0 / (1.0 + jnp.exp(-logits)) - jnp.where(text_index == image_index, 1.0, 0.0)
     grad = jnp.dot(two_parts(slope * per_norm), text, preferred_element_type=F32)
@@ -189,7 +180,7 @@
 
 def per_device(rows_in, patch_counts, row_slots, w_qkv, w_out, w_fc1, w_fc2, text_embeds, multiplier, shift):
     row_count, width = rows_in.shape
-    half_rows, quarter, ring = row_count // 2, row_count // 4, N_YH * N_Z
+    half_rows, quarter, ring = row_count // 2, row_count // 4, N_Z * N_XL
     shape = jax.ShapeDtypeStruct
     pair = [(0, 1), (1, 0)]
 
@@ -197,10 +188,10 @@
         attend_kernel,
         [VMEM, VMEM, HBM, HBM, HBM],
         [
-            shape((half_rows, width), BF16),
-            shape((half_rows, width), BF16),
-            shape((half_rows, width), BF16),
-            shape((half_rows, 128), BF16),
+            pltpu.VMEM((half_rows, width), BF16),
+            pltpu.VMEM((half_rows, width), BF16),
+            pltpu.VMEM((half_rows, width), BF16),
+            pltpu.VMEM((half_rows, 128), BF16),
         ],
         [
             pltpu.VMEM((row_count, width), BF16),
@@ -213,7 +204,7 @@
         ATTEND_LIMIT,
         2 * 10**9,
         8 * 10**6,
-    )(patch_counts, row_slots, rows_in, w_qkv.T, w_out)
+    )(*(pltpu.with_memory_space_constraint(x, pltpu.HBM) for x in (patch_counts, row_slots, rows_in, w_qkv.T, w_out)))
 
     got = lax.ppermute(send, "core", pair)
     own_sum = call(add_kernel, [VMEM] * 2, shape((half_rows, width), BF16), limit=SMALL, flops=ADD_FLOPS)(keep, got)
@@ -222,12 +213,11 @@
     far_w1 = lax.ppermute(far_w1, "core", pair)
     far_w2 = lax.ppermute(far_w2, "core", pair)
 
-    hidden = w_fc2.shape[0]
     resid, normed, part = call(
         near_kernel,
-        [VMEM, VMEM, VMEM, HBM, HBM],
+        [VMEM] * 5,
         [shape((half_rows, width), BF16), shape((half_rows, width), BF16), shape((half_rows, width), F32)],
-        [pltpu.VMEM((hidden, width), BF16), pltpu.VMEM((hidden, width), BF16), pltpu.SemaphoreType.DMA((2,))],
+        (),
         NEAR_LIMIT,
         NEAR_FLOPS,
         16 * 10**6,
@@ -251,19 +241,19 @@
 
     pooled = call(pool_kernel, [VMEM] * 4, shape((8, width), F32), limit=SMALL, flops=POOL_FLOPS)(resid, share, far_share, member)
     pooled_far = lax.ppermute(pooled, "core", pair)
-    where = jnp.stack([lax.axis_index(DP) * 2, lax.axis_index(TP) * 2]).astype(I32)
+    where = jnp.stack([lax.axis_index(DP) * 2, lax.axis_index("yl") * 128 + lax.axis_index("core") * 4]).astype(I32)
     grad = call(loss_kernel, [SMEM] * 4 + [VMEM] * 3, shape((2, width), BF16), limit=SMALL)(
         where, patch_counts, multiplier, shift, pooled, pooled_far, arrived[:, 2:].reshape(quarter, width)
     )
 
     bundle = jnp.concatenate([arrived[:, :2], grad[None]], axis=0)
     bundle = lax.all_gather(bundle, TP, axis=1, tiled=False)
-    rows_out = bundle[:ring].reshape(row_count, width)
+    rows_out = bundle[:ring].reshape(N_Z, N_XL, N_YH, N_XH, 2, width).transpose(2, 0, 3, 1, 4, 5).reshape(row_count, width)
     return rows_out, jnp.sum(bundle[ring].astype(F32), axis=0)
 
 
 def solution(mesh):
-    fine = Mesh(mesh.devices.reshape(N_YH, N_Z, N_X, N_YL, N_CORE), DP + TP)
+    fine = Mesh(mesh.devices.reshape(N_YH, N_Z, N_XH, N_XL, N_YL, N_CORE), DP + TP)
     placed = (
         P(DP, None),
         P(DP, None),

time: 98.7 us -> 93.2 us (0.944)
  blocking collectives: 15.1 us -> 9.96 us
  waiting for transfers between devices: 21.5 us -> 24.7 us
  Pallas kernels: 12.6 us -> 10.7 us
  starting transfers between devices: 42.3 us -> 41 us
    all_gather x1, blocking collectives: 15.1 us -> 9.96 us  [per_device(): bundle = lax.all_gather(bundle, TP, axis=1, tiled=False)]
    all_to_all x1, waiting for transfers between devices: 16.3 us -> 19.4 us  [per_device(): lax.all_to_all(jnp.concatenate([layer, text], axis=1), RING, 0, 0, tiled=...]
    ppermute x2, starting transfers between devices: 7.46 us -> 10 us  [swap_quarters(): return lax.ppermute(values, QUARTER + TP, pairs)]
    ppermute x1, starting transfers between devices: 4.13 us -> 1.92 us  [per_device(): pooled_far = lax.ppermute(pooled, 'core', pair)]
    unnamed x15 -> x8, local copies, waits for them, and re-layouts: 1.98 us -> 0.02 us
    pallas_call x2, Pallas kernels: 9.27 us -> 7.35 us  [the longest x1 5.67 us: per_device(): call(attend_kernel, [VMEM, VMEM, HBM, HBM, HBM], [pltpu.VMEM((half_rows,...]
    all_to_all x1, starting transfers between devices: 13.5 us -> 11.9 us  [per_device(): lax.all_to_all(jnp.concatenate([layer, text], axis=1), RING, 0, 0, tiled=...]
    reshape x0 -> x2, local copies, waits for them, and re-layouts: none -> 1.26 us  [per_device(): bundle[:ring].reshape(N_Z, N_XL, N_YH, N_XH, 2, width)]
  transfers between devices with their start and end apart: 9 -> 9, of which waited for: 3 -> 4; matrix products, arithmetic and copies ran while one was open for 2% -> 2% of each run, Pallas kernels for 3% -> 2%
where the time goes in v5:
time: 93.2 us; the launch traced here: 92.8 us
  starting transfers between devices  41 us (44%)
  waiting for transfers between devices  24.7 us (27%)
  Pallas kernels  10.7 us (11%)
  blocking collectives  9.96 us (11%)
  local copies, waits for them, and re-layouts  2.24 us (2%)
  between operations  2.21 us (2%)
  other arithmetic  2.05 us (2%)
    all_to_all x1, waiting for transfers between devices, per_device(): lax.all_to_all(jnp.concatenate([layer, text], axis=1), RING, 0, 0, tiled=...  19.4 us
    all_to_all x1, starting transfers between devices, per_device(): lax.all_to_all(jnp.concatenate([layer, text], axis=1), RING, 0, 0, tiled=...  11.9 us
    ppermute x2, starting transfers between devices, swap_quarters(): return lax.ppermute(values, QUARTER + TP, pairs)  10 us
    all_gather x1, blocking collectives, per_device(): bundle = lax.all_gather(bundle, TP, axis=1, tiled=False)  9.96 us
    ppermute x1, starting transfers between devices, per_device(): got = lax.ppermute(send, 'core', pair)  8.78 us
    pallas_call x1, Pallas kernels, per_device(): call(attend_kernel, [VMEM, VMEM, HBM, HBM, HBM], [pltpu.VMEM((half_rows,...  5.67 us
    ppermute x1, waiting for transfers between devices, per_device(): far_sum = lax.ppermute(own_sum, 'yl', pair)  3.82 us
    ppermute x1, starting transfers between devices, per_device(): far_w1 = lax.ppermute(far_w1, 'core', pair)  2.28 us
  transfers between devices with their start and end apart: 9, of which 4 were waited for; matrix products, arithmetic and copies ran while one was open for 2% of the time, Pallas kernels for 2%

profile of v5, /device:TPU:1, one launch (start us, length us, event | category | flops | bytes accessed | tf_op | source)
XLA Modules:
  0.0 92.8 jit_solution(8208422537533233718)
XLA Ops:
  0.6 5.7 %shard_map.113 = (bf16[128,1152]{1,0:T(8,128)(2,1)S(1)}, bf16[128,1152]{1,0:T(8,128)(2,1)S(1)}, bf16[128,1152]{1,0:T(8,128)(2,1)S(1)}, bf16[128,128]{1,0:T(8,128)(2,1)S(1)}) custom-call(s32[1,2]{1,0:T(1,128)} %counts.3, s32[1,256]{1,0:T(1,128)} %slots.1, bf16[256,1152]{1,0:T(8,128)(2,1)} %rows_hbm.1, bf16[864,1152]{1,0:T(8,128)(2,1)} %bitcast.12, ...), custom_call_target="tpu_custom_call" | custom-call | flops 2000000000 | bytes 8000000 | tf_op jit(solution)/shard_map/pallas_call | solution.py:187
  6.3 8.8 %collective-permute-start = (bf16[128,1152]{1,0:T(8,128)(2,1)S(1)}, bf16[128,1152]{1,0:T(8,128)(2,1)S(1)}, u32[]{:S(2)}, u32[]{:S(2)}) collective-permute-start(bf16[128,1152]{1,0:T(8,128)(2,1)S(1)} %get-tuple-element.17), channel_id=1, source_target_pairs={{0,1},{1,0},{2,3},{3,2},{4,5},{5,4},{6,7},{7,6},{8,9},{9,8},{10,11... | collective-permute-start | bytes 884744 | tf_op jit(solution)/shard_map/ppermute | solution.py:209
  15.1 1.2 %collective-permute-done.far = bf16[128,1152]{1,0:T(8,128)(2,1)S(1)} collective-permute-done((bf16[128,1152]{1,0:T(8,128)(2,1)S(1)}, bf16[128,1152]{1,0:T(8,128)(2,1)S(1)}, u32[]{:S(2)}, u32[]{:S(2)}) %collective-permute-start) | collective-permute-done | bytes 294944 | tf_op jit(solution)/shard_map/ppermute | solution.py:209
  16.3 0.0 copy-start.1
  16.3 0.0 copy-start.2
  16.3 0.1 shard_map.114.own_sum
  16.4 2.2 %collective-permute-start.1 = (bf16[128,1152]{1,0:T(8,128)(2,1)S(1)}, bf16[128,1152]{1,0:T(8,128)(2,1)S(1)}, u32[]{:S(2)}, u32[]{:S(2)}) collective-permute-start(bf16[128,1152]{1,0:T(8,128)(2,1)S(1)} %shard_map.114.own_sum), channel_id=1, source_target_pairs={{0,2},{2,0},{1,3},{3,1},{4,6},{6,4},{5,7},{7,5},{8,10},{10,8},{9,1... | collective-permute-start | bytes 884744 | tf_op jit(solution)/shard_map/ppermute | solution.py:212
  18.6 0.0 copy-done.1
  18.6 2.3 %collective-permute-start.2 = (bf16[1076,1152]{1,0:T(8,128)(2,1)S(1)}, bf16[1076,1152]{1,0:T(8,128)(2,1)S(1)}, u32[]{:S(2)}, u32[]{:S(2)}) collective-permute-start(bf16[1076,1152]{1,0:T(8,128)(2,1)S(1)} %bitcast.9), channel_id=1, source_target_pairs={{0,1},{1,0},{2,3},{3,2},{4,5},{5,4},{6,7},{7,6},{8,9},{9,8},{10,11... | collective-permute-start | bytes 7437320 | tf_op jit(solution)/shard_map/ppermute | solution.py:213
  20.9 0.0 copy-done.2
  20.9 2.0 %collective-permute-start.3 = (bf16[1076,1152]{1,0:T(8,128)(2,1)S(1)}, bf16[1076,1152]{1,0:T(8,128)(2,1)S(1)}, u32[]{:S(2)}, u32[]{:S(2)}) collective-permute-start(bf16[1076,1152]{1,0:T(8,128)(2,1)S(1)} %copy-done.2), channel_id=1, source_target_pairs={{0,1},{1,0},{2,3},{3,2},{4,5},{5,4},{6,7},{7,6},{8,9},{9,8},{10,11... | collective-permute-start | bytes 7437320 | tf_op jit(solution)/shard_map/ppermute | solution.py:214
  22.9 3.8 %collective-permute-done.1.far_sum = bf16[128,1152]{1,0:T(8,128)(2,1)S(1)} collective-permute-done((bf16[128,1152]{1,0:T(8,128)(2,1)S(1)}, bf16[128,1152]{1,0:T(8,128)(2,1)S(1)}, u32[]{:S(2)}, u32[]{:S(2)}) %collective-permute-start.1) | collective-permute-done | bytes 294944 | tf_op jit(solution)/shard_map/ppermute | solution.py:212
  26.7 0.0 copy-start.3
  26.7 1.7 %shard_map.115 = (bf16[128,1152]{1,0:T(8,128)(2,1)S(1)}, bf16[128,1152]{1,0:T(8,128)(2,1)S(1)}, f32[128,1152]{1,0:T(8,128)S(1)}) custom-call(bf16[128,1152]{1,0:T(8,128)(2,1)S(1)} %get-tuple-element.15.half, bf16[128,1152]{1,0:T(8,128)(2,1)S(1)} %shard_map.114.own_sum, bf16[128,1152]{1,0:T(8,128)(2,1)S(1)} %collective-permute-done.1.far_sum, ...), custom_call_target="tpu_custom_call" | custom-call | flops 49999998976 | bytes 16000000 | tf_op jit(solution)/shard_map/pallas_call | solution.py:216
  28.4 0.0 collective-permute-done.2.w1
  28.4 0.3 collective-permute-done.3.w2
  28.7 0.0 copy-done.3
  28.7 1.5 %shard_map.116 = (bf16[80,1152]{1,0:T(8,128)(2,1)S(1)}, bf16[64,1152]{1,0:T(8,128)(2,1)S(1)}, bf16[128,1152]{1,0:T(8,128)(2,1)S(1)}) custom-call(bf16[128,1152]{1,0:T(8,128)(2,1)S(1)} %get-tuple-element.19.resid, bf16[128,1152]{1,0:T(8,128)(2,1)S(1)} %get-tuple-element.20.normed, f32[128,1152]{1,0:T(8,128)S(1)} %get-tuple-element.21.part, ...), custom_call_target="tpu_custom_call" | custom-call | flops 4000000000 | bytes 16000000 | tf_op jit(solution)/shard_map/pallas_call | solution.py:225
  30.3 1.9 %collective-permute-start.4 = (bf16[80,1152]{1,0:T(8,128)(2,1)S(1)}, bf16[80,1152]{1,0:T(8,128)(2,1)S(1)}, u32[]{:S(2)}, u32[]{:S(2)}) collective-permute-start(bf16[80,1152]{1,0:T(8,128)(2,1)S(1)} %get-tuple-element.24), channel_id=1, source_target_pairs={{0,0},{1,8},{2,256},{3,264},{8,1},{9,9},{10,257},{11,265},{256,2},... | collective-permute-start | bytes 552968 | tf_op jit(solution)/shard_map/ppermute | solution.py:43
  32.2 8.1 %collective-permute-start.5 = (bf16[64,1152]{1,0:T(8,128)(2,1)S(1)}, bf16[64,1152]{1,0:T(8,128)(2,1)S(1)}, u32[]{:S(2)}, u32[]{:S(2)}) collective-permute-start(bf16[64,1152]{1,0:T(8,128)(2,1)S(1)} %get-tuple-element.25), channel_id=1, source_target_pairs={{0,256},{1,264},{2,0},{3,8},{8,257},{9,265},{10,1},{11,9},{256,258... | collective-permute-start | bytes 442376 | tf_op jit(solution)/shard_map/ppermute | solution.py:43
  41.6 0.1 pad_add_fusion.where
  41.7 1.9 %collective-permute-start.6 = (bf16[128,1152]{1,0:T(8,128)(2,1)S(1)}, bf16[128,1152]{1,0:T(8,128)(2,1)S(1)}, u32[]{:S(2)}, u32[]{:S(2)}) collective-permute-start(bf16[128,1152]{1,0:T(8,128)(2,1)S(1)} %get-tuple-element.26.own_share), channel_id=1, source_target_pairs={{0,2},{2,0},{1,3},{3,1},{4,6},{6,4},{5,7},{7,5},{8,10},{10,8},{9,1... | collective-permute-start | bytes 884744 | tf_op jit(solution)/shard_map/ppermute | solution.py:237
  43.6 0.0 collective-permute-done.5
  43.6 0.0 collective-permute-done.4
  43.7 0.1 reshape.18
  43.8 0.1 broadcast_in_dim.4
  43.8 1.0 %pad_maximum_fusion = bf16[32,4,1152]{2,1,0:T(4,128)(2,1)} fusion(bf16[32,2,1152]{2,1,0:T(2,128)(2,1)S(1)} %broadcast_in_dim.4, bf16[32,2,1152]{2,1,0:T(2,128)(2,1)S(1)} %reshape.18), kind=kLoop, calls=%fused_computation | loop fusion | flops 589824 | bytes 589824 | tf_op jit(solution)/shard_map/concatenate | solution.py:240
  44.9 11.9 %all-to-all-start = ((bf16[32,4,1152]{2,1,0:T(4,128)(2,1)}), bf16[32,4,1152]{2,1,0:T(4,128)(2,1)S(1)}, u32[]{:S(2)}, u32[]{:S(2)}) async-start(bf16[32,4,1152]{2,1,0:T(4,128)(2,1)} %pad_maximum_fusion), calls=%async_computation | async-start | bytes 589824 | tf_op jit(solution)/shard_map/all_to_all | solution.py:240
  56.7 0.0 collective-permute-done.6.far_share
  56.8 0.0 copy-start
  56.8 0.6 shard_map.117.pooled_own
  57.4 1.9 %collective-permute-start.7 = (f32[8,1152]{1,0:T(8,128)S(1)}, f32[8,1152]{1,0:T(8,128)S(1)}, u32[]{:S(2)}, u32[]{:S(2)}) collective-permute-start(f32[8,1152]{1,0:T(8,128)S(1)} %shard_map.117.pooled_own), channel_id=1, source_target_pairs={{0,1},{1,0},{2,3},{3,2},{4,5},{5,4},{6,7},{7,6},{8,9},{9,8},{10,11... | collective-permute-start | bytes 110600 | tf_op jit(solution)/shard_map/ppermute | solution.py:243
  59.3 19.4 %all-to-all-done = bf16[32,4,1152]{2,1,0:T(4,128)(2,1)S(1)} async-done(((bf16[32,4,1152]{2,1,0:T(4,128)(2,1)}), bf16[32,4,1152]{2,1,0:T(4,128)(2,1)S(1)}, u32[]{:S(2)}, u32[]{:S(2)}) %all-to-all-start) | async-done | bytes 294944 | tf_op jit(solution)/shard_map/all_to_all | solution.py:240
  78.7 0.2 fusion.1
  78.9 0.1 reshape.19.texts
  78.9 0.0 collective-permute-done.7.pooled_far
  78.9 0.0 copy-done
  79.0 1.1 %shard_map.118 = bf16[2,1152]{1,0:T(2,128)(2,1)S(1)} custom-call(s32[2]{0:T(128)S(1)} %pad_add_fusion.where, s32[1,2]{1,0:T(1,128)S(1)} %copy-done, f32[1]{0:T(128)S(6)} %copy.20.multiplier, f32[1]{0:T(128)S(6)} %copy.21.shift, f32[8,1152]{1,0:T(8,128)S(1)} %shard_map.117.pooled_own, f32[8,1152]{1,0:T(8,128)S(1)} %collective-permute-done.7.pooled_far, ...), custom_call_target="tpu_custom_call" | custom-call | flops 10000000 | bytes 1000000 | tf_op jit(solution)/shard_map/pallas_call | solution.py:245
  80.1 0.2 pad_maximum_fusion.1
  80.3 10.0 %all-gather = bf16[33,8,1152]{2,0,1:T(8,128)(2,1)S(1)} all-gather(bf16[33,2,1152]{2,0,1:T(8,128)(2,1)S(1)} %copy.17), channel_id=2, replica_groups=mesh['yh'=2,'z'=16,'xh'=2,'xl'=2,'yl'=2,'core'=2] {'yl','core'}, dimensions={1}, use_global_device_ids=true | all-gather | bytes 760320 | tf_op jit(solution)/shard_map/all_gather | solution.py:250
  90.3 0.1 fusion
  90.4 0.2 reshape.20
  90.7 0.5 copy.18
  91.1 1.0 %reshape.21 = bf16[256,1152]{1,0:T(8,128)(2,1)} reshape(bf16[2,16,2,2,2,1152]{5,4,3,2,1,0:T(2,128)(2,1)S(1)} %copy.18) | data formatting | bytes 1179648 | tf_op jit(solution)/shard_map/reshape | solution.py:251
  92.2 0.6 reduce.1
  (5 shorter events, 0.1 us)
Async XLA Ops:
  6.3 10.0 %collective-permute-start = (bf16[128,1152]{1,0:T(8,128)(2,1)S(1)}, bf16[128,1152]{1,0:T(8,128)(2,1)S(1)}, u32[]{:S(2)}, u32[]{:S(2)}) collective-permute-start(bf16[128,1152]{1,0:T(8,128)(2,1)S(1)} %get-tuple-element.17), channel_id=1, source_target_pairs={{0,1},{1,0},{2,3},{3,2},{4,5},{5,4},{6,7},{7,6},{8,9},{9,8},{10,11... | collective-permute-start | bytes 884744 | tf_op jit(solution)/shard_map/ppermute | solution.py:209
  16.3 2.3 %copy-start.1 = (bf16[1152,1076]{0,1:T(8,128)(2,1)S(1)}, bf16[1152,1076]{0,1:T(8,128)(2,1)}, u32[]{:S(2)}) copy-start(bf16[1152,1076]{0,1:T(8,128)(2,1)} %param.15) | copy-start | bytes 7437316
  16.3 4.6 %copy-start.2 = (bf16[1076,1152]{1,0:T(8,128)(2,1)S(1)}, bf16[1076,1152]{1,0:T(8,128)(2,1)}, u32[]{:S(2)}) copy-start(bf16[1076,1152]{1,0:T(8,128)(2,1)} %w2.1) | copy-start | bytes 7437316
  16.4 10.4 %collective-permute-start.1 = (bf16[128,1152]{1,0:T(8,128)(2,1)S(1)}, bf16[128,1152]{1,0:T(8,128)(2,1)S(1)}, u32[]{:S(2)}, u32[]{:S(2)}) collective-permute-start(bf16[128,1152]{1,0:T(8,128)(2,1)S(1)} %shard_map.114.own_sum), channel_id=1, source_target_pairs={{0,2},{2,0},{1,3},{3,1},{4,6},{6,4},{5,7},{7,5},{8,10},{10,8},{9,1... | collective-permute-start | bytes 884744 | tf_op jit(solution)/shard_map/ppermute | solution.py:212
  18.6 9.9 %collective-permute-start.2 = (bf16[1076,1152]{1,0:T(8,128)(2,1)S(1)}, bf16[1076,1152]{1,0:T(8,128)(2,1)S(1)}, u32[]{:S(2)}, u32[]{:S(2)}) collective-permute-start(bf16[1076,1152]{1,0:T(8,128)(2,1)S(1)} %bitcast.9), channel_id=1, source_target_pairs={{0,1},{1,0},{2,3},{3,2},{4,5},{5,4},{6,7},{7,6},{8,9},{9,8},{10,11... | collective-permute-start | bytes 7437320 | tf_op jit(solution)/shard_map/ppermute | solution.py:213
  20.9 7.9 %collective-permute-start.3 = (bf16[1076,1152]{1,0:T(8,128)(2,1)S(1)}, bf16[1076,1152]{1,0:T(8,128)(2,1)S(1)}, u32[]{:S(2)}, u32[]{:S(2)}) collective-permute-start(bf16[1076,1152]{1,0:T(8,128)(2,1)S(1)} %copy-done.2), channel_id=1, source_target_pairs={{0,1},{1,0},{2,3},{3,2},{4,5},{5,4},{6,7},{7,6},{8,9},{9,8},{10,11... | collective-permute-start | bytes 7437320 | tf_op jit(solution)/shard_map/ppermute | solution.py:214
  26.7 2.0 %copy-start.3 = (bf16[2,1152]{1,0:T(2,128)(2,1)S(1)}, bf16[2,1152]{1,0:T(2,128)(2,1)}, u32[]{:S(2)}) copy-start(bf16[2,1152]{1,0:T(2,128)(2,1)} %text.1) | copy-start | bytes 13828
  30.3 13.3 %collective-permute-start.4 = (bf16[80,1152]{1,0:T(8,128)(2,1)S(1)}, bf16[80,1152]{1,0:T(8,128)(2,1)S(1)}, u32[]{:S(2)}, u32[]{:S(2)}) collective-permute-start(bf16[80,1152]{1,0:T(8,128)(2,1)S(1)} %get-tuple-element.24), channel_id=1, source_target_pairs={{0,0},{1,8},{2,256},{3,264},{8,1},{9,9},{10,257},{11,265},{256,2},... | collective-permute-start | bytes 552968 | tf_op jit(solution)/shard_map/ppermute | solution.py:43
  32.2 11.4 %collective-permute-start.5 = (bf16[64,1152]{1,0:T(8,128)(2,1)S(1)}, bf16[64,1152]{1,0:T(8,128)(2,1)S(1)}, u32[]{:S(2)}, u32[]{:S(2)}) collective-permute-start(bf16[64,1152]{1,0:T(8,128)(2,1)S(1)} %get-tuple-element.25), channel_id=1, source_target_pairs={{0,256},{1,264},{2,0},{3,8},{8,257},{9,265},{10,1},{11,9},{256,258... | collective-permute-start | bytes 442376 | tf_op jit(solution)/shard_map/ppermute | solution.py:43
  41.7 15.1 %collective-permute-start.6 = (bf16[128,1152]{1,0:T(8,128)(2,1)S(1)}, bf16[128,1152]{1,0:T(8,128)(2,1)S(1)}, u32[]{:S(2)}, u32[]{:S(2)}) collective-permute-start(bf16[128,1152]{1,0:T(8,128)(2,1)S(1)} %get-tuple-element.26.own_share), channel_id=1, source_target_pairs={{0,2},{2,0},{1,3},{3,1},{4,6},{6,4},{5,7},{7,5},{8,10},{10,8},{9,1... | collective-permute-start | bytes 884744 | tf_op jit(solution)/shard_map/ppermute | solution.py:237
  44.9 33.8 %all-to-all-start = ((bf16[32,4,1152]{2,1,0:T(4,128)(2,1)}), bf16[32,4,1152]{2,1,0:T(4,128)(2,1)S(1)}, u32[]{:S(2)}, u32[]{:S(2)}) async-start(bf16[32,4,1152]{2,1,0:T(4,128)(2,1)} %pad_maximum_fusion), calls=%async_computation | async-start | bytes 589824 | tf_op jit(solution)/shard_map/all_to_all | solution.py:240
  56.8 22.2 %copy-start = (s32[1,2]{1,0:T(1,128)S(1)}, s32[1,2]{1,0:T(1,128)}, u32[]{:S(2)}) copy-start(s32[1,2]{1,0:T(1,128)} %counts.3) | copy-start | bytes 28
  57.4 21.6 %collective-permute-start.7 = (f32[8,1152]{1,0:T(8,128)S(1)}, f32[8,1152]{1,0:T(8,128)S(1)}, u32[]{:S(2)}, u32[]{:S(2)}) collective-permute-start(f32[8,1152]{1,0:T(8,128)S(1)} %shard_map.117.pooled_own), channel_id=1, source_target_pairs={{0,1},{1,0},{2,3},{3,2},{4,5},{5,4},{6,7},{7,6},{8,9},{9,8},{10,11... | collective-permute-start | bytes 110600 | tf_op jit(solution)/shard_map/ppermute | solution.py:243

commit v6 on v5

--- a/solution.py
+++ b/solution.py
@@ -73,10 +73,10 @@
     ordered = jnp.dot(moved, rows[...], preferred_element_type=F32)
     packed[...] = ordered.astype(BF16)
     normed = layer_norm(ordered).astype(BF16)
-    qkv = []
-    for i, third in enumerate(thirds):
+    for i in range(3):
         fetches[1 + i].wait()
-        qkv.append(lax.dot_general(normed, w_qkv[third, :], CONTRACT_LAST, preferred_element_type=F32))
+    qkv = lax.dot_general(normed, w_qkv[...], CONTRACT_LAST, preferred_element_type=F32)
+    qkv = [qkv[:, i * width : (i + 1) * width] for i in range(3)]
     outs = []
     for h in range(width // HEAD_DIM):
         q, k, v = (piece[:, h * HEAD_DIM : (h + 1) * HEAD_DIM].astype(BF16) for piece in qkv)
@@ -165,6 +165,28 @@
     grad_out[...] = ((grad - unit * jnp.sum(unit * grad, axis=1, keepdims=True)) / norm_img)[:2].astype(BF16)
 
 
+def place_kernel(gathered, rows_out, grad_out):
+    planes, count, _ = gathered.shape
+    per_half = planes // N_YH
+    row = lax.broadcasted_iota(I32, (128, count), 0)
+    column = lax.broadcasted_iota(I32, (128, count), 1)
+    last = jnp.where(lax.broadcasted_iota(I32, (16, count), 1) == count - 1, 1.0, 0.0).astype(BF16)
+    grads = [None] * 2
+    for half in range(N_YH):
+        total = None
+        for k in range(per_half):
+            plane = gathered[half * per_half + k]
+            xh, image = k // 2, k % 2
+            target = (column >> 1) * 8 + xh * 4 + (column & 1) * 2 + image
+            pick = jnp.where((row == target) & (column < count - 1), 1.0, 0.0).astype(BF16)
+            piece = jnp.dot(pick, plane, preferred_element_type=F32)
+            total = piece if total is None else total + piece
+            share = jnp.dot(last, plane, preferred_element_type=F32)[:1]
+            grads[image] = share if grads[image] is None else grads[image] + share
+        rows_out[half * 128 : (half + 1) * 128, :] = total.astype(BF16)
+    grad_out[...] = jnp.concatenate(grads, axis=0)
+
+
 def call(kernel, specs, outs, scratch=(), limit=None, flops=10**7, nbytes=10**6):
     many = isinstance(outs, list)
     return pl.pallas_call(
@@ -248,8 +270,8 @@
 
     bundle = jnp.concatenate([arrived[:, :2], grad[None]], axis=0)
     bundle = lax.all_gather(bundle, TP, axis=1, tiled=False)
-    rows_out = bundle[:ring].reshape(N_Z, N_XL, N_YH, N_XH, 2, width).transpose(2, 0, 3, 1, 4, 5).reshape(row_count, width)
-    return rows_out, jnp.sum(bundle[ring].astype(F32), axis=0)
+    gathered = bundle.reshape(ring + 1, 8, width).transpose(1, 0, 2)
+    return call(place_kernel, [VMEM], [shape((row_count, width), BF16), shape((2, width), F32)], limit=SMALL)(gathered)
 
 
 def solution(mesh):

time: 93.2 us -> 91.5 us (0.982)
  local copies, waits for them, and re-layouts: 2.24 us -> 0.45 us
    pallas_call x0 -> x1, Pallas kernels: none -> 1.69 us  [per_device(): call(place_kernel, [VMEM], [shape((row_count, width), BF16), shape((2, wi...]
    reshape x2 -> x0, local copies, waits for them, and re-layouts: 1.26 us -> none  [per_device(): bundle[:ring].reshape(N_Z, N_XL, N_YH, N_XH, 2, width)]
  transfers between devices with their start and end apart: 9 -> 9, of which waited for: 4 -> 4; matrix products, arithmetic and copies ran while one was open for 2% -> 2% of each run, Pallas kernels for 2% -> 3%
where the time goes in v6:
time: 91.5 us; the launch traced here: 91.1 us
  starting transfers between devices  41 us (45%)
  waiting for transfers between devices  24.7 us (27%)
  Pallas kernels  11.4 us (12%)
  blocking collectives  9.96 us (11%)
  between operations  2.18 us (2%)
  other arithmetic  1.34 us (1%)
    all_to_all x1, waiting for transfers between devices, per_device(): lax.all_to_all(jnp.concatenate([layer, text], axis=1), RING, 0, 0, tiled=...  19.3 us
    all_to_all x1, starting transfers between devices, per_device(): lax.all_to_all(jnp.concatenate([layer, text], axis=1), RING, 0, 0, tiled=...  11.9 us
    ppermute x2, starting transfers between devices, swap_quarters(): return lax.ppermute(values, QUARTER + TP, pairs)  10 us
    all_gather x1, blocking collectives, per_device(): bundle = lax.all_gather(bundle, TP, axis=1, tiled=False)  9.96 us
    ppermute x1, starting transfers between devices, per_device(): got = lax.ppermute(send, 'core', pair)  8.79 us
    pallas_call x1, Pallas kernels, per_device(): call(attend_kernel, [VMEM, VMEM, HBM, HBM, HBM], [pltpu.VMEM((half_rows,...  4.76 us
    ppermute x1, waiting for transfers between devices, per_device(): far_sum = lax.ppermute(own_sum, 'yl', pair)  3.82 us
    ppermute x1, starting transfers between devices, per_device(): far_w1 = lax.ppermute(far_w1, 'core', pair)  2.28 us
  transfers between devices with their start and end apart: 9, of which 4 were waited for; matrix products, arithmetic and copies ran while one was open for 2% of the time, Pallas kernels for 3%

profile of v6, /device:TPU:1, one launch (start us, length us, event | category | flops | bytes accessed | tf_op | source)
XLA Modules:
  0.0 91.1 jit_solution(5436249862014776214)
XLA Ops:
  0.6 4.8 %shard_map.113 = (bf16[128,1152]{1,0:T(8,128)(2,1)S(1)}, bf16[128,1152]{1,0:T(8,128)(2,1)S(1)}, bf16[128,1152]{1,0:T(8,128)(2,1)S(1)}, bf16[128,128]{1,0:T(8,128)(2,1)S(1)}) custom-call(s32[1,2]{1,0:T(1,128)} %counts.3, s32[1,256]{1,0:T(1,128)} %slots.1, bf16[256,1152]{1,0:T(8,128)(2,1)} %rows_hbm.1, bf16[864,1152]{1,0:T(8,128)(2,1)} %bitcast.10, ...), custom_call_target="tpu_custom_call" | custom-call | flops 2000000000 | bytes 8000000 | tf_op jit(solution)/shard_map/pallas_call | solution.py:209
  5.4 8.8 %collective-permute-start = (bf16[128,1152]{1,0:T(8,128)(2,1)S(1)}, bf16[128,1152]{1,0:T(8,128)(2,1)S(1)}, u32[]{:S(2)}, u32[]{:S(2)}) collective-permute-start(bf16[128,1152]{1,0:T(8,128)(2,1)S(1)} %get-tuple-element.17), channel_id=1, source_target_pairs={{0,1},{1,0},{2,3},{3,2},{4,5},{5,4},{6,7},{7,6},{8,9},{9,8},{10,11... | collective-permute-start | bytes 884744 | tf_op jit(solution)/shard_map/ppermute | solution.py:231
  14.2 1.2 %collective-permute-done.far = bf16[128,1152]{1,0:T(8,128)(2,1)S(1)} collective-permute-done((bf16[128,1152]{1,0:T(8,128)(2,1)S(1)}, bf16[128,1152]{1,0:T(8,128)(2,1)S(1)}, u32[]{:S(2)}, u32[]{:S(2)}) %collective-permute-start) | collective-permute-done | bytes 294944 | tf_op jit(solution)/shard_map/ppermute | solution.py:231
  15.4 0.0 copy-start.1
  15.4 0.0 copy-start.2
  15.4 0.1 shard_map.114.own_sum
  15.5 2.2 %collective-permute-start.1 = (bf16[128,1152]{1,0:T(8,128)(2,1)S(1)}, bf16[128,1152]{1,0:T(8,128)(2,1)S(1)}, u32[]{:S(2)}, u32[]{:S(2)}) collective-permute-start(bf16[128,1152]{1,0:T(8,128)(2,1)S(1)} %shard_map.114.own_sum), channel_id=1, source_target_pairs={{0,2},{2,0},{1,3},{3,1},{4,6},{6,4},{5,7},{7,5},{8,10},{10,8},{9,1... | collective-permute-start | bytes 884744 | tf_op jit(solution)/shard_map/ppermute | solution.py:234
  17.7 0.0 copy-done.1
  17.7 2.3 %collective-permute-start.2 = (bf16[1076,1152]{1,0:T(8,128)(2,1)S(1)}, bf16[1076,1152]{1,0:T(8,128)(2,1)S(1)}, u32[]{:S(2)}, u32[]{:S(2)}) collective-permute-start(bf16[1076,1152]{1,0:T(8,128)(2,1)S(1)} %bitcast.8), channel_id=1, source_target_pairs={{0,1},{1,0},{2,3},{3,2},{4,5},{5,4},{6,7},{7,6},{8,9},{9,8},{10,11... | collective-permute-start | bytes 7437320 | tf_op jit(solution)/shard_map/ppermute | solution.py:235
  20.0 0.0 copy-done.2
  20.0 2.0 %collective-permute-start.3 = (bf16[1076,1152]{1,0:T(8,128)(2,1)S(1)}, bf16[1076,1152]{1,0:T(8,128)(2,1)S(1)}, u32[]{:S(2)}, u32[]{:S(2)}) collective-permute-start(bf16[1076,1152]{1,0:T(8,128)(2,1)S(1)} %copy-done.2), channel_id=1, source_target_pairs={{0,1},{1,0},{2,3},{3,2},{4,5},{5,4},{6,7},{7,6},{8,9},{9,8},{10,11... | collective-permute-start | bytes 7437320 | tf_op jit(solution)/shard_map/ppermute | solution.py:236
  22.0 3.8 %collective-permute-done.1.far_sum = bf16[128,1152]{1,0:T(8,128)(2,1)S(1)} collective-permute-done((bf16[128,1152]{1,0:T(8,128)(2,1)S(1)}, bf16[128,1152]{1,0:T(8,128)(2,1)S(1)}, u32[]{:S(2)}, u32[]{:S(2)}) %collective-permute-start.1) | collective-permute-done | bytes 294944 | tf_op jit(solution)/shard_map/ppermute | solution.py:234
  25.8 0.0 copy-start.3
  25.8 1.7 %shard_map.115 = (bf16[128,1152]{1,0:T(8,128)(2,1)S(1)}, bf16[128,1152]{1,0:T(8,128)(2,1)S(1)}, f32[128,1152]{1,0:T(8,128)S(1)}) custom-call(bf16[128,1152]{1,0:T(8,128)(2,1)S(1)} %get-tuple-element.15.half, bf16[128,1152]{1,0:T(8,128)(2,1)S(1)} %shard_map.114.own_sum, bf16[128,1152]{1,0:T(8,128)(2,1)S(1)} %collective-permute-done.1.far_sum, ...), custom_call_target="tpu_custom_call" | custom-call | flops 49999998976 | bytes 16000000 | tf_op jit(solution)/shard_map/pallas_call | solution.py:238
  27.5 0.0 collective-permute-done.2.w1
  27.5 0.3 collective-permute-done.3.w2
  27.8 0.0 copy-done.3
  27.8 1.5 %shard_map.116 = (bf16[80,1152]{1,0:T(8,128)(2,1)S(1)}, bf16[64,1152]{1,0:T(8,128)(2,1)S(1)}, bf16[128,1152]{1,0:T(8,128)(2,1)S(1)}) custom-call(bf16[128,1152]{1,0:T(8,128)(2,1)S(1)} %get-tuple-element.19.resid, bf16[128,1152]{1,0:T(8,128)(2,1)S(1)} %get-tuple-element.20.normed, f32[128,1152]{1,0:T(8,128)S(1)} %get-tuple-element.21.part, ...), custom_call_target="tpu_custom_call" | custom-call | flops 4000000000 | bytes 16000000 | tf_op jit(solution)/shard_map/pallas_call | solution.py:247
  29.4 1.9 %collective-permute-start.4 = (bf16[80,1152]{1,0:T(8,128)(2,1)S(1)}, bf16[80,1152]{1,0:T(8,128)(2,1)S(1)}, u32[]{:S(2)}, u32[]{:S(2)}) collective-permute-start(bf16[80,1152]{1,0:T(8,128)(2,1)S(1)} %get-tuple-element.24), channel_id=1, source_target_pairs={{0,0},{1,8},{2,256},{3,264},{8,1},{9,9},{10,257},{11,265},{256,2},... | collective-permute-start | bytes 552968 | tf_op jit(solution)/shard_map/ppermute | solution.py:43
  31.3 8.1 %collective-permute-start.5 = (bf16[64,1152]{1,0:T(8,128)(2,1)S(1)}, bf16[64,1152]{1,0:T(8,128)(2,1)S(1)}, u32[]{:S(2)}, u32[]{:S(2)}) collective-permute-start(bf16[64,1152]{1,0:T(8,128)(2,1)S(1)} %get-tuple-element.25), channel_id=1, source_target_pairs={{0,256},{1,264},{2,0},{3,8},{8,257},{9,265},{10,1},{11,9},{256,258... | collective-permute-start | bytes 442376 | tf_op jit(solution)/shard_map/ppermute | solution.py:43
  40.7 0.1 pad_add_fusion.where
  40.8 1.9 %collective-permute-start.6 = (bf16[128,1152]{1,0:T(8,128)(2,1)S(1)}, bf16[128,1152]{1,0:T(8,128)(2,1)S(1)}, u32[]{:S(2)}, u32[]{:S(2)}) collective-permute-start(bf16[128,1152]{1,0:T(8,128)(2,1)S(1)} %get-tuple-element.26.own_share), channel_id=1, source_target_pairs={{0,2},{2,0},{1,3},{3,1},{4,6},{6,4},{5,7},{7,5},{8,10},{10,8},{9,1... | collective-permute-start | bytes 884744 | tf_op jit(solution)/shard_map/ppermute | solution.py:259
  42.7 0.0 collective-permute-done.5
  42.7 0.0 collective-permute-done.4
  42.8 0.1 reshape.14
  42.9 0.1 broadcast_in_dim.4
  42.9 1.0 %pad_maximum_fusion = bf16[32,4,1152]{2,1,0:T(4,128)(2,1)} fusion(bf16[32,2,1152]{2,1,0:T(2,128)(2,1)S(1)} %broadcast_in_dim.4, bf16[32,2,1152]{2,1,0:T(2,128)(2,1)S(1)} %reshape.14), kind=kLoop, calls=%fused_computation | loop fusion | flops 589824 | bytes 589824 | tf_op jit(solution)/shard_map/concatenate | solution.py:262
  44.0 11.9 %all-to-all-start = ((bf16[32,4,1152]{2,1,0:T(4,128)(2,1)}), bf16[32,4,1152]{2,1,0:T(4,128)(2,1)S(1)}, u32[]{:S(2)}, u32[]{:S(2)}) async-start(bf16[32,4,1152]{2,1,0:T(4,128)(2,1)} %pad_maximum_fusion), calls=%async_computation | async-start | bytes 589824 | tf_op jit(solution)/shard_map/all_to_all | solution.py:262
  55.9 0.0 collective-permute-done.6.far_share
  55.9 0.0 copy-start
  55.9 0.6 shard_map.117.pooled_own
  56.5 1.9 %collective-permute-start.7 = (f32[8,1152]{1,0:T(8,128)S(1)}, f32[8,1152]{1,0:T(8,128)S(1)}, u32[]{:S(2)}, u32[]{:S(2)}) collective-permute-start(f32[8,1152]{1,0:T(8,128)S(1)} %shard_map.117.pooled_own), channel_id=1, source_target_pairs={{0,1},{1,0},{2,3},{3,2},{4,5},{5,4},{6,7},{7,6},{8,9},{9,8},{10,11... | collective-permute-start | bytes 110600 | tf_op jit(solution)/shard_map/ppermute | solution.py:265
  58.4 19.3 %all-to-all-done = bf16[32,4,1152]{2,1,0:T(4,128)(2,1)S(1)} async-done(((bf16[32,4,1152]{2,1,0:T(4,128)(2,1)}), bf16[32,4,1152]{2,1,0:T(4,128)(2,1)S(1)}, u32[]{:S(2)}, u32[]{:S(2)}) %all-to-all-start) | async-done | bytes 294944 | tf_op jit(solution)/shard_map/all_to_all | solution.py:262
  77.8 0.2 fusion
  78.0 0.1 reshape.15.texts
  78.0 0.0 collective-permute-done.7.pooled_far
  78.0 0.0 copy-done
  78.0 1.1 %shard_map.118 = bf16[2,1152]{1,0:T(2,128)(2,1)S(1)} custom-call(s32[2]{0:T(128)S(1)} %pad_add_fusion.where, s32[1,2]{1,0:T(1,128)S(1)} %copy-done, f32[1]{0:T(128)S(6)} %copy.16.multiplier, f32[1]{0:T(128)S(6)} %copy.17.shift, f32[8,1152]{1,0:T(8,128)S(1)} %shard_map.117.pooled_own, f32[8,1152]{1,0:T(8,128)S(1)} %collective-permute-done.7.pooled_far, ...), custom_call_target="tpu_custom_call" | custom-call | flops 10000000 | bytes 1000000 | tf_op jit(solution)/shard_map/pallas_call | solution.py:267
  79.2 0.2 pad_maximum_fusion.1
  79.4 10.0 %all-gather = bf16[33,8,1152]{2,0,1:T(8,128)(2,1)S(1)} all-gather(bf16[33,2,1152]{2,0,1:T(8,128)(2,1)S(1)} %copy.15), channel_id=2, replica_groups=mesh['yh'=2,'z'=16,'xh'=2,'xl'=2,'yl'=2,'core'=2] {'yl','core'}, dimensions={1}, use_global_device_ids=true | all-gather | bytes 760320 | tf_op jit(solution)/shard_map/all_gather | solution.py:272
  89.4 1.7 %shard_map.119 = (bf16[256,1152]{1,0:T(8,128)(2,1)}, f32[2,1152]{1,0:T(2,128)}) custom-call(bf16[8,33,1152]{2,1,0:T(8,128)(2,1)S(1)} %bitcast.6), custom_call_target="tpu_custom_call" | custom-call | flops 10000000 | bytes 1000000 | tf_op jit(solution)/shard_map/pallas_call | solution.py:274
  (3 shorter events, 0.1 us)
Async XLA Ops:
  5.4 10.0 %collective-permute-start = (bf16[128,1152]{1,0:T(8,128)(2,1)S(1)}, bf16[128,1152]{1,0:T(8,128)(2,1)S(1)}, u32[]{:S(2)}, u32[]{:S(2)}) collective-permute-start(bf16[128,1152]{1,0:T(8,128)(2,1)S(1)} %get-tuple-element.17), channel_id=1, source_target_pairs={{0,1},{1,0},{2,3},{3,2},{4,5},{5,4},{6,7},{7,6},{8,9},{9,8},{10,11... | collective-permute-start | bytes 884744 | tf_op jit(solution)/shard_map/ppermute | solution.py:231
  15.4 2.3 %copy-start.1 = (bf16[1152,1076]{0,1:T(8,128)(2,1)S(1)}, bf16[1152,1076]{0,1:T(8,128)(2,1)}, u32[]{:S(2)}) copy-start(bf16[1152,1076]{0,1:T(8,128)(2,1)} %param.15) | copy-start | bytes 7437316
  15.4 4.6 %copy-start.2 = (bf16[1076,1152]{1,0:T(8,128)(2,1)S(1)}, bf16[1076,1152]{1,0:T(8,128)(2,1)}, u32[]{:S(2)}) copy-start(bf16[1076,1152]{1,0:T(8,128)(2,1)} %w2.1) | copy-start | bytes 7437316
  15.5 10.4 %collective-permute-start.1 = (bf16[128,1152]{1,0:T(8,128)(2,1)S(1)}, bf16[128,1152]{1,0:T(8,128)(2,1)S(1)}, u32[]{:S(2)}, u32[]{:S(2)}) collective-permute-start(bf16[128,1152]{1,0:T(8,128)(2,1)S(1)} %shard_map.114.own_sum), channel_id=1, source_target_pairs={{0,2},{2,0},{1,3},{3,1},{4,6},{6,4},{5,7},{7,5},{8,10},{10,8},{9,1... | collective-permute-start | bytes 884744 | tf_op jit(solution)/shard_map/ppermute | solution.py:234
  17.7 9.9 %collective-permute-start.2 = (bf16[1076,1152]{1,0:T(8,128)(2,1)S(1)}, bf16[1076,1152]{1,0:T(8,128)(2,1)S(1)}, u32[]{:S(2)}, u32[]{:S(2)}) collective-permute-start(bf16[1076,1152]{1,0:T(8,128)(2,1)S(1)} %bitcast.8), channel_id=1, source_target_pairs={{0,1},{1,0},{2,3},{3,2},{4,5},{5,4},{6,7},{7,6},{8,9},{9,8},{10,11... | collective-permute-start | bytes 7437320 | tf_op jit(solution)/shard_map/ppermute | solution.py:235
  20.0 7.9 %collective-permute-start.3 = (bf16[1076,1152]{1,0:T(8,128)(2,1)S(1)}, bf16[1076,1152]{1,0:T(8,128)(2,1)S(1)}, u32[]{:S(2)}, u32[]{:S(2)}) collective-permute-start(bf16[1076,1152]{1,0:T(8,128)(2,1)S(1)} %copy-done.2), channel_id=1, source_target_pairs={{0,1},{1,0},{2,3},{3,2},{4,5},{5,4},{6,7},{7,6},{8,9},{9,8},{10,11... | collective-permute-start | bytes 7437320 | tf_op jit(solution)/shard_map/ppermute | solution.py:236
  25.8 2.0 %copy-start.3 = (bf16[2,1152]{1,0:T(2,128)(2,1)S(1)}, bf16[2,1152]{1,0:T(2,128)(2,1)}, u32[]{:S(2)}) copy-start(bf16[2,1152]{1,0:T(2,128)(2,1)} %text.1) | copy-start | bytes 13828
  29.4 13.4 %collective-permute-start.4 = (bf16[80,1152]{1,0:T(8,128)(2,1)S(1)}, bf16[80,1152]{1,0:T(8,128)(2,1)S(1)}, u32[]{:S(2)}, u32[]{:S(2)}) collective-permute-start(bf16[80,1152]{1,0:T(8,128)(2,1)S(1)} %get-tuple-element.24), channel_id=1, source_target_pairs={{0,0},{1,8},{2,256},{3,264},{8,1},{9,9},{10,257},{11,265},{256,2},... | collective-permute-start | bytes 552968 | tf_op jit(solution)/shard_map/ppermute | solution.py:43
  31.3 11.4 %collective-permute-start.5 = (bf16[64,1152]{1,0:T(8,128)(2,1)S(1)}, bf16[64,1152]{1,0:T(8,128)(2,1)S(1)}, u32[]{:S(2)}, u32[]{:S(2)}) collective-permute-start(bf16[64,1152]{1,0:T(8,128)(2,1)S(1)} %get-tuple-element.25), channel_id=1, source_target_pairs={{0,256},{1,264},{2,0},{3,8},{8,257},{9,265},{10,1},{11,9},{256,258... | collective-permute-start | bytes 442376 | tf_op jit(solution)/shard_map/ppermute | solution.py:43
  40.8 15.1 %collective-permute-start.6 = (bf16[128,1152]{1,0:T(8,128)(2,1)S(1)}, bf16[128,1152]{1,0:T(8,128)(2,1)S(1)}, u32[]{:S(2)}, u32[]{:S(2)}) collective-permute-start(bf16[128,1152]{1,0:T(8,128)(2,1)S(1)} %get-tuple-element.26.own_share), channel_id=1, source_target_pairs={{0,2},{2,0},{1,3},{3,1},{4,6},{6,4},{5,7},{7,5},{8,10},{10,8},{9,1... | collective-permute-start | bytes 884744 | tf_op jit(solution)/shard_map/ppermute | solution.py:259
  44.0 33.8 %all-to-all-start = ((bf16[32,4,1152]{2,1,0:T(4,128)(2,1)}), bf16[32,4,1152]{2,1,0:T(4,128)(2,1)S(1)}, u32[]{:S(2)}, u32[]{:S(2)}) async-start(bf16[32,4,1152]{2,1,0:T(4,128)(2,1)} %pad_maximum_fusion), calls=%async_computation | async-start | bytes 589824 | tf_op jit(solution)/shard_map/all_to_all | solution.py:262
  55.9 22.2 %copy-start = (s32[1,2]{1,0:T(1,128)S(1)}, s32[1,2]{1,0:T(1,128)}, u32[]{:S(2)}) copy-start(s32[1,2]{1,0:T(1,128)} %counts.3) | copy-start | bytes 28
  56.5 21.5 %collective-permute-start.7 = (f32[8,1152]{1,0:T(8,128)S(1)}, f32[8,1152]{1,0:T(8,128)S(1)}, u32[]{:S(2)}, u32[]{:S(2)}) collective-permute-start(f32[8,1152]{1,0:T(8,128)S(1)} %shard_map.117.pooled_own), channel_id=1, source_target_pairs={{0,1},{1,0},{2,3},{3,2},{4,5},{5,4},{6,7},{7,6},{8,9},{9,8},{10,11... | collective-permute-start | bytes 110600 | tf_op jit(solution)/shard_map/ppermute | solution.py:265

commit v7 on v5

--- a/solution.py
+++ b/solution.py
@@ -73,10 +73,10 @@
     ordered = jnp.dot(moved, rows[...], preferred_element_type=F32)
     packed[...] = ordered.astype(BF16)
     normed = layer_norm(ordered).astype(BF16)
-    qkv = []
-    for i, third in enumerate(thirds):
+    for i in range(3):
         fetches[1 + i].wait()
-        qkv.append(lax.dot_general(normed, w_qkv[third, :], CONTRACT_LAST, preferred_element_type=F32))
+    qkv = lax.dot_general(normed, w_qkv[...], CONTRACT_LAST, preferred_element_type=F32)
+    qkv = [qkv[:, i * width : (i + 1) * width] for i in range(3)]
     outs = []
     for h in range(width // HEAD_DIM):
         q, k, v = (piece[:, h * HEAD_DIM : (h + 1) * HEAD_DIM].astype(BF16) for piece in qkv)
@@ -165,6 +165,26 @@
     grad_out[...] = ((grad - unit * jnp.sum(unit * grad, axis=1, keepdims=True)) / norm_img)[:2].astype(BF16)
 
 
+def place_kernel(gathered, rows_out, grad_out):
+    planes, count, width = gathered.shape
+    per_half, ring = planes // N_YH, count - 1
+    row = lax.broadcasted_iota(I32, (128, 128), 0)
+    column = lax.broadcasted_iota(I32, (128, 128), 1)
+    plane, member = column // ring, column % ring
+    target = (member >> 1) * 8 + (plane >> 1) * 4 + (member & 1) * 2 + (plane & 1)
+    pick = jnp.where(row == target, 1.0, 0.0).astype(BF16)
+    is_share = lax.broadcasted_iota(I32, (count, width), 0) == ring
+    shares = [jnp.zeros((count, width), F32) for _ in range(2)]
+    for half in range(N_YH):
+        mine = [gathered[half * per_half + k] for k in range(per_half)]
+        ordered = jnp.dot(pick, jnp.concatenate([p[:ring] for p in mine], axis=0), preferred_element_type=F32)
+        rows_out[half * 128 : (half + 1) * 128, :] = ordered.astype(BF16)
+        for k in range(per_half):
+            shares[k % 2] += mine[k].astype(F32)
+    grads = [jnp.sum(jnp.where(is_share, share, 0.0), axis=0, keepdims=True) for share in shares]
+    grad_out[...] = jnp.concatenate(grads, axis=0)
+
+
 def call(kernel, specs, outs, scratch=(), limit=None, flops=10**7, nbytes=10**6):
     many = isinstance(outs, list)
     return pl.pallas_call(
@@ -248,8 +268,8 @@
 
     bundle = jnp.concatenate([arrived[:, :2], grad[None]], axis=0)
     bundle = lax.all_gather(bundle, TP, axis=1, tiled=False)
-    rows_out = bundle[:ring].reshape(N_Z, N_XL, N_YH, N_XH, 2, width).transpose(2, 0, 3, 1, 4, 5).reshape(row_count, width)
-    return rows_out, jnp.sum(bundle[ring].astype(F32), axis=0)
+    gathered = bundle.reshape(ring + 1, 8, width).transpose(1, 0, 2)
+    return call(place_kernel, [VMEM], [shape((row_count, width), BF16), shape((2, width), F32)], limit=SMALL)(gathered)
 
 
 def solution(mesh):

time: 93.2 us -> 90.9 us (0.975)
  local copies, waits for them, and re-layouts: 2.24 us -> 0.45 us
    reshape x2 -> x0, local copies, waits for them, and re-layouts: 1.26 us -> none  [per_device(): bundle[:ring].reshape(N_Z, N_XL, N_YH, N_XH, 2, width)]
    pallas_call x0 -> x1, Pallas kernels: none -> 1.12 us  [per_device(): call(place_kernel, [VMEM], [shape((row_count, width), BF16), shape((2, wi...]
  transfers between devices with their start and end apart: 9 -> 9, of which waited for: 4 -> 4; matrix products, arithmetic and copies ran while one was open for 2% -> 2% of each run, Pallas kernels for 2% -> 3%
where the time goes in v7:
time: 90.9 us; the launch traced here: 90.5 us
  starting transfers between devices  41 us (45%)
  waiting for transfers between devices  24.7 us (27%)
  Pallas kernels  10.9 us (12%)
  blocking collectives  9.96 us (11%)
  between operations  2.18 us (2%)
  other arithmetic  1.34 us (1%)
    all_to_all x1, waiting for transfers between devices, per_device(): lax.all_to_all(jnp.concatenate([layer, text], axis=1), RING, 0, 0, tiled=...  19.3 us
    all_to_all x1, starting transfers between devices, per_device(): lax.all_to_all(jnp.concatenate([layer, text], axis=1), RING, 0, 0, tiled=...  11.9 us
    ppermute x2, starting transfers between devices, swap_quarters(): return lax.ppermute(values, QUARTER + TP, pairs)  10 us
    all_gather x1, blocking collectives, per_device(): bundle = lax.all_gather(bundle, TP, axis=1, tiled=False)  9.96 us
    ppermute x1, starting transfers between devices, per_device(): got = lax.ppermute(send, 'core', pair)  8.79 us
    pallas_call x1, Pallas kernels, per_device(): call(attend_kernel, [VMEM, VMEM, HBM, HBM, HBM], [pltpu.VMEM((half_rows,...  4.76 us
    ppermute x1, waiting for transfers between devices, per_device(): far_sum = lax.ppermute(own_sum, 'yl', pair)  3.82 us
    ppermute x1, starting transfers between devices, per_device(): far_w1 = lax.ppermute(far_w1, 'core', pair)  2.28 us
  transfers between devices with their start and end apart: 9, of which 4 were waited for; matrix products, arithmetic and copies ran while one was open for 2% of the time, Pallas kernels for 3%

profile of v7, /device:TPU:1, one launch (start us, length us, event | category | flops | bytes accessed | tf_op | source)
XLA Modules:
  0.0 90.5 jit_solution(2902890844681547616)
XLA Ops:
  0.6 4.8 %shard_map.113 = (bf16[128,1152]{1,0:T(8,128)(2,1)S(1)}, bf16[128,1152]{1,0:T(8,128)(2,1)S(1)}, bf16[128,1152]{1,0:T(8,128)(2,1)S(1)}, bf16[128,128]{1,0:T(8,128)(2,1)S(1)}) custom-call(s32[1,2]{1,0:T(1,128)} %counts.3, s32[1,256]{1,0:T(1,128)} %slots.1, bf16[256,1152]{1,0:T(8,128)(2,1)} %rows_hbm.1, bf16[864,1152]{1,0:T(8,128)(2,1)} %bitcast.10, ...), custom_call_target="tpu_custom_call" | custom-call | flops 2000000000 | bytes 8000000 | tf_op jit(solution)/shard_map/pallas_call | solution.py:207
  5.4 8.8 %collective-permute-start = (bf16[128,1152]{1,0:T(8,128)(2,1)S(1)}, bf16[128,1152]{1,0:T(8,128)(2,1)S(1)}, u32[]{:S(2)}, u32[]{:S(2)}) collective-permute-start(bf16[128,1152]{1,0:T(8,128)(2,1)S(1)} %get-tuple-element.17), channel_id=1, source_target_pairs={{0,1},{1,0},{2,3},{3,2},{4,5},{5,4},{6,7},{7,6},{8,9},{9,8},{10,11... | collective-permute-start | bytes 884744 | tf_op jit(solution)/shard_map/ppermute | solution.py:229
  14.2 1.2 %collective-permute-done.far = bf16[128,1152]{1,0:T(8,128)(2,1)S(1)} collective-permute-done((bf16[128,1152]{1,0:T(8,128)(2,1)S(1)}, bf16[128,1152]{1,0:T(8,128)(2,1)S(1)}, u32[]{:S(2)}, u32[]{:S(2)}) %collective-permute-start) | collective-permute-done | bytes 294944 | tf_op jit(solution)/shard_map/ppermute | solution.py:229
  15.4 0.0 copy-start.1
  15.4 0.0 copy-start.2
  15.4 0.1 shard_map.114.own_sum
  15.5 2.2 %collective-permute-start.1 = (bf16[128,1152]{1,0:T(8,128)(2,1)S(1)}, bf16[128,1152]{1,0:T(8,128)(2,1)S(1)}, u32[]{:S(2)}, u32[]{:S(2)}) collective-permute-start(bf16[128,1152]{1,0:T(8,128)(2,1)S(1)} %shard_map.114.own_sum), channel_id=1, source_target_pairs={{0,2},{2,0},{1,3},{3,1},{4,6},{6,4},{5,7},{7,5},{8,10},{10,8},{9,1... | collective-permute-start | bytes 884744 | tf_op jit(solution)/shard_map/ppermute | solution.py:232
  17.7 0.0 copy-done.1
  17.7 2.3 %collective-permute-start.2 = (bf16[1076,1152]{1,0:T(8,128)(2,1)S(1)}, bf16[1076,1152]{1,0:T(8,128)(2,1)S(1)}, u32[]{:S(2)}, u32[]{:S(2)}) collective-permute-start(bf16[1076,1152]{1,0:T(8,128)(2,1)S(1)} %bitcast.8), channel_id=1, source_target_pairs={{0,1},{1,0},{2,3},{3,2},{4,5},{5,4},{6,7},{7,6},{8,9},{9,8},{10,11... | collective-permute-start | bytes 7437320 | tf_op jit(solution)/shard_map/ppermute | solution.py:233
  20.0 0.0 copy-done.2
  20.0 2.0 %collective-permute-start.3 = (bf16[1076,1152]{1,0:T(8,128)(2,1)S(1)}, bf16[1076,1152]{1,0:T(8,128)(2,1)S(1)}, u32[]{:S(2)}, u32[]{:S(2)}) collective-permute-start(bf16[1076,1152]{1,0:T(8,128)(2,1)S(1)} %copy-done.2), channel_id=1, source_target_pairs={{0,1},{1,0},{2,3},{3,2},{4,5},{5,4},{6,7},{7,6},{8,9},{9,8},{10,11... | collective-permute-start | bytes 7437320 | tf_op jit(solution)/shard_map/ppermute | solution.py:234
  22.0 3.8 %collective-permute-done.1.far_sum = bf16[128,1152]{1,0:T(8,128)(2,1)S(1)} collective-permute-done((bf16[128,1152]{1,0:T(8,128)(2,1)S(1)}, bf16[128,1152]{1,0:T(8,128)(2,1)S(1)}, u32[]{:S(2)}, u32[]{:S(2)}) %collective-permute-start.1) | collective-permute-done | bytes 294944 | tf_op jit(solution)/shard_map/ppermute | solution.py:232
  25.8 0.0 copy-start.3
  25.8 1.7 %shard_map.115 = (bf16[128,1152]{1,0:T(8,128)(2,1)S(1)}, bf16[128,1152]{1,0:T(8,128)(2,1)S(1)}, f32[128,1152]{1,0:T(8,128)S(1)}) custom-call(bf16[128,1152]{1,0:T(8,128)(2,1)S(1)} %get-tuple-element.15.half, bf16[128,1152]{1,0:T(8,128)(2,1)S(1)} %shard_map.114.own_sum, bf16[128,1152]{1,0:T(8,128)(2,1)S(1)} %collective-permute-done.1.far_sum, ...), custom_call_target="tpu_custom_call" | custom-call | flops 49999998976 | bytes 16000000 | tf_op jit(solution)/shard_map/pallas_call | solution.py:236
  27.5 0.0 collective-permute-done.2.w1
  27.5 0.3 collective-permute-done.3.w2
  27.8 0.0 copy-done.3
  27.8 1.5 %shard_map.116 = (bf16[80,1152]{1,0:T(8,128)(2,1)S(1)}, bf16[64,1152]{1,0:T(8,128)(2,1)S(1)}, bf16[128,1152]{1,0:T(8,128)(2,1)S(1)}) custom-call(bf16[128,1152]{1,0:T(8,128)(2,1)S(1)} %get-tuple-element.19.resid, bf16[128,1152]{1,0:T(8,128)(2,1)S(1)} %get-tuple-element.20.normed, f32[128,1152]{1,0:T(8,128)S(1)} %get-tuple-element.21.part, ...), custom_call_target="tpu_custom_call" | custom-call | flops 4000000000 | bytes 16000000 | tf_op jit(solution)/shard_map/pallas_call | solution.py:245
  29.4 1.9 %collective-permute-start.4 = (bf16[80,1152]{1,0:T(8,128)(2,1)S(1)}, bf16[80,1152]{1,0:T(8,128)(2,1)S(1)}, u32[]{:S(2)}, u32[]{:S(2)}) collective-permute-start(bf16[80,1152]{1,0:T(8,128)(2,1)S(1)} %get-tuple-element.24), channel_id=1, source_target_pairs={{0,0},{1,8},{2,256},{3,264},{8,1},{9,9},{10,257},{11,265},{256,2},... | collective-permute-start | bytes 552968 | tf_op jit(solution)/shard_map/ppermute | solution.py:43
  31.3 8.1 %collective-permute-start.5 = (bf16[64,1152]{1,0:T(8,128)(2,1)S(1)}, bf16[64,1152]{1,0:T(8,128)(2,1)S(1)}, u32[]{:S(2)}, u32[]{:S(2)}) collective-permute-start(bf16[64,1152]{1,0:T(8,128)(2,1)S(1)} %get-tuple-element.25), channel_id=1, source_target_pairs={{0,256},{1,264},{2,0},{3,8},{8,257},{9,265},{10,1},{11,9},{256,258... | collective-permute-start | bytes 442376 | tf_op jit(solution)/shard_map/ppermute | solution.py:43
  40.7 0.1 pad_add_fusion.where
  40.8 1.9 %collective-permute-start.6 = (bf16[128,1152]{1,0:T(8,128)(2,1)S(1)}, bf16[128,1152]{1,0:T(8,128)(2,1)S(1)}, u32[]{:S(2)}, u32[]{:S(2)}) collective-permute-start(bf16[128,1152]{1,0:T(8,128)(2,1)S(1)} %get-tuple-element.26.own_share), channel_id=1, source_target_pairs={{0,2},{2,0},{1,3},{3,1},{4,6},{6,4},{5,7},{7,5},{8,10},{10,8},{9,1... | collective-permute-start | bytes 884744 | tf_op jit(solution)/shard_map/ppermute | solution.py:257
  42.7 0.0 collective-permute-done.5
  42.7 0.0 collective-permute-done.4
  42.8 0.1 reshape.14
  42.9 0.1 broadcast_in_dim.4
  42.9 1.0 %pad_maximum_fusion = bf16[32,4,1152]{2,1,0:T(4,128)(2,1)} fusion(bf16[32,2,1152]{2,1,0:T(2,128)(2,1)S(1)} %broadcast_in_dim.4, bf16[32,2,1152]{2,1,0:T(2,128)(2,1)S(1)} %reshape.14), kind=kLoop, calls=%fused_computation | loop fusion | flops 589824 | bytes 589824 | tf_op jit(solution)/shard_map/concatenate | solution.py:260
  44.0 11.9 %all-to-all-start = ((bf16[32,4,1152]{2,1,0:T(4,128)(2,1)}), bf16[32,4,1152]{2,1,0:T(4,128)(2,1)S(1)}, u32[]{:S(2)}, u32[]{:S(2)}) async-start(bf16[32,4,1152]{2,1,0:T(4,128)(2,1)} %pad_maximum_fusion), calls=%async_computation | async-start | bytes 589824 | tf_op jit(solution)/shard_map/all_to_all | solution.py:260
  55.9 0.0 collective-permute-done.6.far_share
  55.9 0.0 copy-start
  55.9 0.6 shard_map.117.pooled_own
  56.5 1.9 %collective-permute-start.7 = (f32[8,1152]{1,0:T(8,128)S(1)}, f32[8,1152]{1,0:T(8,128)S(1)}, u32[]{:S(2)}, u32[]{:S(2)}) collective-permute-start(f32[8,1152]{1,0:T(8,128)S(1)} %shard_map.117.pooled_own), channel_id=1, source_target_pairs={{0,1},{1,0},{2,3},{3,2},{4,5},{5,4},{6,7},{7,6},{8,9},{9,8},{10,11... | collective-permute-start | bytes 110600 | tf_op jit(solution)/shard_map/ppermute | solution.py:263
  58.4 19.3 %all-to-all-done = bf16[32,4,1152]{2,1,0:T(4,128)(2,1)S(1)} async-done(((bf16[32,4,1152]{2,1,0:T(4,128)(2,1)}), bf16[32,4,1152]{2,1,0:T(4,128)(2,1)S(1)}, u32[]{:S(2)}, u32[]{:S(2)}) %all-to-all-start) | async-done | bytes 294944 | tf_op jit(solution)/shard_map/all_to_all | solution.py:260
  77.8 0.2 fusion
  78.0 0.1 reshape.15.texts
  78.0 0.0 collective-permute-done.7.pooled_far
  78.0 0.0 copy-done
  78.0 1.1 %shard_map.118 = bf16[2,1152]{1,0:T(2,128)(2,1)S(1)} custom-call(s32[2]{0:T(128)S(1)} %pad_add_fusion.where, s32[1,2]{1,0:T(1,128)S(1)} %copy-done, f32[1]{0:T(128)S(6)} %copy.16.multiplier, f32[1]{0:T(128)S(6)} %copy.17.shift, f32[8,1152]{1,0:T(8,128)S(1)} %shard_map.117.pooled_own, f32[8,1152]{1,0:T(8,128)S(1)} %collective-permute-done.7.pooled_far, ...), custom_call_target="tpu_custom_call" | custom-call | flops 10000000 | bytes 1000000 | tf_op jit(solution)/shard_map/pallas_call | solution.py:265
  79.2 0.2 pad_maximum_fusion.1
  79.4 10.0 %all-gather = bf16[33,8,1152]{2,0,1:T(8,128)(2,1)S(1)} all-gather(bf16[33,2,1152]{2,0,1:T(8,128)(2,1)S(1)} %copy.15), channel_id=2, replica_groups=mesh['yh'=2,'z'=16,'xh'=2,'xl'=2,'yl'=2,'core'=2] {'yl','core'}, dimensions={1}, use_global_device_ids=true | all-gather | bytes 760320 | tf_op jit(solution)/shard_map/all_gather | solution.py:270
  89.4 1.1 %shard_map.119 = (bf16[256,1152]{1,0:T(8,128)(2,1)}, f32[2,1152]{1,0:T(2,128)}) custom-call(bf16[8,33,1152]{2,1,0:T(8,128)(2,1)S(1)} %bitcast.6), custom_call_target="tpu_custom_call" | custom-call | flops 10000000 | bytes 1000000 | tf_op jit(solution)/shard_map/pallas_call | solution.py:272
  (3 shorter events, 0.1 us)
Async XLA Ops:
  5.4 10.0 %collective-permute-start = (bf16[128,1152]{1,0:T(8,128)(2,1)S(1)}, bf16[128,1152]{1,0:T(8,128)(2,1)S(1)}, u32[]{:S(2)}, u32[]{:S(2)}) collective-permute-start(bf16[128,1152]{1,0:T(8,128)(2,1)S(1)} %get-tuple-element.17), channel_id=1, source_target_pairs={{0,1},{1,0},{2,3},{3,2},{4,5},{5,4},{6,7},{7,6},{8,9},{9,8},{10,11... | collective-permute-start | bytes 884744 | tf_op jit(solution)/shard_map/ppermute | solution.py:229
  15.4 2.3 %copy-start.1 = (bf16[1152,1076]{0,1:T(8,128)(2,1)S(1)}, bf16[1152,1076]{0,1:T(8,128)(2,1)}, u32[]{:S(2)}) copy-start(bf16[1152,1076]{0,1:T(8,128)(2,1)} %param.15) | copy-start | bytes 7437316
  15.4 4.6 %copy-start.2 = (bf16[1076,1152]{1,0:T(8,128)(2,1)S(1)}, bf16[1076,1152]{1,0:T(8,128)(2,1)}, u32[]{:S(2)}) copy-start(bf16[1076,1152]{1,0:T(8,128)(2,1)} %w2.1) | copy-start | bytes 7437316
  15.5 10.4 %collective-permute-start.1 = (bf16[128,1152]{1,0:T(8,128)(2,1)S(1)}, bf16[128,1152]{1,0:T(8,128)(2,1)S(1)}, u32[]{:S(2)}, u32[]{:S(2)}) collective-permute-start(bf16[128,1152]{1,0:T(8,128)(2,1)S(1)} %shard_map.114.own_sum), channel_id=1, source_target_pairs={{0,2},{2,0},{1,3},{3,1},{4,6},{6,4},{5,7},{7,5},{8,10},{10,8},{9,1... | collective-permute-start | bytes 884744 | tf_op jit(solution)/shard_map/ppermute | solution.py:232
  17.7 9.9 %collective-permute-start.2 = (bf16[1076,1152]{1,0:T(8,128)(2,1)S(1)}, bf16[1076,1152]{1,0:T(8,128)(2,1)S(1)}, u32[]{:S(2)}, u32[]{:S(2)}) collective-permute-start(bf16[1076,1152]{1,0:T(8,128)(2,1)S(1)} %bitcast.8), channel_id=1, source_target_pairs={{0,1},{1,0},{2,3},{3,2},{4,5},{5,4},{6,7},{7,6},{8,9},{9,8},{10,11... | collective-permute-start | bytes 7437320 | tf_op jit(solution)/shard_map/ppermute | solution.py:233
  20.0 7.9 %collective-permute-start.3 = (bf16[1076,1152]{1,0:T(8,128)(2,1)S(1)}, bf16[1076,1152]{1,0:T(8,128)(2,1)S(1)}, u32[]{:S(2)}, u32[]{:S(2)}) collective-permute-start(bf16[1076,1152]{1,0:T(8,128)(2,1)S(1)} %copy-done.2), channel_id=1, source_target_pairs={{0,1},{1,0},{2,3},{3,2},{4,5},{5,4},{6,7},{7,6},{8,9},{9,8},{10,11... | collective-permute-start | bytes 7437320 | tf_op jit(solution)/shard_map/ppermute | solution.py:234
  25.8 2.0 %copy-start.3 = (bf16[2,1152]{1,0:T(2,128)(2,1)S(1)}, bf16[2,1152]{1,0:T(2,128)(2,1)}, u32[]{:S(2)}) copy-start(bf16[2,1152]{1,0:T(2,128)(2,1)} %text.1) | copy-start | bytes 13828
  29.4 13.4 %collective-permute-start.4 = (bf16[80,1152]{1,0:T(8,128)(2,1)S(1)}, bf16[80,1152]{1,0:T(8,128)(2,1)S(1)}, u32[]{:S(2)}, u32[]{:S(2)}) collective-permute-start(bf16[80,1152]{1,0:T(8,128)(2,1)S(1)} %get-tuple-element.24), channel_id=1, source_target_pairs={{0,0},{1,8},{2,256},{3,264},{8,1},{9,9},{10,257},{11,265},{256,2},... | collective-permute-start | bytes 552968 | tf_op jit(solution)/shard_map/ppermute | solution.py:43
  31.3 11.4 %collective-permute-start.5 = (bf16[64,1152]{1,0:T(8,128)(2,1)S(1)}, bf16[64,1152]{1,0:T(8,128)(2,1)S(1)}, u32[]{:S(2)}, u32[]{:S(2)}) collective-permute-start(bf16[64,1152]{1,0:T(8,128)(2,1)S(1)} %get-tuple-element.25), channel_id=1, source_target_pairs={{0,256},{1,264},{2,0},{3,8},{8,257},{9,265},{10,1},{11,9},{256,258... | collective-permute-start | bytes 442376 | tf_op jit(solution)/shard_map/ppermute | solution.py:43
  40.8 15.1 %collective-permute-start.6 = (bf16[128,1152]{1,0:T(8,128)(2,1)S(1)}, bf16[128,1152]{1,0:T(8,128)(2,1)S(1)}, u32[]{:S(2)}, u32[]{:S(2)}) collective-permute-start(bf16[128,1152]{1,0:T(8,128)(2,1)S(1)} %get-tuple-element.26.own_share), channel_id=1, source_target_pairs={{0,2},{2,0},{1,3},{3,1},{4,6},{6,4},{5,7},{7,5},{8,10},{10,8},{9,1... | collective-permute-start | bytes 884744 | tf_op jit(solution)/shard_map/ppermute | solution.py:257
  44.0 33.8 %all-to-all-start = ((bf16[32,4,1152]{2,1,0:T(4,128)(2,1)}), bf16[32,4,1152]{2,1,0:T(4,128)(2,1)S(1)}, u32[]{:S(2)}, u32[]{:S(2)}) async-start(bf16[32,4,1152]{2,1,0:T(4,128)(2,1)} %pad_maximum_fusion), calls=%async_computation | async-start | bytes 589824 | tf_op jit(solution)/shard_map/all_to_all | solution.py:260
  55.9 22.2 %copy-start = (s32[1,2]{1,0:T(1,128)S(1)}, s32[1,2]{1,0:T(1,128)}, u32[]{:S(2)}) copy-start(s32[1,2]{1,0:T(1,128)} %counts.3) | copy-start | bytes 28
  56.5 21.5 %collective-permute-start.7 = (f32[8,1152]{1,0:T(8,128)S(1)}, f32[8,1152]{1,0:T(8,128)S(1)}, u32[]{:S(2)}, u32[]{:S(2)}) collective-permute-start(f32[8,1152]{1,0:T(8,128)S(1)} %shard_map.117.pooled_own), channel_id=1, source_target_pairs={{0,1},{1,0},{2,3},{3,2},{4,5},{5,4},{6,7},{7,6},{8,9},{9,8},{10,11... | collective-permute-start | bytes 110600 | tf_op jit(solution)/shard_map/ppermute | solution.py:263

commit v8 on v7

--- a/solution.py
+++ b/solution.py
@@ -44,7 +44,7 @@
 
 
 def attend_kernel(
-    counts, slots, rows_hbm, w_qkv_hbm, w_out_hbm, keep, send, half, member, packed, part, rows, w_qkv, w_out, sems
+    counts, slots, rows_hbm, w_qkv_hbm, w_out_hbm, send, kept, half, member, packed, attended, rows, w_qkv, w_out, sems
 ):
     n, width = rows.shape[0], w_out.shape[0]
     thirds = [pl.ds(i * width, width) for i in range(3)]
@@ -85,16 +85,19 @@
         raised = jnp.exp(scores - jnp.max(scores, axis=-1, keepdims=True))
         total = jnp.sum(raised, axis=-1, keepdims=True)
         outs.append(jnp.dot(raised.astype(BF16), v, preferred_element_type=F32) / total)
-    attended = jnp.concatenate(outs, axis=1).astype(BF16)
+    attended[...] = jnp.concatenate(outs, axis=1).astype(BF16)
+    mine, other = pl.multiple_of(core * 128, 128), pl.multiple_of(128 - core * 128, 128)
+    kept[...] = attended[pl.ds(mine, 128), :]
     fetches[4].wait()
-    part[...] = jnp.dot(attended, w_out[...], preferred_element_type=F32).astype(BF16)
-    mine, other = pl.multiple_of(core * 128, 128), pl.multiple_of(128 - core * 128, 128)
-    keep[...] = part[pl.ds(mine, 128), :]
-    send[...] = part[pl.ds(other, 128), :]
+    send[...] = jnp.dot(attended[pl.ds(other, 128), :], w_out[...], preferred_element_type=F32).astype(BF16)
     half[...] = packed[pl.ds(mine, 128), :]
     images = lax.broadcasted_iota(I32, (n, 128), 1).astype(F32)
     packed[:, :128] = jnp.where(seg_rows == images, 1.0, 0.0).astype(BF16)
     member[...] = packed[pl.ds(mine, 128), :128]
+
+
+def keep_kernel(kept, w_out, keep):
+    keep[...] = jnp.dot(kept[...], w_out[...], preferred_element_type=F32).astype(BF16)
 
 
 def add_kernel(own, far, out):
@@ -204,18 +207,18 @@
     shape = jax.ShapeDtypeStruct
     pair = [(0, 1), (1, 0)]
 
-    keep, send, half, member = call(
+    send, kept, half, member = call(
         attend_kernel,
         [VMEM, VMEM, HBM, HBM, HBM],
         [
             pltpu.VMEM((half_rows, width), BF16),
-            pltpu.VMEM((half_rows, width), BF16),
+            pltpu.VMEM((half_rows, w_out.shape[0]), BF16),
             pltpu.VMEM((half_rows, width), BF16),
             pltpu.VMEM((half_rows, 128), BF16),
         ],
         [
             pltpu.VMEM((row_count, width), BF16),
-            pltpu.VMEM((row_count, width), BF16),
+            pltpu.VMEM((row_count, w_out.shape[0]), BF16),
             pltpu.VMEM((row_count, width), BF16),
             pltpu.VMEM((w_qkv.shape[1], width), BF16),
             pltpu.VMEM(w_out.shape, BF16),
@@ -227,6 +230,9 @@
     )(*(pltpu.with_memory_space_constraint(x, pltpu.HBM) for x in (patch_counts, row_slots, rows_in, w_qkv.T, w_out)))
 
     got = lax.ppermute(send, "core", pair)
+    keep = call(keep_kernel, [VMEM] * 2, pltpu.VMEM((half_rows, width), BF16), limit=SMALL, flops=10**9)(
+        kept, pltpu.with_memory_space_constraint(w_out, pltpu.HBM)
+    )
     own_sum = call(add_kernel, [VMEM] * 2, shape((half_rows, width), BF16), limit=SMALL, flops=ADD_FLOPS)(keep, got)
     own_sum, far_w1, far_w2 = lax.optimization_barrier((own_sum, w_fc1.T, w_fc2))
     far_sum = lax.ppermute(own_sum, "yl", pair)

time: 90.9 us -> 90.7 us (level)
  waiting for transfers between devices: 24.7 us -> 23.5 us
  Pallas kernels: 10.9 us -> 12 us
    pallas_call x0 -> x1, Pallas kernels: none -> 1.39 us  [per_device(): call(keep_kernel, [VMEM] * 2, pltpu.VMEM((half_rows, width), BF16), limit...]
    ppermute x1, waiting for transfers between devices: 1.19 us -> 0.01 us  [per_device(): got = lax.ppermute(send, 'core', pair)]
  transfers between devices with their start and end apart: 9 -> 9, of which waited for: 4 -> 2; matrix products, arithmetic and copies ran while one was open for 2% -> 2% of each run, Pallas kernels for 3% -> 4%
where the time goes in v8:
time: 90.7 us; the launch traced here: 90.3 us
  starting transfers between devices  40.8 us (45%)
  waiting for transfers between devices  23.5 us (26%)
  Pallas kernels  12 us (13%)
  blocking collectives  9.96 us (11%)
  between operations  2.22 us (2%)
  other arithmetic  1.34 us (1%)
    all_to_all x1, waiting for transfers between devices, per_device(): lax.all_to_all(jnp.concatenate([layer, text], axis=1), RING, 0, 0, tiled=...  19.3 us
    all_to_all x1, starting transfers between devices, per_device(): lax.all_to_all(jnp.concatenate([layer, text], axis=1), RING, 0, 0, tiled=...  11.9 us
    all_gather x1, blocking collectives, per_device(): bundle = lax.all_gather(bundle, TP, axis=1, tiled=False)  9.96 us
    ppermute x2, starting transfers between devices, swap_quarters(): return lax.ppermute(values, QUARTER + TP, pairs)  9.8 us
    ppermute x1, starting transfers between devices, per_device(): got = lax.ppermute(send, 'core', pair)  8.79 us
    pallas_call x1, Pallas kernels, per_device(): call(attend_kernel, [VMEM, VMEM, HBM, HBM, HBM], [pltpu.VMEM((half_rows,...  4.53 us
    ppermute x1, waiting for transfers between devices, per_device(): far_sum = lax.ppermute(own_sum, 'yl', pair)  4.08 us
    ppermute x1, starting transfers between devices, per_device(): far_w2 = lax.ppermute(far_w2, 'core', pair)  2.3 us
  transfers between devices with their start and end apart: 9, of which 2 were waited for; matrix products, arithmetic and copies ran while one was open for 2% of the time, Pallas kernels for 4%

profile of v8, /device:TPU:1, one launch (start us, length us, event | category | flops | bytes accessed | tf_op | source)
XLA Modules:
  0.0 90.3 jit_solution(12570901191293744541)
XLA Ops:
  0.6 4.5 %shard_map.113 = (bf16[128,1152]{1,0:T(8,128)(2,1)S(1)}, bf16[128,288]{1,0:T(8,128)(2,1)S(1)}, bf16[128,1152]{1,0:T(8,128)(2,1)S(1)}, bf16[128,128]{1,0:T(8,128)(2,1)S(1)}) custom-call(s32[1,2]{1,0:T(1,128)} %counts.3, s32[1,256]{1,0:T(1,128)} %slots.1, bf16[256,1152]{1,0:T(8,128)(2,1)} %rows_hbm.1, bf16[864,1152]{1,0:T(8,128)(2,1)} %bitcast.10, ...), custom_call_target="tpu_custom_call" | custom-call | flops 2000000000 | bytes 8000000 | tf_op jit(solution)/shard_map/pallas_call | solution.py:210
  5.2 8.8 %collective-permute-start = (bf16[128,1152]{1,0:T(8,128)(2,1)S(1)}, bf16[128,1152]{1,0:T(8,128)(2,1)S(1)}, u32[]{:S(2)}, u32[]{:S(2)}) collective-permute-start(bf16[128,1152]{1,0:T(8,128)(2,1)S(1)} %get-tuple-element.17), channel_id=1, source_target_pairs={{0,1},{1,0},{2,3},{3,2},{4,5},{5,4},{6,7},{7,6},{8,9},{9,8},{10,11... | collective-permute-start | bytes 884744 | tf_op jit(solution)/shard_map/ppermute | solution.py:232
  14.0 1.4 %shard_map.114.own = bf16[128,1152]{1,0:T(8,128)(2,1)S(1)} custom-call(bf16[128,288]{1,0:T(8,128)(2,1)S(1)} %get-tuple-element.16.kept, bf16[288,1152]{1,0:T(8,128)(2,1)} %w_out.1), custom_call_target="tpu_custom_call" | custom-call | flops 1000000000 | bytes 1000000 | tf_op jit(solution)/shard_map/pallas_call | solution.py:233
  15.4 0.0 collective-permute-done.far
  15.4 0.0 copy-start.1
  15.4 0.0 copy-start.2
  15.4 0.1 shard_map.115.own_sum
  15.5 2.2 %collective-permute-start.1 = (bf16[128,1152]{1,0:T(8,128)(2,1)S(1)}, bf16[128,1152]{1,0:T(8,128)(2,1)S(1)}, u32[]{:S(2)}, u32[]{:S(2)}) collective-permute-start(bf16[128,1152]{1,0:T(8,128)(2,1)S(1)} %shard_map.115.own_sum), channel_id=1, source_target_pairs={{0,2},{2,0},{1,3},{3,1},{4,6},{6,4},{5,7},{7,5},{8,10},{10,8},{9,1... | collective-permute-start | bytes 884744 | tf_op jit(solution)/shard_map/ppermute | solution.py:238
  17.7 0.0 copy-done.1
  17.7 2.0 %collective-permute-start.2 = (bf16[1076,1152]{1,0:T(8,128)(2,1)S(1)}, bf16[1076,1152]{1,0:T(8,128)(2,1)S(1)}, u32[]{:S(2)}, u32[]{:S(2)}) collective-permute-start(bf16[1076,1152]{1,0:T(8,128)(2,1)S(1)} %bitcast.8), channel_id=1, source_target_pairs={{0,1},{1,0},{2,3},{3,2},{4,5},{5,4},{6,7},{7,6},{8,9},{9,8},{10,11... | collective-permute-start | bytes 7437320 | tf_op jit(solution)/shard_map/ppermute | solution.py:239
  19.7 0.0 copy-done.2
  19.7 2.3 %collective-permute-start.3 = (bf16[1076,1152]{1,0:T(8,128)(2,1)S(1)}, bf16[1076,1152]{1,0:T(8,128)(2,1)S(1)}, u32[]{:S(2)}, u32[]{:S(2)}) collective-permute-start(bf16[1076,1152]{1,0:T(8,128)(2,1)S(1)} %copy-done.2), channel_id=1, source_target_pairs={{0,1},{1,0},{2,3},{3,2},{4,5},{5,4},{6,7},{7,6},{8,9},{9,8},{10,11... | collective-permute-start | bytes 7437320 | tf_op jit(solution)/shard_map/ppermute | solution.py:240
  22.0 4.1 %collective-permute-done.1.far_sum = bf16[128,1152]{1,0:T(8,128)(2,1)S(1)} collective-permute-done((bf16[128,1152]{1,0:T(8,128)(2,1)S(1)}, bf16[128,1152]{1,0:T(8,128)(2,1)S(1)}, u32[]{:S(2)}, u32[]{:S(2)}) %collective-permute-start.1) | collective-permute-done | bytes 294944 | tf_op jit(solution)/shard_map/ppermute | solution.py:238
  26.1 0.0 copy-start.3
  26.1 1.7 %shard_map.116 = (bf16[128,1152]{1,0:T(8,128)(2,1)S(1)}, bf16[128,1152]{1,0:T(8,128)(2,1)S(1)}, f32[128,1152]{1,0:T(8,128)S(1)}) custom-call(bf16[128,1152]{1,0:T(8,128)(2,1)S(1)} %get-tuple-element.15.half, bf16[128,1152]{1,0:T(8,128)(2,1)S(1)} %shard_map.115.own_sum, bf16[128,1152]{1,0:T(8,128)(2,1)S(1)} %collective-permute-done.1.far_sum, ...), custom_call_target="tpu_custom_call" | custom-call | flops 49999998976 | bytes 16000000 | tf_op jit(solution)/shard_map/pallas_call | solution.py:242
  27.8 0.0 collective-permute-done.2.w1
  27.8 0.0 collective-permute-done.3.w2
  27.9 0.0 copy-done.3
  27.9 1.5 %shard_map.117 = (bf16[80,1152]{1,0:T(8,128)(2,1)S(1)}, bf16[64,1152]{1,0:T(8,128)(2,1)S(1)}, bf16[128,1152]{1,0:T(8,128)(2,1)S(1)}) custom-call(bf16[128,1152]{1,0:T(8,128)(2,1)S(1)} %get-tuple-element.19.resid, bf16[128,1152]{1,0:T(8,128)(2,1)S(1)} %get-tuple-element.20.normed, f32[128,1152]{1,0:T(8,128)S(1)} %get-tuple-element.21.part, ...), custom_call_target="tpu_custom_call" | custom-call | flops 4000000000 | bytes 16000000 | tf_op jit(solution)/shard_map/pallas_call | solution.py:251
  29.4 1.9 %collective-permute-start.4 = (bf16[80,1152]{1,0:T(8,128)(2,1)S(1)}, bf16[80,1152]{1,0:T(8,128)(2,1)S(1)}, u32[]{:S(2)}, u32[]{:S(2)}) collective-permute-start(bf16[80,1152]{1,0:T(8,128)(2,1)S(1)} %get-tuple-element.24), channel_id=1, source_target_pairs={{0,0},{1,8},{2,256},{3,264},{8,1},{9,9},{10,257},{11,265},{256,2},... | collective-permute-start | bytes 552968 | tf_op jit(solution)/shard_map/ppermute | solution.py:43
  31.3 7.9 %collective-permute-start.5 = (bf16[64,1152]{1,0:T(8,128)(2,1)S(1)}, bf16[64,1152]{1,0:T(8,128)(2,1)S(1)}, u32[]{:S(2)}, u32[]{:S(2)}) collective-permute-start(bf16[64,1152]{1,0:T(8,128)(2,1)S(1)} %get-tuple-element.25), channel_id=1, source_target_pairs={{0,256},{1,264},{2,0},{3,8},{8,257},{9,265},{10,1},{11,9},{256,258... | collective-permute-start | bytes 442376 | tf_op jit(solution)/shard_map/ppermute | solution.py:43
  40.5 0.1 pad_add_fusion.where
  40.6 1.9 %collective-permute-start.6 = (bf16[128,1152]{1,0:T(8,128)(2,1)S(1)}, bf16[128,1152]{1,0:T(8,128)(2,1)S(1)}, u32[]{:S(2)}, u32[]{:S(2)}) collective-permute-start(bf16[128,1152]{1,0:T(8,128)(2,1)S(1)} %get-tuple-element.26.own_share), channel_id=1, source_target_pairs={{0,2},{2,0},{1,3},{3,1},{4,6},{6,4},{5,7},{7,5},{8,10},{10,8},{9,1... | collective-permute-start | bytes 884744 | tf_op jit(solution)/shard_map/ppermute | solution.py:263
  42.5 0.0 collective-permute-done.5
  42.5 0.0 collective-permute-done.4
  42.6 0.1 reshape.14
  42.7 0.1 broadcast_in_dim.4
  42.7 1.0 %pad_maximum_fusion = bf16[32,4,1152]{2,1,0:T(4,128)(2,1)} fusion(bf16[32,2,1152]{2,1,0:T(2,128)(2,1)S(1)} %broadcast_in_dim.4, bf16[32,2,1152]{2,1,0:T(2,128)(2,1)S(1)} %reshape.14), kind=kLoop, calls=%fused_computation | loop fusion | flops 589824 | bytes 589824 | tf_op jit(solution)/shard_map/concatenate | solution.py:266
  43.8 11.9 %all-to-all-start = ((bf16[32,4,1152]{2,1,0:T(4,128)(2,1)}), bf16[32,4,1152]{2,1,0:T(4,128)(2,1)S(1)}, u32[]{:S(2)}, u32[]{:S(2)}) async-start(bf16[32,4,1152]{2,1,0:T(4,128)(2,1)} %pad_maximum_fusion), calls=%async_computation | async-start | bytes 589824 | tf_op jit(solution)/shard_map/all_to_all | solution.py:266
  55.7 0.0 collective-permute-done.6.far_share
  55.7 0.0 copy-start
  55.7 0.6 shard_map.118.pooled_own
  56.3 1.9 %collective-permute-start.7 = (f32[8,1152]{1,0:T(8,128)S(1)}, f32[8,1152]{1,0:T(8,128)S(1)}, u32[]{:S(2)}, u32[]{:S(2)}) collective-permute-start(f32[8,1152]{1,0:T(8,128)S(1)} %shard_map.118.pooled_own), channel_id=1, source_target_pairs={{0,1},{1,0},{2,3},{3,2},{4,5},{5,4},{6,7},{7,6},{8,9},{9,8},{10,11... | collective-permute-start | bytes 110600 | tf_op jit(solution)/shard_map/ppermute | solution.py:269
  58.2 19.3 %all-to-all-done = bf16[32,4,1152]{2,1,0:T(4,128)(2,1)S(1)} async-done(((bf16[32,4,1152]{2,1,0:T(4,128)(2,1)}), bf16[32,4,1152]{2,1,0:T(4,128)(2,1)S(1)}, u32[]{:S(2)}, u32[]{:S(2)}) %all-to-all-start) | async-done | bytes 294944 | tf_op jit(solution)/shard_map/all_to_all | solution.py:266
  77.5 0.2 fusion
  77.8 0.1 reshape.15.texts
  77.8 0.0 collective-permute-done.7.pooled_far
  77.8 0.0 copy-done
  77.8 1.1 %shard_map.119 = bf16[2,1152]{1,0:T(2,128)(2,1)S(1)} custom-call(s32[2]{0:T(128)S(1)} %pad_add_fusion.where, s32[1,2]{1,0:T(1,128)S(1)} %copy-done, f32[1]{0:T(128)S(6)} %copy.16.multiplier, f32[1]{0:T(128)S(6)} %copy.17.shift, f32[8,1152]{1,0:T(8,128)S(1)} %shard_map.118.pooled_own, f32[8,1152]{1,0:T(8,128)S(1)} %collective-permute-done.7.pooled_far, ...), custom_call_target="tpu_custom_call" | custom-call | flops 10000000 | bytes 1000000 | tf_op jit(solution)/shard_map/pallas_call | solution.py:271
  79.0 0.2 pad_maximum_fusion.1
  79.2 10.0 %all-gather = bf16[33,8,1152]{2,0,1:T(8,128)(2,1)S(1)} all-gather(bf16[33,2,1152]{2,0,1:T(8,128)(2,1)S(1)} %copy.15), channel_id=2, replica_groups=mesh['yh'=2,'z'=16,'xh'=2,'xl'=2,'yl'=2,'core'=2] {'yl','core'}, dimensions={1}, use_global_device_ids=true | all-gather | bytes 760320 | tf_op jit(solution)/shard_map/all_gather | solution.py:276
  89.2 1.1 %shard_map.120 = (bf16[256,1152]{1,0:T(8,128)(2,1)}, f32[2,1152]{1,0:T(2,128)}) custom-call(bf16[8,33,1152]{2,1,0:T(8,128)(2,1)S(1)} %bitcast.6), custom_call_target="tpu_custom_call" | custom-call | flops 10000000 | bytes 1000000 | tf_op jit(solution)/shard_map/pallas_call | solution.py:278
  (3 shorter events, 0.1 us)
Async XLA Ops:
  5.2 10.2 %collective-permute-start = (bf16[128,1152]{1,0:T(8,128)(2,1)S(1)}, bf16[128,1152]{1,0:T(8,128)(2,1)S(1)}, u32[]{:S(2)}, u32[]{:S(2)}) collective-permute-start(bf16[128,1152]{1,0:T(8,128)(2,1)S(1)} %get-tuple-element.17), channel_id=1, source_target_pairs={{0,1},{1,0},{2,3},{3,2},{4,5},{5,4},{6,7},{7,6},{8,9},{9,8},{10,11... | collective-permute-start | bytes 884744 | tf_op jit(solution)/shard_map/ppermute | solution.py:232
  15.4 2.3 %copy-start.1 = (bf16[1152,1076]{0,1:T(8,128)(2,1)S(1)}, bf16[1152,1076]{0,1:T(8,128)(2,1)}, u32[]{:S(2)}) copy-start(bf16[1152,1076]{0,1:T(8,128)(2,1)} %param.15) | copy-start | bytes 7437316
  15.4 4.3 %copy-start.2 = (bf16[1076,1152]{1,0:T(8,128)(2,1)S(1)}, bf16[1076,1152]{1,0:T(8,128)(2,1)}, u32[]{:S(2)}) copy-start(bf16[1076,1152]{1,0:T(8,128)(2,1)} %w2.1) | copy-start | bytes 7437316
  15.5 10.6 %collective-permute-start.1 = (bf16[128,1152]{1,0:T(8,128)(2,1)S(1)}, bf16[128,1152]{1,0:T(8,128)(2,1)S(1)}, u32[]{:S(2)}, u32[]{:S(2)}) collective-permute-start(bf16[128,1152]{1,0:T(8,128)(2,1)S(1)} %shard_map.115.own_sum), channel_id=1, source_target_pairs={{0,2},{2,0},{1,3},{3,1},{4,6},{6,4},{5,7},{7,5},{8,10},{10,8},{9,1... | collective-permute-start | bytes 884744 | tf_op jit(solution)/shard_map/ppermute | solution.py:238
  17.7 10.1 %collective-permute-start.2 = (bf16[1076,1152]{1,0:T(8,128)(2,1)S(1)}, bf16[1076,1152]{1,0:T(8,128)(2,1)S(1)}, u32[]{:S(2)}, u32[]{:S(2)}) collective-permute-start(bf16[1076,1152]{1,0:T(8,128)(2,1)S(1)} %bitcast.8), channel_id=1, source_target_pairs={{0,1},{1,0},{2,3},{3,2},{4,5},{5,4},{6,7},{7,6},{8,9},{9,8},{10,11... | collective-permute-start | bytes 7437320 | tf_op jit(solution)/shard_map/ppermute | solution.py:239
  19.7 8.1 %collective-permute-start.3 = (bf16[1076,1152]{1,0:T(8,128)(2,1)S(1)}, bf16[1076,1152]{1,0:T(8,128)(2,1)S(1)}, u32[]{:S(2)}, u32[]{:S(2)}) collective-permute-start(bf16[1076,1152]{1,0:T(8,128)(2,1)S(1)} %copy-done.2), channel_id=1, source_target_pairs={{0,1},{1,0},{2,3},{3,2},{4,5},{5,4},{6,7},{7,6},{8,9},{9,8},{10,11... | collective-permute-start | bytes 7437320 | tf_op jit(solution)/shard_map/ppermute | solution.py:240
  26.1 1.7 %copy-start.3 = (bf16[2,1152]{1,0:T(2,128)(2,1)S(1)}, bf16[2,1152]{1,0:T(2,128)(2,1)}, u32[]{:S(2)}) copy-start(bf16[2,1152]{1,0:T(2,128)(2,1)} %text.1) | copy-start | bytes 13828
  29.4 13.1 %collective-permute-start.4 = (bf16[80,1152]{1,0:T(8,128)(2,1)S(1)}, bf16[80,1152]{1,0:T(8,128)(2,1)S(1)}, u32[]{:S(2)}, u32[]{:S(2)}) collective-permute-start(bf16[80,1152]{1,0:T(8,128)(2,1)S(1)} %get-tuple-element.24), channel_id=1, source_target_pairs={{0,0},{1,8},{2,256},{3,264},{8,1},{9,9},{10,257},{11,265},{256,2},... | collective-permute-start | bytes 552968 | tf_op jit(solution)/shard_map/ppermute | solution.py:43
  31.3 11.2 %collective-permute-start.5 = (bf16[64,1152]{1,0:T(8,128)(2,1)S(1)}, bf16[64,1152]{1,0:T(8,128)(2,1)S(1)}, u32[]{:S(2)}, u32[]{:S(2)}) collective-permute-start(bf16[64,1152]{1,0:T(8,128)(2,1)S(1)} %get-tuple-element.25), channel_id=1, source_target_pairs={{0,256},{1,264},{2,0},{3,8},{8,257},{9,265},{10,1},{11,9},{256,258... | collective-permute-start | bytes 442376 | tf_op jit(solution)/shard_map/ppermute | solution.py:43
  40.6 15.1 %collective-permute-start.6 = (bf16[128,1152]{1,0:T(8,128)(2,1)S(1)}, bf16[128,1152]{1,0:T(8,128)(2,1)S(1)}, u32[]{:S(2)}, u32[]{:S(2)}) collective-permute-start(bf16[128,1152]{1,0:T(8,128)(2,1)S(1)} %get-tuple-element.26.own_share), channel_id=1, source_target_pairs={{0,2},{2,0},{1,3},{3,1},{4,6},{6,4},{5,7},{7,5},{8,10},{10,8},{9,1... | collective-permute-start | bytes 884744 | tf_op jit(solution)/shard_map/ppermute | solution.py:263
  43.8 33.8 %all-to-all-start = ((bf16[32,4,1152]{2,1,0:T(4,128)(2,1)}), bf16[32,4,1152]{2,1,0:T(4,128)(2,1)S(1)}, u32[]{:S(2)}, u32[]{:S(2)}) async-start(bf16[32,4,1152]{2,1,0:T(4,128)(2,1)} %pad_maximum_fusion), calls=%async_computation | async-start | bytes 589824 | tf_op jit(solution)/shard_map/all_to_all | solution.py:266
  55.7 22.2 %copy-start = (s32[1,2]{1,0:T(1,128)S(1)}, s32[1,2]{1,0:T(1,128)}, u32[]{:S(2)}) copy-start(s32[1,2]{1,0:T(1,128)} %counts.3) | copy-start | bytes 28
  56.3 21.5 %collective-permute-start.7 = (f32[8,1152]{1,0:T(8,128)S(1)}, f32[8,1152]{1,0:T(8,128)S(1)}, u32[]{:S(2)}, u32[]{:S(2)}) collective-permute-start(f32[8,1152]{1,0:T(8,128)S(1)} %shard_map.118.pooled_own), channel_id=1, source_target_pairs={{0,1},{1,0},{2,3},{3,2},{4,5},{5,4},{6,7},{7,6},{8,9},{9,8},{10,11... | collective-permute-start | bytes 110600 | tf_op jit(solution)/shard_map/ppermute | solution.py:269
